TPU v7x, 512 devices: a whole 4x4x16 slice. The times are simulated.
512 devices in a mesh: lat: 16 (over z_hi, x), lon: 32 (over y, z_lo, core).
Axes of the slice: x: 4, y: 4, z: 16 (z_hi: 4, z_lo: 4; z = z_hi * 4 + z_lo), core: 2. Of those that a mesh axis runs over, the one named last changes fastest.
Arguments:
- tracer: float32 [6, 16, 128, 4096], P(None, None, 'lat', 'lon'), may hold values from -6 to 6
- east_vel: float32 [16, 128, 4096], P(None, 'lat', 'lon'), may hold values from -0.25 to 0.25
- north_vel: float32 [16, 128, 4096], P(None, 'lat', 'lon'), may hold values from -0.25 to 0.25
- wet_mask: int32 [16, 128, 4096], P(None, 'lat', 'lon'), may hold values from 0 to 1, as said below
- bottom_level: int32 [128, 4096], P('lat', 'lon'), may hold values from 0 to 16, as said below
- vertical_mix: float32 [16, 128, 4096], P(None, 'lat', 'lon'), may hold values from 0.05 to 5
Outputs:
- updated: float32 [6, 16, 128, 4096], P(None, None, 'lat', 'lon')
Inputs may be any that keep to these rules, and one draw needn't show every extreme that they name: bottom_level is the number of levels above a column's sea floor; 0 on land. wet_mask is 0 at every level at or below its column's bottom_level.
All inputs are finite; a program needn't handle non-finite values.
Results may differ from a plain program's by a relative error of at most 0.00002.
Values sent between devices are 32-bit elements; how exact they have to be, the bound alone decides.
No kernel may reach another device: no remote copies, remote signals or barrier semaphores. Data moves between devices by JAX's collectives and lax.ppermute only.
A program may use at most 64 MiB of HBM per device.

v0:
```python
import jax
import jax.numpy as jnp
from jax import lax
from jax.sharding import PartitionSpec as P

lateral_mixing = 0.08


def extended(cells, sides, width):
    for axis, dim in sides:
        count = lax.axis_size(axis)
        head = lax.slice_in_dim(cells, 0, width, axis=dim)
        tail = lax.slice_in_dim(cells, cells.shape[dim] - width, cells.shape[dim], axis=dim)
        cells = jnp.concatenate(
            [
                lax.ppermute(tail, axis, [(i, (i + 1) % count) for i in range(count)]),
                cells,
                lax.ppermute(head, axis, [((i + 1) % count, i) for i in range(count)]),
            ],
            axis=dim,
        )
    return cells


def flux_sum(tracer_pad, east_pad, north_pad, mask_pad):
    east_speed = 0.5 * (east_pad[..., 1:-1, :-1] + east_pad[..., 1:-1, 1:])
    east_open = mask_pad[..., 1:-1, :-1] * mask_pad[..., 1:-1, 1:]
    west_side = tracer_pad[..., 1:-1, :-1]
    east_side = tracer_pad[..., 1:-1, 1:]
    east_flux = east_open * (
        jnp.maximum(east_speed, 0.0) * west_side
        + jnp.minimum(east_speed, 0.0) * east_side
        - lateral_mixing * (east_side - west_side)
    )
    north_speed = 0.5 * (north_pad[..., :-1, 1:-1] + north_pad[..., 1:, 1:-1])
    north_open = mask_pad[..., :-1, 1:-1] * mask_pad[..., 1:, 1:-1]
    south_side = tracer_pad[..., :-1, 1:-1]
    north_side = tracer_pad[..., 1:, 1:-1]
    north_flux = north_open * (
        jnp.maximum(north_speed, 0.0) * south_side
        + jnp.minimum(north_speed, 0.0) * north_side
        - lateral_mixing * (north_side - south_side)
    )
    return mask_pad[..., 1:-1, 1:-1] * (
        east_flux[..., :-1] - east_flux[..., 1:] + north_flux[..., :-1, :] - north_flux[..., 1:, :]
    )


def solve_columns(rhs_field, couple):
    level_count = couple.shape[0]
    ratios = []
    values = []
    upper_c = couple[0]
    denom = 1.0 + upper_c
    ratio_prev = -upper_c / denom
    value_prev = rhs_field[..., 0, :, :] / denom
    ratios.append(ratio_prev)
    values.append(value_prev)
    for level_index in range(1, level_count):
        lower_c = couple[level_index - 1]
        upper_c = couple[level_index]
        denom = 1.0 + lower_c + upper_c + lower_c * ratio_prev
        ratio_prev = -upper_c / denom
        value_prev = (rhs_field[..., level_index, :, :] + lower_c * value_prev) / denom
        ratios.append(ratio_prev)
        values.append(value_prev)
    result_rows = [values[level_count - 1]]
    for level_index in range(level_count - 2, -1, -1):
        result_rows.append(values[level_index] - ratios[level_index] * result_rows[-1])
    return jnp.stack(result_rows[::-1], axis=-3)


def fold_fix(inner_field, padded, halo_depth, sign_factors):
    row_count = inner_field.shape[2]
    ghosts = padded[:, :, row_count : row_count + halo_depth, ::-1][:, :, ::-1, :]
    ghost_shape = ghosts.shape
    flat_rows = ghosts.reshape(-1)
    total_count = flat_rows.shape[0]
    group_size = lax.axis_size("lon")
    piece_len = (total_count + group_size - 1) // group_size
    flat_rows = flat_rows.reshape(group_size, piece_len)
    spread = lax.all_to_all(flat_rows, "lon", split_axis=0, concat_axis=0, tiled=True)
    returned = lax.all_to_all(spread[::-1], "lon", split_axis=0, concat_axis=0, tiled=True)
    ghosts = returned.reshape(-1).reshape(ghost_shape)
    is_top = lax.axis_index("lat") == lax.axis_size("lat") - 1
    is_south = lax.axis_index("lat") == 0
    north_rows = jnp.where(is_top, sign_factors * ghosts, padded[:, :, row_count + halo_depth :, :])
    south_old = padded[:, :, :halo_depth, :]
    south_rows = jnp.where(is_south, jnp.zeros_like(south_old), south_old)
    return jnp.concatenate(
        [south_rows, padded[:, :, halo_depth : row_count + halo_depth, :], north_rows], axis=2
    )


def on_device(tracer, east_vel, north_vel, wet_mask, bottom_level, vertical_mix):
    tracer_count = tracer.shape[0]
    mask_float = wet_mask.astype(jnp.float32)
    stacked = jnp.concatenate([tracer, east_vel[None], north_vel[None], mask_float[None]], axis=0)
    tracer_signs = jnp.ones((tracer_count, 1, 1, 1), jnp.float32)
    sign_full = jnp.concatenate(
        [tracer_signs, -jnp.ones((2, 1, 1, 1), jnp.float32), jnp.ones((1, 1, 1, 1), jnp.float32)],
        axis=0,
    )
    level_ids = lax.broadcasted_iota(jnp.int32, vertical_mix.shape, 0)
    couple = jnp.where(level_ids + 1 < bottom_level[None, :, :], vertical_mix, jnp.float32(0.0))
    padded = extended(stacked, (("lat", 2), ("lon", 3)), 1)
    padded = fold_fix(stacked, padded, 1, sign_full)
    tracer_pad = padded[:tracer_count]
    east_pad = padded[tracer_count]
    north_pad = padded[tracer_count + 1]
    mask_pad = padded[tracer_count + 2]
    section_one = tracer + flux_sum(tracer_pad, east_pad, north_pad, mask_pad)
    again = extended(section_one, (("lat", 2), ("lon", 3)), 1)
    again = fold_fix(section_one, again, 1, tracer_signs)
    section_two = 0.5 * (tracer + section_one + flux_sum(again, east_pad, north_pad, mask_pad))
    return solve_columns(section_two, couple)


def solution(mesh):
    in_specs = (
        P(None, None, "lat", "lon"),
        P(None, "lat", "lon"),
        P(None, "lat", "lon"),
        P(None, "lat", "lon"),
        P("lat", "lon"),
        P(None, "lat", "lon"),
    )
    out_specs = P(None, None, "lat", "lon")
    return jax.shard_map(
        on_device, mesh=mesh, in_specs=in_specs, out_specs=out_specs, check_vma=False
    )
```

profile of v0, /device:TPU:1, one launch (start us, length us, event | category | flops | bytes accessed | tf_op | source)
XLA Modules:
  0.0 145.6 jit_solution(17640214490928353695)
XLA Ops:
  0.0 0.9 fusion.8
  0.9 1.1 copy.27
  2.0 0.9 copy_bitcast_fusion.2
  2.9 15.5 %collective-permute-start.1 = (f32[9,16,1,128]{3,1,0,2:T(8,128)S(1)}, f32[9,16,1,128]{3,1,0,2:T(8,128)S(1)}, u32[]{:S(2)}, u32[]{:S(2)}) collective-permute-start(f32[9,16,1,128]{3,1,0,2:T(8,128)S(1)} %get-tuple-element.74), channel_id=1, source_target_pairs={{32,0},{64,32},{96,64},{128,96},{160,128},{192,160},{224,192},{256... | collective-permute-start | bytes 221192 | tf_op jit(solution)/shard_map/ppermute | solution.py:18
  18.4 1.9 %collective-permute-start = (f32[9,16,1,128]{3,1,0,2:T(8,128)S(1)}, f32[9,16,1,128]{3,1,0,2:T(8,128)S(1)}, u32[]{:S(2)}, u32[]{:S(2)}) collective-permute-start(f32[9,16,1,128]{3,1,0,2:T(8,128)S(1)} %get-tuple-element.73), channel_id=1, source_target_pairs={{0,32},{32,64},{64,96},{96,128},{128,160},{160,192},{192,224},{224... | collective-permute-start | bytes 221192 | tf_op jit(solution)/shard_map/ppermute | solution.py:16
  20.4 0.6 fusion.27
  21.1 0.6 fusion.28
  21.7 0.6 fusion.29
  22.3 0.6 fusion.30
  22.9 0.6 fusion.31
  23.5 0.6 fusion.32
  24.1 0.6 fusion.33
  24.7 5.1 %collective-permute-done = f32[9,16,1,128]{3,1,0,2:T(8,128)S(1)} collective-permute-done((f32[9,16,1,128]{3,1,0,2:T(8,128)S(1)}, f32[9,16,1,128]{3,1,0,2:T(8,128)S(1)}, u32[]{:S(2)}, u32[]{:S(2)}) %collective-permute-start) | collective-permute-done | bytes 73760 | tf_op jit(solution)/shard_map/ppermute | solution.py:16
  29.9 0.3 fusion.55
  30.1 0.6 copy.19
  30.7 7.3 %collective-permute-start.3 = (f32[9,16,10,1]{1,3,2,0:T(1,128)S(1)}, f32[9,16,10,1]{1,3,2,0:T(1,128)S(1)}, u32[]{:S(2)}, u32[]{:S(2)}) collective-permute-start(f32[9,16,10,1]{1,3,2,0:T(1,128)S(1)} %copy.19), channel_id=1, source_target_pairs={{1,0},{2,1},{3,2},{4,3},{5,4},{6,5},{7,6},{8,7},{9,8},{10,9},{11,1... | collective-permute-start | bytes 17288 | tf_op jit(solution)/shard_map/ppermute | solution.py:18
  38.0 0.6 copy.18
  38.6 3.2 %collective-permute-start.2 = (f32[9,16,10,1]{1,3,2,0:T(1,128)S(1)}, f32[9,16,10,1]{1,3,2,0:T(1,128)S(1)}, u32[]{:S(2)}, u32[]{:S(2)}) collective-permute-start(f32[9,16,10,1]{1,3,2,0:T(1,128)S(1)} %copy.18), channel_id=1, source_target_pairs={{0,1},{1,2},{2,3},{3,4},{4,5},{5,6},{6,7},{7,8},{8,9},{9,10},{10,1... | collective-permute-start | bytes 17288 | tf_op jit(solution)/shard_map/ppermute | solution.py:16
  41.8 0.6 fusion.34
  42.4 0.6 copy.21
  43.0 0.3 collective-permute-done.2
  43.3 0.6 copy.20
  43.9 0.6 pad_maximum_fusion
  44.6 1.1 copy-done
  46.0 0.8 all_to_all.38
  46.8 10.2 %all-to-all-start = ((f32[32,1,585]{2,1,0:T(1,128)}), f32[32,1,585]{2,1,0:T(1,128)S(1)}, u32[]{:S(2)}, u32[]{:S(2)}) async-start(f32[32,1,585]{2,1,0:T(1,128)} %all_to_all.38), calls=%async_computation | async-start | bytes 163840 | tf_op jit(solution)/shard_map/all_to_all | solution.py:82
  57.0 0.6 fusion.35
  57.6 0.6 fusion.36
  58.2 6.9 %all-to-all-done = f32[32,1,585]{2,1,0:T(1,128)S(1)} async-done(((f32[32,1,585]{2,1,0:T(1,128)}), f32[32,1,585]{2,1,0:T(1,128)S(1)}, u32[]{:S(2)}, u32[]{:S(2)}) %all-to-all-start) | async-done | bytes 74912 | tf_op jit(solution)/shard_map/all_to_all | solution.py:82
  65.3 0.7 copy.23
  66.0 4.1 %all-to-all-start.1 = ((f32[32,1,585]{2,1,0:T(1,128)}), f32[32,1,585]{2,1,0:T(1,128)S(1)}, u32[]{:S(2)}, u32[]{:S(2)}) async-start(f32[32,1,585]{2,1,0:T(1,128)} %copy.23), calls=%async_computation.1 | async-start | bytes 163840 | tf_op jit(solution)/shard_map/all_to_all | solution.py:83
  70.0 0.6 fusion.37
  70.7 0.6 fusion.38
  71.3 1.4 slice.350
  72.6 5.6 %all-to-all-done.1 = f32[32,1,585]{2,1,0:T(1,128)S(1)} async-done(((f32[32,1,585]{2,1,0:T(1,128)}), f32[32,1,585]{2,1,0:T(1,128)S(1)}, u32[]{:S(2)}, u32[]{:S(2)}) %all-to-all-start.1) | async-done | bytes 74912 | tf_op jit(solution)/shard_map/all_to_all | solution.py:83
  78.5 1.1 slice_select_fusion.1
  80.2 0.3 subtract_multiply_fusion.3
  80.9 0.3 subtract_multiply_fusion.1
  81.3 0.6 copy-done.1
  82.1 1.9 %collective-permute-start.5 = (f32[6,16,1,128]{3,1,0,2:T(8,128)S(1)}, f32[6,16,1,128]{3,1,0,2:T(8,128)S(1)}, u32[]{:S(2)}, u32[]{:S(2)}) collective-permute-start(f32[6,16,1,128]{3,1,0,2:T(8,128)S(1)} %get-tuple-element.78), channel_id=1, source_target_pairs={{32,0},{64,32},{96,64},{128,96},{160,128},{192,160},{224,192},{256... | collective-permute-start | bytes 147464 | tf_op jit(solution)/shard_map/ppermute | solution.py:18
  84.0 3.4 %collective-permute-start.4 = (f32[6,16,1,128]{3,1,0,2:T(8,128)S(1)}, f32[6,16,1,128]{3,1,0,2:T(8,128)S(1)}, u32[]{:S(2)}, u32[]{:S(2)}) collective-permute-start(f32[6,16,1,128]{3,1,0,2:T(8,128)S(1)} %get-tuple-element.77), channel_id=1, source_target_pairs={{0,32},{32,64},{64,96},{96,128},{128,160},{160,192},{192,224},{224... | collective-permute-start | bytes 147464 | tf_op jit(solution)/shard_map/ppermute | solution.py:16
  87.4 0.6 fusion.39
  88.0 10.2 %collective-permute-done.4 = f32[6,16,1,128]{3,1,0,2:T(8,128)S(1)} collective-permute-done((f32[6,16,1,128]{3,1,0,2:T(8,128)S(1)}, f32[6,16,1,128]{3,1,0,2:T(8,128)S(1)}, u32[]{:S(2)}, u32[]{:S(2)}) %collective-permute-start.4) | collective-permute-done | bytes 49184 | tf_op jit(solution)/shard_map/ppermute | solution.py:16
  98.3 0.2 fusion.56
  98.5 2.5 %collective-permute-start.7 = (f32[6,16,10,1]{3,1,0,2:T(8,128)S(1)}, f32[6,16,10,1]{3,1,0,2:T(8,128)S(1)}, u32[]{:S(2)}, u32[]{:S(2)}) collective-permute-start(f32[6,16,10,1]{3,1,0,2:T(8,128)S(1)} %get-tuple-element.76), channel_id=1, source_target_pairs={{1,0},{2,1},{3,2},{4,3},{5,4},{6,5},{7,6},{8,7},{9,8},{10,9},{11,1... | collective-permute-start | bytes 11528 | tf_op jit(solution)/shard_map/ppermute | solution.py:18
  101.0 3.1 %collective-permute-start.6 = (f32[6,16,10,1]{3,1,0,2:T(8,128)S(1)}, f32[6,16,10,1]{3,1,0,2:T(8,128)S(1)}, u32[]{:S(2)}, u32[]{:S(2)}) collective-permute-start(f32[6,16,10,1]{3,1,0,2:T(8,128)S(1)} %get-tuple-element.75), channel_id=1, source_target_pairs={{0,1},{1,2},{2,3},{3,4},{4,5},{5,6},{6,7},{7,8},{8,9},{9,10},{10,1... | collective-permute-start | bytes 11528 | tf_op jit(solution)/shard_map/ppermute | solution.py:16
  104.1 0.6 fusion.40
  104.7 9.5 %collective-permute-done.7 = f32[6,16,10,1]{3,1,0,2:T(8,128)S(1)} collective-permute-done((f32[6,16,10,1]{3,1,0,2:T(8,128)S(1)}, f32[6,16,10,1]{3,1,0,2:T(8,128)S(1)}, u32[]{:S(2)}, u32[]{:S(2)}) %collective-permute-start.7) | collective-permute-done | bytes 3872 | tf_op jit(solution)/shard_map/ppermute | solution.py:18
  114.6 0.8 all_to_all.39
  115.5 4.4 %all-to-all-start.2 = ((f32[32,1,390]{2,1,0:T(1,128)}), f32[32,1,390]{2,1,0:T(1,128)S(1)}, u32[]{:S(2)}, u32[]{:S(2)}) async-start(f32[32,1,390]{2,1,0:T(1,128)} %all_to_all.39), calls=%async_computation.2 | async-start | bytes 131072 | tf_op jit(solution)/shard_map/all_to_all | solution.py:82
  119.8 0.7 fusion.25
  120.5 0.4 pad_maximum_fusion.1
  121.0 6.8 %all-to-all-done.2 = f32[32,1,390]{2,1,0:T(1,128)S(1)} async-done(((f32[32,1,390]{2,1,0:T(1,128)}), f32[32,1,390]{2,1,0:T(1,128)S(1)}, u32[]{:S(2)}, u32[]{:S(2)}) %all-to-all-start.2) | async-done | bytes 49952 | tf_op jit(solution)/shard_map/all_to_all | solution.py:82
  127.8 0.7 copy.29
  128.5 4.0 %all-to-all-start.3 = ((f32[32,1,390]{2,1,0:T(1,128)}), f32[32,1,390]{2,1,0:T(1,128)S(1)}, u32[]{:S(2)}, u32[]{:S(2)}) async-start(f32[32,1,390]{2,1,0:T(1,128)} %copy.29), calls=%async_computation.3 | async-start | bytes 131072 | tf_op jit(solution)/shard_map/all_to_all | solution.py:83
  132.5 1.2 subtract_multiply_fusion
  133.7 6.7 %all-to-all-done.3 = f32[32,1,390]{2,1,0:T(1,128)S(1)} async-done(((f32[32,1,390]{2,1,0:T(1,128)}), f32[32,1,390]{2,1,0:T(1,128)S(1)}, u32[]{:S(2)}, u32[]{:S(2)}) %all-to-all-start.3) | async-done | bytes 49952 | tf_op jit(solution)/shard_map/all_to_all | solution.py:83
  140.8 0.7 slice-done
  141.5 0.3 subtract_multiply_fusion.2
  142.2 0.2 fusion.2
  142.7 0.6 fusion.10
  143.5 0.5 multiply_subtract_fusion
  144.0 0.6 stack.2
  144.6 1.0 copy.30
  (141 shorter events, 3.3 us)
Async XLA Ops:
  0.0 20.3 %copy-start.20 = (f32[16,8,128]{2,1,0:T(8,128)S(1)}, f32[16,8,128]{2,1,0:T(8,128)}, u32[]{:S(2)}) copy-start(f32[16,8,128]{2,1,0:T(8,128)} %param.11) | copy-start | bytes 196612
  0.0 20.3 %copy-start.53 = (s32[8,128]{1,0:T(8,128)S(1)}, s32[8,128]{1,0:T(8,128)}, u32[]{:S(2)}) copy-start(s32[8,128]{1,0:T(8,128)} %param.10) | copy-start | bytes 12292
  2.9 21.8 %collective-permute-start.1 = (f32[9,16,1,128]{3,1,0,2:T(8,128)S(1)}, f32[9,16,1,128]{3,1,0,2:T(8,128)S(1)}, u32[]{:S(2)}, u32[]{:S(2)}) collective-permute-start(f32[9,16,1,128]{3,1,0,2:T(8,128)S(1)} %get-tuple-element.74), channel_id=1, source_target_pairs={{32,0},{64,32},{96,64},{128,96},{160,128},{192,160},{224,192},{256... | collective-permute-start | bytes 221192 | tf_op jit(solution)/shard_map/ppermute | solution.py:18
  18.4 11.4 %collective-permute-start = (f32[9,16,1,128]{3,1,0,2:T(8,128)S(1)}, f32[9,16,1,128]{3,1,0,2:T(8,128)S(1)}, u32[]{:S(2)}, u32[]{:S(2)}) collective-permute-start(f32[9,16,1,128]{3,1,0,2:T(8,128)S(1)} %get-tuple-element.73), channel_id=1, source_target_pairs={{0,32},{32,64},{64,96},{96,128},{128,160},{160,192},{192,224},{224... | collective-permute-start | bytes 221192 | tf_op jit(solution)/shard_map/ppermute | solution.py:16
  20.4 50.2 %copy-start.6 = (f32[16,8,128]{2,1,0:T(8,128)}, f32[16,8,128]{2,1,0:T(8,128)S(1)}, u32[]{:S(2)}) copy-start(f32[16,8,128]{2,1,0:T(8,128)S(1)} %compare_select_fusion) | copy-start | bytes 196612
  24.7 19.2 %copy-start.14 = (f32[9,16,1,128]{3,1,0,2:T(8,128)}, f32[9,16,1,128]{3,1,0,2:T(8,128)S(1)}, u32[]{:S(2)}) copy-start(f32[9,16,1,128]{3,1,0,2:T(8,128)S(1)} %collective-permute-done.1) | copy-start | bytes 221188
  29.8 14.1 %copy-start.16 = (f32[9,16,1,128]{3,1,0,2:T(8,128)}, f32[9,16,1,128]{3,1,0,2:T(8,128)S(1)}, u32[]{:S(2)}) copy-start(f32[9,16,1,128]{3,1,0,2:T(8,128)S(1)} %collective-permute-done) | copy-start | bytes 221188
  30.7 11.7 %collective-permute-start.3 = (f32[9,16,10,1]{1,3,2,0:T(1,128)S(1)}, f32[9,16,10,1]{1,3,2,0:T(1,128)S(1)}, u32[]{:S(2)}, u32[]{:S(2)}) collective-permute-start(f32[9,16,10,1]{1,3,2,0:T(1,128)S(1)} %copy.19), channel_id=1, source_target_pairs={{1,0},{2,1},{3,2},{4,3},{5,4},{6,5},{7,6},{8,7},{9,8},{10,9},{11,1... | collective-permute-start | bytes 17288 | tf_op jit(solution)/shard_map/ppermute | solution.py:18
  38.6 4.7 %collective-permute-start.2 = (f32[9,16,10,1]{1,3,2,0:T(1,128)S(1)}, f32[9,16,10,1]{1,3,2,0:T(1,128)S(1)}, u32[]{:S(2)}, u32[]{:S(2)}) collective-permute-start(f32[9,16,10,1]{1,3,2,0:T(1,128)S(1)} %copy.18), channel_id=1, source_target_pairs={{0,1},{1,2},{2,3},{3,4},{4,5},{5,6},{6,7},{7,8},{8,9},{9,10},{10,1... | collective-permute-start | bytes 17288 | tf_op jit(solution)/shard_map/ppermute | solution.py:16
  44.5 1.1 copy-start
  46.8 18.3 %all-to-all-start = ((f32[32,1,585]{2,1,0:T(1,128)}), f32[32,1,585]{2,1,0:T(1,128)S(1)}, u32[]{:S(2)}, u32[]{:S(2)}) async-start(f32[32,1,585]{2,1,0:T(1,128)} %all_to_all.38), calls=%async_computation | async-start | bytes 163840 | tf_op jit(solution)/shard_map/all_to_all | solution.py:82
  66.0 12.5 %copy-start.54 = (f32[9]{0:T(128)S(1)}, f32[9]{0:T(128)}, u32[]{:S(2)}) copy-start(f32[9]{0:T(128)} %constant.15.clone.1) | copy-start | bytes 112
  66.0 12.2 %all-to-all-start.1 = ((f32[32,1,585]{2,1,0:T(1,128)}), f32[32,1,585]{2,1,0:T(1,128)S(1)}, u32[]{:S(2)}, u32[]{:S(2)}) async-start(f32[32,1,585]{2,1,0:T(1,128)} %copy.23), calls=%async_computation.1 | async-start | bytes 163840 | tf_op jit(solution)/shard_map/all_to_all | solution.py:83
  79.8 0.8 copy-start.8
  79.9 1.3 copy-start.18
  80.0 0.9 copy-start.15
  80.0 0.9 copy-start.17
  80.2 1.0 copy-start.4
  80.9 1.0 copy-start.1
  81.9 5.5 %copy-start.7 = (f32[16,8,128]{2,1,0:T(8,128)S(1)}, f32[16,8,128]{2,1,0:T(8,128)}, u32[]{:S(2)}) copy-start(f32[16,8,128]{2,1,0:T(8,128)} %copy-done.6) | copy-start | bytes 196612
  82.1 5.9 %collective-permute-start.5 = (f32[6,16,1,128]{3,1,0,2:T(8,128)S(1)}, f32[6,16,1,128]{3,1,0,2:T(8,128)S(1)}, u32[]{:S(2)}, u32[]{:S(2)}) collective-permute-start(f32[6,16,1,128]{3,1,0,2:T(8,128)S(1)} %get-tuple-element.78), channel_id=1, source_target_pairs={{32,0},{64,32},{96,64},{128,96},{160,128},{192,160},{224,192},{256... | collective-permute-start | bytes 147464 | tf_op jit(solution)/shard_map/ppermute | solution.py:18
  84.0 14.2 %collective-permute-start.4 = (f32[6,16,1,128]{3,1,0,2:T(8,128)S(1)}, f32[6,16,1,128]{3,1,0,2:T(8,128)S(1)}, u32[]{:S(2)}, u32[]{:S(2)}) collective-permute-start(f32[6,16,1,128]{3,1,0,2:T(8,128)S(1)} %get-tuple-element.77), channel_id=1, source_target_pairs={{0,32},{32,64},{64,96},{96,128},{128,160},{160,192},{192,224},{224... | collective-permute-start | bytes 147464 | tf_op jit(solution)/shard_map/ppermute | solution.py:16
  98.5 15.7 %collective-permute-start.7 = (f32[6,16,10,1]{3,1,0,2:T(8,128)S(1)}, f32[6,16,10,1]{3,1,0,2:T(8,128)S(1)}, u32[]{:S(2)}, u32[]{:S(2)}) collective-permute-start(f32[6,16,10,1]{3,1,0,2:T(8,128)S(1)} %get-tuple-element.76), channel_id=1, source_target_pairs={{1,0},{2,1},{3,2},{4,3},{5,4},{6,5},{7,6},{8,7},{9,8},{10,9},{11,1... | collective-permute-start | bytes 11528 | tf_op jit(solution)/shard_map/ppermute | solution.py:18
  101.0 13.2 %collective-permute-start.6 = (f32[6,16,10,1]{3,1,0,2:T(8,128)S(1)}, f32[6,16,10,1]{3,1,0,2:T(8,128)S(1)}, u32[]{:S(2)}, u32[]{:S(2)}) collective-permute-start(f32[6,16,10,1]{3,1,0,2:T(8,128)S(1)} %get-tuple-element.75), channel_id=1, source_target_pairs={{0,1},{1,2},{2,3},{3,4},{4,5},{5,6},{6,7},{7,8},{8,9},{9,10},{10,1... | collective-permute-start | bytes 11528 | tf_op jit(solution)/shard_map/ppermute | solution.py:16
  115.5 12.3 %all-to-all-start.2 = ((f32[32,1,390]{2,1,0:T(1,128)}), f32[32,1,390]{2,1,0:T(1,128)S(1)}, u32[]{:S(2)}, u32[]{:S(2)}) async-start(f32[32,1,390]{2,1,0:T(1,128)} %all_to_all.39), calls=%async_computation.2 | async-start | bytes 131072 | tf_op jit(solution)/shard_map/all_to_all | solution.py:82
  121.0 12.8 %copy-start.2 = (f32[6,16,10,130]{3,1,0,2:T(8,128)}, f32[6,16,10,130]{3,1,0,2:T(8,128)S(1)}, u32[]{:S(2)}) copy-start(f32[6,16,10,130]{3,1,0,2:T(8,128)S(1)} %pad_maximum_fusion.1) | copy-start | bytes 1497604
  121.0 11.5 %copy-start.5 = (f32[16,8,129]{2,0,1:T(8,128)S(1)}, f32[16,8,129]{2,0,1:T(8,128)}, u32[]{:S(2)}) copy-start(f32[16,8,129]{2,0,1:T(8,128)} %copy-done.4) | copy-start | bytes 198148
  128.5 11.9 %all-to-all-start.3 = ((f32[32,1,390]{2,1,0:T(1,128)}), f32[32,1,390]{2,1,0:T(1,128)S(1)}, u32[]{:S(2)}, u32[]{:S(2)}) async-start(f32[32,1,390]{2,1,0:T(1,128)} %copy.29), calls=%async_computation.3 | async-start | bytes 131072 | tf_op jit(solution)/shard_map/all_to_all | solution.py:83
  133.7 7.1 %copy-start.9 = (f32[16,9,128]{2,0,1:T(8,128)S(1)}, f32[16,9,128]{2,0,1:T(8,128)}, u32[]{:S(2)}) copy-start(f32[16,9,128]{2,0,1:T(8,128)} %copy-done.8) | copy-start | bytes 221188
  133.7 7.1 %copy-start.11 = (f32[16,9,128]{2,0,1:T(8,128)S(1)}, f32[16,9,128]{2,0,1:T(8,128)}, u32[]{:S(2)}) copy-start(f32[16,9,128]{2,0,1:T(8,128)} %copy-done.10) | copy-start | bytes 221188
  133.7 7.1 %copy-start.13 = (f32[16,9,128]{2,0,1:T(8,128)S(1)}, f32[16,9,128]{2,0,1:T(8,128)}, u32[]{:S(2)}) copy-start(f32[16,9,128]{2,0,1:T(8,128)} %copy-done.12) | copy-start | bytes 221188
  140.4 1.1 slice-start
  140.7 1.2 copy-start.3
  140.7 1.2 copy-start.19
  141.9 0.7 copy-start.39
  141.9 0.7 copy-start.40
  141.9 0.7 copy-start.41
  141.9 0.7 copy-start.42
  141.9 0.7 copy-start.43
  141.9 0.7 copy-start.44
  141.9 0.7 copy-start.45
  141.9 0.7 copy-start.46
  142.0 0.7 copy-start.47
  142.0 0.7 copy-start.48
  142.0 0.7 copy-start.49
  142.0 0.7 copy-start.50
  142.0 0.7 copy-start.51
  142.0 1.3 copy-start.21
  142.0 1.3 copy-start.22
  142.0 1.3 copy-start.23
  142.0 1.3 copy-start.24
  142.0 1.3 copy-start.25
  142.1 1.3 copy-start.26
  142.1 1.3 copy-start.27
  142.1 1.3 copy-start.28
  142.1 1.3 copy-start.29
  142.1 1.3 copy-start.30
  142.1 1.3 copy-start.31
  142.1 1.3 copy-start.32
  142.1 1.3 copy-start.33
  142.1 1.3 copy-start.34
  142.1 1.3 copy-start.35
  142.2 1.3 copy-start.36
  142.2 1.3 copy-start.52
  (4 other events, 2.6 us)
where the time goes:
time: 147 us; the launch traced here: 146 us
  starting transfers between devices  61.3 us (42%)
  waiting for transfers between devices  51.1 us (35%)
  other arithmetic  17.2 us (12%)
  local copies, waits for them, and re-layouts  15.1 us (10%)
    ppermute x4, starting transfers between devices, extended(): lax.ppermute(head, axis, [((i + 1) % count, i) for i in range(count)])  27.1 us
    ppermute x4, waiting for transfers between devices, extended(): lax.ppermute(tail, axis, [(i, (i + 1) % count) for i in range(count)])  15.6 us
    all_to_all x2, starting transfers between devices, fold_fix(): lax.all_to_all(flat_rows, 'lon', split_axis=0, concat_axis=0, tiled=True)  14.5 us
    all_to_all x2, waiting for transfers between devices, fold_fix(): lax.all_to_all(flat_rows, 'lon', split_axis=0, concat_axis=0, tiled=True)  13.7 us
    all_to_all x2, waiting for transfers between devices, fold_fix(): lax.all_to_all(spread[::-1], 'lon', split_axis=0, concat_axis=0, tiled=True)  12.2 us
    ppermute x4, starting transfers between devices, extended(): lax.ppermute(tail, axis, [(i, (i + 1) % count) for i in range(count)])  11.6 us
    ppermute x4, waiting for transfers between devices, extended(): lax.ppermute(head, axis, [((i + 1) % count, i) for i in range(count)])  9.54 us
    mul x14, other arithmetic, solve_columns(): ratios[level_index] * result_rows[-1]  8.5 us
  transfers between devices with their start and end apart: 12, of which 8 were waited for; matrix products, arithmetic and copies ran while one was open for 9% of the time, Pallas kernels for 0%

commit v1 on v0

v1 whole, which is shorter than its diff:
```python
import jax
import jax.numpy as jnp
from jax import lax
from jax.experimental import pallas as pl
from jax.experimental.pallas import tpu as pltpu
from jax.sharding import PartitionSpec as P

ROWS = 8
COLS = 128
NT = 6
K = 16
TILES = NT * K
mixing = 0.08
AXES = ("lat", "lon")

FIELDS = NT + 3
PACKS = (FIELDS + 1) // 2
PACK_ROWS = PACKS * ROWS
TPACKS = NT // 2

ROW_T = 0
ROW_P = TILES
ROW_V = 2 * TILES
ROW_M = ROW_V + K
ROW_C = ROW_M + K
PAY_ROWS = ROW_C + ROWS

AUX_F = 0
AUX_Q = TPACKS
AUX_T = 2 * TPACKS
AUX_V = 3 * TPACKS
AUX_M = AUX_V + 1
AUX_A = AUX_M + 1
AUX_B = AUX_A + 1
AUX = AUX_T + ROWS


def roll(x, shift, axis):
    shift %= x.shape[axis]
    return pltpu.roll(x, shift, axis) if shift else x


def lanes(rows=ROWS):
    return lax.broadcasted_iota(jnp.int32, (rows, COLS), 1)


def row_ids():
    return lax.broadcasted_iota(jnp.int32, (ROWS, COLS), 0)


def face(speed, opening):
    return opening * (jnp.maximum(speed, 0.0) + mixing), opening * (jnp.minimum(speed, 0.0) - mixing)


def tile(ref, index):
    return ref[index * ROWS : (index + 1) * ROWS, :]


def edge_kernel(tracer, east, north, mask, pack):
    group = lanes() // 4
    for half_pair in range(PACKS):
        total = jnp.zeros((ROWS, COLS), jnp.float32)
        for half in range(2):
            field = 2 * half_pair + half
            if field >= FIELDS:
                continue
            for k in range(K):
                if field < NT:
                    x = tile(tracer, field * K + k)
                elif field == NT:
                    x = tile(east, k)
                elif field == NT + 1:
                    x = tile(mask, k).astype(jnp.float32)
                else:
                    x = tile(north, k)
                base = 64 * half + 4 * k
                total = jnp.where(group == base // 4, roll(x, base - 126, 1), total)
        pack[half_pair * ROWS : (half_pair + 1) * ROWS, :] = total


def level_faces(east, north, mask, k):
    u, v, m = tile(east, k), tile(north, k), tile(mask, k).astype(jnp.float32)
    inner_x = lanes() < COLS - 1
    inner_y = row_ids() < ROWS - 1
    open_x = jnp.where(inner_x, m * roll(m, -1, 1), 0.0)
    open_y = jnp.where(inner_y, m * roll(m, -1, 0), 0.0)
    ax, bx = face(0.5 * (u + roll(u, -1, 1)), open_x)
    ay, by = face(0.5 * (v + roll(v, -1, 0)), open_y)
    return ax, bx, ay, by


def inner_sum(t, faces):
    ax, bx, ay, by = faces
    fe = ax * t + bx * roll(t, -1, 1)
    gn = ay * t + by * roll(t, -1, 0)
    return (roll(fe, 1, 1) - fe) + (roll(gn, 1, 0) - gn)


def edge_sign():
    lane = lanes()
    return jnp.where(lane == 0, 1.0, jnp.where(lane == COLS - 1, -1.0, 0.0))


def spread(packed, field, k):
    return roll(packed, COLS - 1 - (64 * (field % 2) + 4 * k + 1), 1)


def both_halves(x, half):
    swapped = roll(x, 64, 1)
    low = lanes() < 64
    return jnp.where(low, x, swapped) if half == 0 else jnp.where(low, swapped, x)


def flipped(x):
    lane = lanes(x.shape[0])
    for step in (1, 2, 4, 8, 16, 32, 64):
        x = jnp.where((lane & step) != 0, roll(x, step, 1), roll(x, -step, 1))
    return x


def first_kernel(own, near, far, tracer, east, north, mask, pay_far, pay_near, part, aux):
    lat_odd = lax.rem(lax.axis_index("lat"), 2)
    lon_odd = lax.rem(lax.axis_index("lon"), 2)
    is_top = lax.axis_index("lat") == lax.axis_size("lat") - 1
    at_east = (lanes() & 3) == 1
    even = lon_odd == 0
    offset = pl.multiple_of((1 - lon_odd) * PACK_ROWS, ROWS)
    one, two, here = [], [], []
    for p in range(PACKS):
        a = near[pl.ds(pl.multiple_of(offset + p * ROWS, ROWS), ROWS), :]
        b = tile(far, p)
        e = jnp.where(even, a, b)
        w = jnp.where(even, b, a)
        here.append(tile(own, p))
        one.append(jnp.where(at_east, roll(e, -1, 1), roll(w, 1, 1)))
        two.append(jnp.where(at_east, roll(e, -2, 1), roll(w, 2, 1)))
    u0, m0 = both_halves(here[TPACKS], 0), both_halves(here[TPACKS], 1)
    u1, m1 = both_halves(one[TPACKS], 0), both_halves(one[TPACKS], 1)
    u2, m2 = both_halves(two[TPACKS], 0), both_halves(two[TPACKS], 1)
    v1 = both_halves(one[TPACKS + 1], 0)
    a1, b1 = face(0.5 * (u0 + u1), m0 * m1)
    a2, b2 = face(0.5 * (u1 + u2), m1 * m2)
    inner_y = row_ids() < ROWS - 1
    ay, by = face(0.5 * (v1 + roll(v1, -1, 0)), jnp.where(inner_y, m1 * roll(m1, -1, 0), 0.0))
    flux = []
    for p in range(TPACKS):
        t0, t1, t2 = here[p], one[p], two[p]
        f1 = a1 * jnp.where(at_east, t0, t1) + b1 * jnp.where(at_east, t1, t0)
        f2 = a2 * jnp.where(at_east, t1, t2) + b2 * jnp.where(at_east, t2, t1)
        gn = ay * t1 + by * roll(t1, -1, 0)
        flux.append(f1)
        q = t1 + jnp.where(at_east, -f2, f2) + (roll(gn, 1, 0) - gn)
        aux[(AUX_F + p) * ROWS : (AUX_F + p + 1) * ROWS, :] = f1
        aux[(AUX_Q + p) * ROWS : (AUX_Q + p + 1) * ROWS, :] = q
        aux[(AUX_T + p) * ROWS : (AUX_T + p + 1) * ROWS, :] = t1
    for place, x in ((AUX_V, v1), (AUX_M, m1), (AUX_A, a1), (AUX_B, b1)):
        aux[place * ROWS : (place + 1) * ROWS, :] = x
    for place in range(AUX_B + 1, AUX):
        aux[place * ROWS : (place + 1) * ROWS, :] = jnp.zeros((ROWS, COLS), jnp.float32)
    sign = edge_sign()
    for k in range(K):
        faces = level_faces(east, north, mask, k)
        for f in range(NT):
            t = tile(tracer, f * K + k)
            index = f * K + k
            part[index * ROWS : (index + 1) * ROWS, :] = (
                t + inner_sum(t, faces) + sign * spread(flux[f // 2], f, k)
            )
    for pay, row in ((pay_far, (ROWS - 1) * lat_odd), (pay_near, (ROWS - 1) * (1 - lat_odd))):
        pay[ROW_T : ROW_T + TILES, :] = tracer[pl.ds(row, TILES, stride=ROWS), :]
        pay[ROW_P : ROW_P + TILES, :] = part[pl.ds(row, TILES, stride=ROWS), :]
        pay[ROW_V : ROW_V + K, :] = north[pl.ds(row, K, stride=ROWS), :]
        pay[ROW_M : ROW_M + K, :] = mask[pl.ds(row, K, stride=ROWS), :].astype(jnp.float32)
        pay[ROW_C : ROW_C + ROWS, :] = aux[pl.ds(AUX_T * ROWS + row, ROWS, stride=ROWS), :]

    @pl.when(is_top)
    def _():
        for start in range(0, ROW_C, K):
            x = flipped(pay_far[start : start + K, :])
            pay_far[start : start + K, :] = -x if start == ROW_V else x
        c = pay_far[ROW_C : ROW_C + ROWS, :]
        c = jnp.where(at_east, roll(c, -1, 1), roll(c, 1, 1))
        pay_far[ROW_C : ROW_C + ROWS, :] = jnp.where(row_ids() == TPACKS, -c, c)


def last_kernel(far, near, tracer, east, north, mask, mix, bottom, part, aux, out, face_n, face_s, one):
    lat_odd = lax.rem(lax.axis_index("lat"), 2)
    odd = lat_odd == 1
    offset = pl.multiple_of((1 - lat_odd) * PAY_ROWS, ROWS)
    at_east = (lanes() & 3) == 1
    rows = row_ids()
    at_south, at_north = rows == 0, rows == ROWS - 1

    def both(start, size):
        a = far[start : start + size, :]
        b = near[pl.ds(pl.multiple_of(offset + start, ROWS), size), :]
        return jnp.where(odd, a, b), jnp.where(odd, b, a)

    def edge(ref, start, size, row):
        return ref[pl.ds(start * ROWS + row, size, stride=ROWS), :]

    v_n, v_s = both(ROW_V, K)
    m_n, m_s = both(ROW_M, K)
    c_n, c_s = both(ROW_C, ROWS)
    an, bn = face(
        0.5 * (edge(north, 0, K, ROWS - 1) + v_n), edge(mask, 0, K, ROWS - 1).astype(jnp.float32) * m_n
    )
    as_, bs = face(0.5 * (v_s + edge(north, 0, K, 0)), m_s * edge(mask, 0, K, 0).astype(jnp.float32))
    s_n, s_s = [], []
    for f in range(NT):
        t_n, t_s = both(ROW_T + f * K, K)
        p_n, p_s = both(ROW_P + f * K, K)
        g_n = an * edge(tracer, f * K, K, ROWS - 1) + bn * t_n
        g_s = as_ * t_s + bs * edge(tracer, f * K, K, 0)
        face_n[f * K : (f + 1) * K, :] = g_n
        face_s[f * K : (f + 1) * K, :] = g_s
        s_n.append(p_n + g_n)
        s_s.append(p_s - g_s)

    def outer(index):
        return jnp.where(at_south, face_s[index : index + 1, :], 0.0) - jnp.where(
            at_north, face_n[index : index + 1, :], 0.0
        )

    group = lanes() // 4
    own = []
    for p in range(TPACKS):
        packed = jnp.zeros((ROWS, COLS), jnp.float32)
        for f in (2 * p, 2 * p + 1):
            for k in range(K):
                index = f * K + k
                s = tile(part, index) + outer(index)
                one[index * ROWS : (index + 1) * ROWS, :] = s
                base = 64 * (f % 2) + 4 * k
                packed = jnp.where(group == base // 4, roll(s, base - 126, 1), packed)
        own.append(packed)
    v1, m1, a1, b1 = (tile(aux, x) for x in (AUX_V, AUX_M, AUX_A, AUX_B))
    acn, bcn = face(0.5 * (v1 + c_n[TPACKS : TPACKS + 1]), m1 * c_n[TPACKS + 1 : TPACKS + 2])
    acs, bcs = face(0.5 * (c_s[TPACKS : TPACKS + 1] + v1), c_s[TPACKS + 1 : TPACKS + 2] * m1)
    flux = []
    for p in range(TPACKS):
        f1, q, t1 = tile(aux, AUX_F + p), tile(aux, AUX_Q + p), tile(aux, AUX_T + p)
        gcn = acn * t1 + bcn * c_n[p : p + 1]
        gcs = acs * c_s[p : p + 1] + bcs * t1
        s1 = (
            q
            + jnp.where(at_east, f1, -f1)
            + jnp.where(at_south, gcs, 0.0)
            - jnp.where(at_north, gcn, 0.0)
        )
        flux.append(a1 * jnp.where(at_east, own[p], s1) + b1 * jnp.where(at_east, s1, own[p]))
    for f in range(NT):
        face_n[f * K : (f + 1) * K, :] = an * edge(one, f * K, K, ROWS - 1) + bn * s_n[f]
        face_s[f * K : (f + 1) * K, :] = as_ * s_s[f] + bs * edge(one, f * K, K, 0)

    depth = bottom[...]
    sign = edge_sign()
    values = [None] * NT
    lower = None
    ratios = []
    for k in range(K):
        faces = level_faces(east, north, mask, k)
        upper = jnp.where(k + 1 < depth, tile(mix, k), 0.0) if k + 1 < K else None
        denom = 1.0
        if upper is not None:
            denom = denom + upper
        if k:
            denom = denom + lower + lower * ratios[-1]
        inverse = 1.0 / denom
        if upper is not None:
            ratios.append(-upper * inverse)
        for f in range(NT):
            index = f * K + k
            s = tile(one, index)
            total = inner_sum(s, faces) + sign * spread(flux[f // 2], f, k) + outer(index)
            rhs = 0.5 * ((tile(tracer, index) + s) + total)
            if k:
                rhs = rhs + lower * values[f]
            values[f] = rhs * inverse
            out[index * ROWS : (index + 1) * ROWS, :] = values[f]
        lower = upper
    for k in range(K - 2, -1, -1):
        for f in range(NT):
            index = f * K + k
            values[f] = tile(out, index) - ratios[k] * values[f]
            out[index * ROWS : (index + 1) * ROWS, :] = values[f]


def call(kernel, out_rows, scratch_rows, *operands):
    vmem = pl.BlockSpec(memory_space=pltpu.VMEM)
    shapes = [jax.ShapeDtypeStruct((rows, COLS), jnp.float32) for rows in out_rows]
    return pl.pallas_call(
        kernel,
        out_shape=shapes,
        in_specs=[vmem] * len(operands),
        out_specs=[vmem] * len(shapes),
        scratch_shapes=[pltpu.VMEM((rows, COLS), jnp.float32) for rows in scratch_rows],
        compiler_params=pltpu.CompilerParams(vmem_limit_bytes=24 * 1024 * 1024),
    )(*operands)


def pairs(lat_count, lon_count):
    def at(i, j):
        return i * lon_count + j % lon_count

    lon_near = [(at(i, j), at(i, j + 1)) for i in range(lat_count) for j in range(0, lon_count, 2)]
    lon_far = [(at(i, j), at(i, j + 1)) for i in range(lat_count) for j in range(1, lon_count, 2)]
    lat_near = [(at(i, j), at(i + 1, j)) for i in range(0, lat_count, 2) for j in range(lon_count)]
    lat_far = [(at(i, j), at(i + 1, j)) for i in range(1, lat_count - 1, 2) for j in range(lon_count)]
    top = lat_count - 1
    lat_far += [(at(top, j), at(top, lon_count - 1 - j)) for j in range(lon_count // 2)]
    return lon_near, lon_far, lat_near, lat_far


def swapped(x, groups):
    return lax.ppermute(x, AXES, [(a, b) for a, b in groups] + [(b, a) for a, b in groups])


def gathered(x, groups):
    both = lax.all_gather(x, AXES, axis_index_groups=[list(g) for g in groups])
    return both.reshape(-1, COLS)


def on_device(tracer, east_vel, north_vel, wet_mask, bottom_level, vertical_mix):
    lon_near, lon_far, lat_near, lat_far = pairs(lax.axis_size("lat"), lax.axis_size("lon"))
    flat = lambda x: x.reshape(-1, COLS)
    t, u, v, m, mix = map(flat, (tracer, east_vel, north_vel, wet_mask, vertical_mix))
    (own,) = call(edge_kernel, [PACK_ROWS], [], t, u, v, m)
    far = swapped(own, lon_far)
    near = gathered(own, lon_near)
    pay_far, pay_near, part, aux = call(
        first_kernel,
        [PAY_ROWS, PAY_ROWS, TILES * ROWS, AUX * ROWS],
        [],
        own, near, far, t, u, v, m,
    )
    far_rows = swapped(pay_far, lat_far)
    near_rows = gathered(pay_near, lat_near)
    (out,) = call(
        last_kernel,
        [TILES * ROWS],
        [TILES, TILES, TILES * ROWS],
        far_rows, near_rows, t, u, v, m, mix, bottom_level, part, aux,
    )
    return out.reshape(tracer.shape)


def solution(mesh):
    fields = P(None, "lat", "lon")
    tracers = P(None, None, "lat", "lon")
    return jax.shard_map(
        on_device,
        mesh=mesh,
        in_specs=(tracers, fields, fields, fields, P("lat", "lon"), fields),
        out_specs=tracers,
        check_vma=False,
    )
```

time: 147 us -> 41.4 us (0.28)
  the two profiles are of different devices: /device:TPU:1 before, /device:TPU:6 now
where the time goes in v1:
time: 41.4 us; the launch traced here: 40.8 us
  starting transfers between devices  17.4 us (42%)
  Pallas kernels  9.45 us (23%)
  blocking collectives  7.67 us (19%)
  local copies, waits for them, and re-layouts  3.52 us (9%)
  waiting for transfers between devices  2.69 us (6%)
    ppermute x2, starting transfers between devices, swapped(): lax.ppermute(x, AXES, [(a, b) for a, b in groups] + [(b, a) for a, b in g...  17.4 us
    pallas_call x3, Pallas kernels, call(): pl.pallas_call(kernel, out_shape=shapes, in_specs=[vmem] * len(operands),...  9.45 us
    all_gather x2, blocking collectives, gathered(): both = lax.all_gather(x, AXES, axis_index_groups=[list(g) for g in groups])  7.67 us
    unnamed x12, local copies, waits for them, and re-layouts  3.52 us
    ppermute x2, waiting for transfers between devices, swapped(): lax.ppermute(x, AXES, [(a, b) for a, b in groups] + [(b, a) for a, b in g...  2.69 us
  transfers between devices with their start and end apart: 2, of which 1 were waited for; matrix products, arithmetic and copies ran while one was open for 0% of the time, Pallas kernels for 0%

profile of v1, /device:TPU:6, one launch (start us, length us, event | category | flops | bytes accessed | tf_op | source)
XLA Modules:
  0.0 40.8 jit_solution(3061928753721599556)
XLA Ops:
  0.0 0.0 copy-start
  0.0 1.0 %copy-done = f32[6,16,8,128]{3,2,1,0:T(8,128)S(1)} copy-done((f32[6,16,8,128]{3,2,1,0:T(8,128)S(1)}, f32[6,16,8,128]{3,2,1,0:T(8,128)}, u32[]{:S(2)}) %copy-start) | copy-done | bytes 393240
  1.0 0.0 copy-start.1
  1.0 0.8 %copy-done.1 = f32[16,8,128]{2,1,0:T(8,128)S(1)} copy-done((f32[16,8,128]{2,1,0:T(8,128)S(1)}, f32[16,8,128]{2,1,0:T(8,128)}, u32[]{:S(2)}) %copy-start.1) | copy-done | bytes 65560
  1.8 0.0 copy-start.2
  1.8 0.8 %copy-done.2 = f32[16,8,128]{2,1,0:T(8,128)S(1)} copy-done((f32[16,8,128]{2,1,0:T(8,128)S(1)}, f32[16,8,128]{2,1,0:T(8,128)}, u32[]{:S(2)}) %copy-start.2) | copy-done | bytes 65560
  2.7 0.0 copy-start.3
  2.7 0.8 %copy-done.3 = s32[16,8,128]{2,1,0:T(8,128)S(1)} copy-done((s32[16,8,128]{2,1,0:T(8,128)S(1)}, s32[16,8,128]{2,1,0:T(8,128)}, u32[]{:S(2)}) %copy-start.3) | copy-done | bytes 65560
  3.5 0.2 shard_map.64.own
  3.7 8.4 %collective-permute-start = (f32[40,128]{1,0:T(8,128)S(1)}, f32[40,128]{1,0:T(8,128)S(1)}, u32[]{:S(2)}, u32[]{:S(2)}) collective-permute-start(f32[40,128]{1,0:T(8,128)S(1)} %shard_map.64.own), channel_id=1, source_target_pairs={{1,2},{3,4},{5,6},{7,8},{9,10},{11,12},{13,14},{15,16},{17,18},{19... | collective-permute-start | bytes 61448 | tf_op jit(solution)/shard_map/ppermute | solution.py:316
  12.2 1.8 %all-gather.near = f32[80,128]{1,0:T(8,128)S(1)} all-gather(f32[40,128]{1,0:T(8,128)S(1)} %shard_map.64.own), channel_id=2, replica_groups={{0,1},{2,3},{4,5},{6,7},{8,9},{10,11},{12,13},{14,15},{16,17},{18,19},{..., dimensions={0}, use_global_device_ids=true | all-gather | bytes 61440 | tf_op jit(solution)/shard_map/all_gather | solution.py:320
  14.0 0.0 collective-permute-done.far
  14.0 3.9 %shard_map.65 = (f32[232,128]{1,0:T(8,128)S(1)}, f32[232,128]{1,0:T(8,128)S(1)}, f32[768,128]{1,0:T(8,128)S(1)}, f32[112,128]{1,0:T(8,128)S(1)}) custom-call(f32[40,128]{1,0:T(8,128)S(1)} %shard_map.64.own, f32[80,128]{1,0:T(8,128)S(1)} %all-gather.near, f32[40,128]{1,0:T(8,128)S(1)} %collective-permute-done.far, f32[768,128]{1,0:T(8,128)S(1)} %bitcast.7, ...), custom_call_target="tpu_custom_call" | custom-call | tf_op jit(solution)/shard_map/pallas_call | solution.py:292
  17.9 9.0 %collective-permute-start.1 = (f32[232,128]{1,0:T(8,128)S(1)}, f32[232,128]{1,0:T(8,128)S(1)}, u32[]{:S(2)}, u32[]{:S(2)}) collective-permute-start(f32[232,128]{1,0:T(8,128)S(1)} %get-tuple-element.9), channel_id=1, source_target_pairs={{32,64},{33,65},{34,66},{35,67},{36,68},{37,69},{38,70},{39,71},{4... | collective-permute-start | bytes 356360 | tf_op jit(solution)/shard_map/ppermute | solution.py:316
  26.9 0.0 copy-start.4
  26.9 5.8 %all-gather.1.near = f32[464,128]{1,0:T(8,128)S(1)} all-gather(f32[232,128]{1,0:T(8,128)S(1)} %get-tuple-element.10), channel_id=3, replica_groups={{0,32},{1,33},{2,34},{3,35},{4,36},{5,37},{6,38},{7,39},{8,40},{9,41},{..., dimensions={0}, use_global_device_ids=true | all-gather | bytes 356352 | tf_op jit(solution)/shard_map/all_gather | solution.py:320
  32.7 0.0 copy-start.5
  32.7 2.7 %collective-permute-done.1.far = f32[232,128]{1,0:T(8,128)S(1)} collective-permute-done((f32[232,128]{1,0:T(8,128)S(1)}, f32[232,128]{1,0:T(8,128)S(1)}, u32[]{:S(2)}, u32[]{:S(2)}) %collective-permute-start.1) | collective-permute-done | bytes 118816 | tf_op jit(solution)/shard_map/ppermute | solution.py:316
  35.4 0.0 copy-done.4
  35.4 0.0 copy-done.5
  35.4 5.4 %shard_map.66 = f32[768,128]{1,0:T(8,128)} custom-call(f32[232,128]{1,0:T(8,128)S(1)} %collective-permute-done.1.far, f32[464,128]{1,0:T(8,128)S(1)} %all-gather.1.near, f32[768,128]{1,0:T(8,128)S(1)} %bitcast.8, f32[128,128]{1,0:T(8,128)S(1)} %bitcast.11, f32[128,128]{1,0:T(8,128)S(1)} %bitcast.14, s32[128,128]{1,0:T(8,128)S(1)} %bitcast.17, ...), custom_call_target="tpu_custom_call" | custom-call | tf_op jit(solution)/shard_map/pallas_call | solution.py:292
Async XLA Ops:
  0.0 1.0 %copy-start = (f32[6,16,8,128]{3,2,1,0:T(8,128)S(1)}, f32[6,16,8,128]{3,2,1,0:T(8,128)}, u32[]{:S(2)}) copy-start(f32[6,16,8,128]{3,2,1,0:T(8,128)} %param.6) | copy-start | bytes 1179652
  1.0 0.8 %copy-start.1 = (f32[16,8,128]{2,1,0:T(8,128)S(1)}, f32[16,8,128]{2,1,0:T(8,128)}, u32[]{:S(2)}) copy-start(f32[16,8,128]{2,1,0:T(8,128)} %param.7) | copy-start | bytes 196612
  1.8 0.8 %copy-start.2 = (f32[16,8,128]{2,1,0:T(8,128)S(1)}, f32[16,8,128]{2,1,0:T(8,128)}, u32[]{:S(2)}) copy-start(f32[16,8,128]{2,1,0:T(8,128)} %param.8) | copy-start | bytes 196612
  2.7 0.8 %copy-start.3 = (s32[16,8,128]{2,1,0:T(8,128)S(1)}, s32[16,8,128]{2,1,0:T(8,128)}, u32[]{:S(2)}) copy-start(s32[16,8,128]{2,1,0:T(8,128)} %param.9) | copy-start | bytes 196612
  3.7 10.3 %collective-permute-start = (f32[40,128]{1,0:T(8,128)S(1)}, f32[40,128]{1,0:T(8,128)S(1)}, u32[]{:S(2)}, u32[]{:S(2)}) collective-permute-start(f32[40,128]{1,0:T(8,128)S(1)} %shard_map.64.own), channel_id=1, source_target_pairs={{1,2},{3,4},{5,6},{7,8},{9,10},{11,12},{13,14},{15,16},{17,18},{19... | collective-permute-start | bytes 61448 | tf_op jit(solution)/shard_map/ppermute | solution.py:316
  17.9 17.6 %collective-permute-start.1 = (f32[232,128]{1,0:T(8,128)S(1)}, f32[232,128]{1,0:T(8,128)S(1)}, u32[]{:S(2)}, u32[]{:S(2)}) collective-permute-start(f32[232,128]{1,0:T(8,128)S(1)} %get-tuple-element.9), channel_id=1, source_target_pairs={{32,64},{33,65},{34,66},{35,67},{36,68},{37,69},{38,70},{39,71},{4... | collective-permute-start | bytes 356360 | tf_op jit(solution)/shard_map/ppermute | solution.py:316
  26.9 8.5 %copy-start.4 = (f32[16,8,128]{2,1,0:T(8,128)S(1)}, f32[16,8,128]{2,1,0:T(8,128)}, u32[]{:S(2)}) copy-start(f32[16,8,128]{2,1,0:T(8,128)} %param.11) | copy-start | bytes 196612
  32.7 2.7 %copy-start.5 = (s32[8,128]{1,0:T(8,128)S(1)}, s32[8,128]{1,0:T(8,128)}, u32[]{:S(2)}) copy-start(s32[8,128]{1,0:T(8,128)} %bottom.1) | copy-start | bytes 12292

commit v2 on v1

v2 whole, which is shorter than its diff:
```python
import jax
import jax.numpy as jnp
from jax import lax
from jax.experimental import pallas as pl
from jax.experimental.pallas import tpu as pltpu
from jax.sharding import PartitionSpec as P

ROWS = 8
COLS = 128
NT = 6
K = 16
TILES = NT * K
mixing = 0.08
AXES = ("lat", "lon")

FIELDS = NT + 3
PACKS = (FIELDS + 1) // 2
PACK_ROWS = PACKS * ROWS
TPACKS = NT // 2

ROW_T = 0
ROW_P = TILES
ROW_V = 2 * TILES
ROW_M = ROW_V + K
ROW_C = ROW_M + K
PAY_ROWS = ROW_C + ROWS

AUX_T = 0
AUX_V = TPACKS
AUX_M = AUX_V + 1
AUX_F = AUX_M + 1
AUX_Q = AUX_F + TPACKS
AUX_A = AUX_Q + TPACKS
AUX_B = AUX_A + 1
AUX = AUX_B + 1


def roll(x, shift, axis):
    shift %= x.shape[axis]
    return pltpu.roll(x, shift, axis) if shift else x


def lanes(rows=ROWS):
    return lax.broadcasted_iota(jnp.int32, (rows, COLS), 1)


def row_ids():
    return lax.broadcasted_iota(jnp.int32, (ROWS, COLS), 0)


def face(speed, opening):
    return opening * (jnp.maximum(speed, 0.0) + mixing), opening * (jnp.minimum(speed, 0.0) - mixing)


def tile(ref, index):
    return ref[index * ROWS : (index + 1) * ROWS, :]


def put(ref, index, value):
    ref[index * ROWS : (index + 1) * ROWS, :] = value


def edge(ref, start, size, row):
    return ref[pl.ds(start * ROWS + row, size, stride=ROWS), :]


def lane_base(field, k):
    return 64 * (field % 2) + 4 * (K - 1 - k)


def packed_edges(load, fields):
    group = lanes() // 4
    total = jnp.zeros((ROWS, COLS), jnp.float32)
    for field in fields:
        for k in range(K):
            base = lane_base(field, k)
            total = jnp.where(group == base // 4, roll(load(field, k), base - 126, 1), total)
    return total


def load_kernel(tracer, east, north, mask, pack, t, u, v, m, sems):
    copies = [
        pltpu.make_async_copy(src, dst, sems.at[i])
        for i, (src, dst) in enumerate(((east, u), (north, v), (mask, m), (tracer, t)))
    ]
    for copy in copies:
        copy.start()
    for copy in copies[:3]:
        copy.wait()

    def load(field, k):
        if field < NT:
            return tile(t, field * K + k)
        if field == NT:
            return tile(u, k)
        if field == NT + 1:
            return tile(m, k).astype(jnp.float32)
        return tile(v, k)

    for p in range(TPACKS, PACKS):
        put(pack, p, packed_edges(load, range(2 * p, min(2 * p + 2, FIELDS))))
    copies[3].wait()
    for p in range(TPACKS):
        put(pack, p, packed_edges(load, range(2 * p, 2 * p + 2)))


def level_faces(east, north, mask, k):
    u, v, m = tile(east, k), tile(north, k), tile(mask, k).astype(jnp.float32)
    open_x = jnp.where(lanes() < COLS - 1, m * roll(m, -1, 1), 0.0)
    open_y = jnp.where(row_ids() < ROWS - 1, m * roll(m, -1, 0), 0.0)
    ax, bx = face(0.5 * (u + roll(u, -1, 1)), open_x)
    ay, by = face(0.5 * (v + roll(v, -1, 0)), open_y)
    return ax, bx, ay, by


def inner_sum(t, faces):
    ax, bx, ay, by = faces
    fe = ax * t + bx * roll(t, -1, 1)
    gn = ay * t + by * roll(t, -1, 0)
    return (roll(fe, 1, 1) - fe) + (roll(gn, 1, 0) - gn)


def flipped(x):
    lane = lanes(x.shape[0])
    for step in (1, 2, 4, 8, 16, 32, 64):
        x = jnp.where((lane & step) != 0, roll(x, step, 1), roll(x, -step, 1))
    return x


def inner_kernel(tracer, east, north, mask, part, coeff, pay_far, pay_near):
    lat_odd = lax.rem(lax.axis_index("lat"), 2)
    is_top = lax.axis_index("lat") == lax.axis_size("lat") - 1
    for k in range(K):
        faces = level_faces(east, north, mask, k)
        for i in range(4):
            put(coeff, i * K + k, faces[i])
        for f in range(NT):
            index = f * K + k
            t = tile(tracer, index)
            put(part, index, t + inner_sum(t, faces))
    for pay, row in ((pay_far, (ROWS - 1) * lat_odd), (pay_near, (ROWS - 1) * (1 - lat_odd))):
        pay[ROW_T : ROW_T + TILES, :] = edge(tracer, 0, TILES, row)
        pay[ROW_P : ROW_P + TILES, :] = edge(part, 0, TILES, row)
        pay[ROW_V : ROW_V + K, :] = edge(north, 0, K, row)
        pay[ROW_M : ROW_M + K, :] = edge(mask, 0, K, row).astype(jnp.float32)
        pay[ROW_C : ROW_C + ROWS, :] = jnp.zeros((ROWS, COLS), jnp.float32)

    @pl.when(is_top)
    def _():
        x = flipped(pay_far[:ROW_C, :])
        pay_far[:ROW_V, :] = x[:ROW_V]
        pay_far[ROW_V:ROW_M, :] = -x[ROW_V:ROW_M]
        pay_far[ROW_M:ROW_C, :] = x[ROW_M:]


def both_halves(x, half):
    swapped = roll(x, 64, 1)
    low = lanes() < 64
    return jnp.where(low, x, swapped) if half == 0 else jnp.where(low, swapped, x)


def edge_sign():
    lane = lanes()
    return jnp.where(lane == 0, 1.0, jnp.where(lane == COLS - 1, -1.0, 0.0))


def outward_kernel(own, near, far, pay_far_in, pay_near_in, pay_far, pay_near, aux):
    lat_odd = lax.rem(lax.axis_index("lat"), 2)
    lon_odd = lax.rem(lax.axis_index("lon"), 2)
    is_top = lax.axis_index("lat") == lax.axis_size("lat") - 1
    place = lanes() & 3
    at_east = place == 1
    even = lon_odd == 0
    offset = pl.multiple_of((1 - lon_odd) * PACK_ROWS, ROWS)
    here, one, two = [], [], []
    for p in range(PACKS):
        a = near[pl.ds(pl.multiple_of(offset + p * ROWS, ROWS), ROWS), :]
        b = tile(far, p)
        e = jnp.where(even, a, b)
        w = jnp.where(even, b, a)
        here.append(tile(own, p))
        one.append(jnp.where(at_east, roll(e, -1, 1), roll(w, 1, 1)))
        two.append(jnp.where(at_east, roll(e, -2, 1), roll(w, 2, 1)))
    u0, m0 = both_halves(here[TPACKS], 0), both_halves(here[TPACKS], 1)
    u1, m1 = both_halves(one[TPACKS], 0), both_halves(one[TPACKS], 1)
    u2, m2 = both_halves(two[TPACKS], 0), both_halves(two[TPACKS], 1)
    v0, v1 = both_halves(here[TPACKS + 1], 0), both_halves(one[TPACKS + 1], 0)
    a1, b1 = face(0.5 * (u0 + u1), m0 * m1)
    a2, b2 = face(0.5 * (u1 + u2), m1 * m2)
    inner_y = row_ids() < ROWS - 1
    ay, by = face(0.5 * (v1 + roll(v1, -1, 0)), jnp.where(inner_y, m1 * roll(m1, -1, 0), 0.0))

    def corner(mine, halo):
        return jnp.where(
            place == 0, roll(mine, -1, 1), jnp.where(place == 3, roll(mine, 1, 1), halo)
        )

    for p in range(TPACKS):
        t0, t1, t2 = here[p], one[p], two[p]
        f1 = a1 * jnp.where(at_east, t0, t1) + b1 * jnp.where(at_east, t1, t0)
        f2 = a2 * jnp.where(at_east, t1, t2) + b2 * jnp.where(at_east, t2, t1)
        gn = ay * t1 + by * roll(t1, -1, 0)
        put(aux, AUX_F + p, f1)
        put(aux, AUX_Q + p, t1 + jnp.where(at_east, -f2, f2) + (roll(gn, 1, 0) - gn))
        put(aux, AUX_T + p, corner(t0, t1))
    put(aux, AUX_V, corner(v0, v1))
    put(aux, AUX_M, corner(m0, m1))
    put(aux, AUX_A, a1)
    put(aux, AUX_B, b1)

    lane = lanes()
    sign = edge_sign()
    sign_top = -sign
    rows = row_ids()
    for pay, source, row, top in (
        (pay_far, pay_far_in, (ROWS - 1) * lat_odd, is_top),
        (pay_near, pay_near_in, (ROWS - 1) * (1 - lat_odd), None),
    ):
        pay[:ROW_P, :] = source[:ROW_P, :]
        pay[ROW_V:ROW_C, :] = source[ROW_V:ROW_C, :]
        for p in range(TPACKS):
            line = jnp.broadcast_to(aux[pl.ds((AUX_F + p) * ROWS + row, 1), :], (ROWS, COLS))
            for f in (2 * p, 2 * p + 1):
                for k in (0, ROWS):
                    shift = COLS - 1 - (lane_base(f, k) + 1)
                    x = sign * pltpu.roll(line, shift, 1, stride=4, stride_axis=0)
                    if top is not None:
                        turned = jnp.where(lane == 0, roll(x, 1, 1), roll(x, -1, 1))
                        x = jnp.where(top, jnp.where(sign != 0.0, turned, 0.0), x)
                    start = ROW_P + f * K + k
                    pay[start : start + ROWS, :] = source[start : start + ROWS, :] + x
        c = aux[pl.ds(AUX_T * ROWS + row, ROWS, stride=ROWS), :]
        if top is not None:
            turned = jnp.where(
                place == 0,
                roll(c, -3, 1),
                jnp.where(place == 1, roll(c, -1, 1), jnp.where(place == 2, roll(c, 1, 1), roll(c, 3, 1))),
            )
            c = jnp.where(top, jnp.where(rows == AUX_V, -turned, turned), c)
        pay[ROW_C : ROW_C + ROWS, :] = c


def column_kernel(tracer, part, aux, own, mix, bottom, full, both, rows_0, rows_7, packs, solve, spread):
    sign = edge_sign()
    for f in range(NT):
        packed = tile(aux, AUX_F + f // 2)
        for k in range(K):
            put(spread, f * K + k, sign * roll(packed, COLS - 1 - (lane_base(f, k) + 1), 1))
    for index in range(TILES):
        x = tile(part, index) + tile(spread, index)
        put(full, index, x)
        put(both, index, tile(tracer, index) + x)
    rows_0[...] = edge(full, 0, TILES, 0)
    rows_7[...] = edge(full, 0, TILES, ROWS - 1)
    for p in range(TPACKS):
        put(packs, p, packed_edges(lambda f, k: tile(full, f * K + k), (2 * p, 2 * p + 1)))
    depth = bottom[...]
    lower = ratio = None
    for k in range(K):
        denom = 1.0
        upper = None
        if k + 1 < K:
            upper = jnp.where(k + 1 < depth, tile(mix, k), 0.0)
            denom = denom + upper
        if k:
            denom = denom + lower + lower * ratio
        inverse = 1.0 / denom
        put(solve, k, 0.5 * inverse)
        if k:
            put(solve, K + k, lower * inverse)
        else:
            put(solve, K + k, jnp.zeros((ROWS, COLS), jnp.float32))
        ratio = -upper * inverse if upper is not None else jnp.zeros((ROWS, COLS), jnp.float32)
        put(solve, 2 * K + k, ratio)
        lower = upper


def last_kernel(
    far, near, tracer, north, mask, coeff, full, both_sums, rows_0, rows_7, packs, solve, own, aux,
    out, edge_1, edge_2, spread,
):
    lat_odd = lax.rem(lax.axis_index("lat"), 2)
    odd = lat_odd == 1
    offset = pl.multiple_of((1 - lat_odd) * PAY_ROWS, ROWS)
    place = lanes() & 3
    at_east = place == 1
    rows = row_ids()
    at_south, at_north = rows == 0, rows == ROWS - 1

    def both(start, size):
        a = far[start : start + size, :]
        b = near[pl.ds(pl.multiple_of(offset + start, ROWS), size), :]
        return jnp.where(odd, a, b), jnp.where(odd, b, a)

    c_n, c_s = both(ROW_C, ROWS)

    def inner_columns(c):
        return jnp.where(at_east, roll(c, 1, 1), roll(c, -1, 1))

    d_n, d_s = inner_columns(c_n), inner_columns(c_s)
    v0, m0 = both_halves(tile(own, TPACKS + 1), 0), both_halves(tile(own, TPACKS), 1)
    v1, m1 = tile(aux, AUX_V), tile(aux, AUX_M)

    def corner_faces(v, m, north_rows, south_rows):
        v_n, v_s = north_rows[AUX_V : AUX_V + 1], south_rows[AUX_V : AUX_V + 1]
        m_n, m_s = north_rows[AUX_M : AUX_M + 1], south_rows[AUX_M : AUX_M + 1]
        an, bn = face(0.5 * (v + v_n), jnp.where(at_north, m * m_n, 0.0))
        as_, bs = face(0.5 * (v_s + v), jnp.where(at_south, m_s * m, 0.0))
        return lambda t, t_n, t_s: (as_ * t_s + bs * t) - (an * t + bn * t_n)

    halo_sum = corner_faces(v1, m1, c_n, c_s)
    own_sum = corner_faces(v0, m0, d_n, d_s)
    a1, b1 = tile(aux, AUX_A), tile(aux, AUX_B)
    sign = edge_sign()
    for p in range(TPACKS):
        f1 = tile(aux, AUX_F + p)
        s1 = tile(aux, AUX_Q + p) + jnp.where(at_east, f1, -f1)
        s1 = s1 + halo_sum(tile(aux, AUX_T + p), c_n[p : p + 1], c_s[p : p + 1])
        s0 = tile(packs, p) + own_sum(tile(own, p), d_n[p : p + 1], d_s[p : p + 1])
        flux = a1 * jnp.where(at_east, s0, s1) + b1 * jnp.where(at_east, s1, s0)
        for f in (2 * p, 2 * p + 1):
            for k in range(K):
                put(spread, f * K + k, sign * roll(flux, COLS - 1 - (lane_base(f, k) + 1), 1))

    v_n, v_s = both(ROW_V, K)
    m_n, m_s = both(ROW_M, K)
    an, bn = face(
        0.5 * (edge(north, 0, K, ROWS - 1) + v_n), edge(mask, 0, K, ROWS - 1).astype(jnp.float32) * m_n
    )
    as_, bs = face(0.5 * (v_s + edge(north, 0, K, 0)), m_s * edge(mask, 0, K, 0).astype(jnp.float32))
    for f in range(NT):
        t_n, t_s = both(ROW_T + f * K, K)
        p_n, p_s = both(ROW_P + f * K, K)
        g_n = an * edge(tracer, f * K, K, ROWS - 1) + bn * t_n
        g_s = as_ * t_s + bs * edge(tracer, f * K, K, 0)
        h_n = an * (rows_7[f * K : (f + 1) * K, :] - g_n) + bn * (p_n + g_n)
        h_s = as_ * (p_s - g_s) + bs * (rows_0[f * K : (f + 1) * K, :] + g_s)
        edge_1[f * K : (f + 1) * K, :] = g_s
        edge_1[TILES + f * K : TILES + (f + 1) * K, :] = -g_n
        edge_2[f * K : (f + 1) * K, :] = g_s + h_s
        edge_2[TILES + f * K : TILES + (f + 1) * K, :] = -(g_n + h_n)

    def outer(ref, index):
        low = ref[index : index + 1, :]
        high = ref[TILES + index : TILES + index + 1, :]
        return jnp.where(at_south, low, jnp.where(at_north, high, 0.0))

    for f in range(NT):
        value = None
        for k in range(K):
            index = f * K + k
            faces = [tile(coeff, i * K + k) for i in range(4)]
            s = tile(full, index) + outer(edge_1, index)
            rhs = (tile(both_sums, index) + inner_sum(s, faces)) + (tile(spread, index) + outer(edge_2, index))
            value_new = rhs * tile(solve, k)
            if k:
                value_new = value_new + tile(solve, K + k) * value
            value = value_new
            put(out, index, value)
        for k in range(K - 2, -1, -1):
            index = f * K + k
            value = tile(out, index) - tile(solve, 2 * K + k) * value
            put(out, index, value)


def call(kernel, outs, scratch_rows, *operands, hbm=False, scratch=(), cost=None):
    vmem = pl.BlockSpec(memory_space=pltpu.VMEM)
    place = pl.BlockSpec(memory_space=pltpu.HBM) if hbm else vmem
    shapes = [
        x if isinstance(x, jax.ShapeDtypeStruct) else jax.ShapeDtypeStruct((x, COLS), jnp.float32)
        for x in outs
    ]
    return pl.pallas_call(
        kernel,
        out_shape=shapes,
        in_specs=[place] * len(operands),
        out_specs=[vmem] * len(shapes),
        scratch_shapes=[pltpu.VMEM((rows, COLS), jnp.float32) for rows in scratch_rows] + list(scratch),
        compiler_params=pltpu.CompilerParams(vmem_limit_bytes=24 * 1024 * 1024),
        cost_estimate=cost,
    )(*operands)


def pairs(lat_count, lon_count):
    def at(i, j):
        return i * lon_count + j % lon_count

    lon_near = [(at(i, j), at(i, j + 1)) for i in range(lat_count) for j in range(0, lon_count, 2)]
    lon_far = [(at(i, j), at(i, j + 1)) for i in range(lat_count) for j in range(1, lon_count, 2)]
    lat_near = [(at(i, j), at(i + 1, j)) for i in range(0, lat_count, 2) for j in range(lon_count)]
    lat_far = [(at(i, j), at(i + 1, j)) for i in range(1, lat_count - 1, 2) for j in range(lon_count)]
    top = lat_count - 1
    lat_far += [(at(top, j), at(top, lon_count - 1 - j)) for j in range(lon_count // 2)]
    return lon_near, lon_far, lat_near, lat_far


def swapped(x, groups):
    return lax.ppermute(x, AXES, [(a, b) for a, b in groups] + [(b, a) for a, b in groups])


def gathered(x, groups):
    both = lax.all_gather(x, AXES, axis_index_groups=[list(g) for g in groups])
    return both.reshape(-1, COLS)


def on_device(tracer, east_vel, north_vel, wet_mask, bottom_level, vertical_mix):
    lon_near, lon_far, lat_near, lat_far = pairs(lax.axis_size("lat"), lax.axis_size("lon"))
    flat = lambda x: x.reshape(-1, COLS)
    fields = [
        pltpu.with_memory_space_constraint(flat(x), pltpu.HBM)
        for x in (tracer, east_vel, north_vel, wet_mask)
    ]
    own, t, u, v, m = call(
        load_kernel,
        [PACK_ROWS] + [jax.ShapeDtypeStruct(x.shape, x.dtype) for x in fields],
        [],
        *fields,
        hbm=True,
        scratch=[pltpu.SemaphoreType.DMA((4,))],
    )
    far = swapped(own, lon_far)
    near = gathered(own, lon_near)
    part, coeff, pay_far, pay_near = call(
        inner_kernel, [TILES * ROWS, 4 * K * ROWS, PAY_ROWS, PAY_ROWS], [], t, u, v, m
    )
    pay_far, pay_near, aux = call(
        outward_kernel, [PAY_ROWS, PAY_ROWS, AUX * ROWS], [], own, near, far, pay_far, pay_near
    )
    far_rows = swapped(pay_far, lat_far)
    near_rows = gathered(pay_near, lat_near)
    full, both, rows_0, rows_7, packs, solve = call(
        column_kernel,
        [TILES * ROWS, TILES * ROWS, TILES, TILES, TPACKS * ROWS, 3 * K * ROWS],
        [TILES * ROWS],
        t, part, aux, own, flat(vertical_mix), bottom_level,
    )
    (out,) = call(
        last_kernel,
        [TILES * ROWS],
        [2 * TILES, 2 * TILES, TILES * ROWS],
        far_rows, near_rows, t, v, m, coeff, full, both, rows_0, rows_7, packs, solve, own, aux,
    )
    return out.reshape(tracer.shape)


def solution(mesh):
    fields = P(None, "lat", "lon")
    tracers = P(None, None, "lat", "lon")
    return jax.shard_map(
        on_device,
        mesh=mesh,
        in_specs=(tracers, fields, fields, fields, P("lat", "lon"), fields),
        out_specs=tracers,
        check_vma=False,
    )
```

time: 41.4 us -> 32.1 us (0.78)
  Pallas kernels: 9.45 us -> 4.16 us
  local copies, waits for them, and re-layouts: 3.52 us -> 0.01 us
    pallas_call x3 -> x5, Pallas kernels: 9.45 us -> 4.16 us  [call(): pl.pallas_call(kernel, out_shape=shapes, in_specs=[place] * len(operands)...]
    unnamed x12 -> x4, local copies, waits for them, and re-layouts: 3.52 us -> 0.01 us
  transfers between devices with their start and end apart: 2 -> 2, of which waited for: 1 -> 1; matrix products, arithmetic and copies ran while one was open for 0% -> 0% of each run, Pallas kernels for 0% -> 4%
where the time goes in v2:
time: 32.1 us; the launch traced here: 31.7 us
  starting transfers between devices  17.4 us (54%)
  blocking collectives  7.53 us (23%)
  Pallas kernels  4.16 us (13%)
  waiting for transfers between devices  2.51 us (8%)
    ppermute x2, starting transfers between devices, swapped(): lax.ppermute(x, AXES, [(a, b) for a, b in groups] + [(b, a) for a, b in g...  17.4 us
    all_gather x2, blocking collectives, gathered(): both = lax.all_gather(x, AXES, axis_index_groups=[list(g) for g in groups])  7.53 us
    pallas_call x5, Pallas kernels, call(): pl.pallas_call(kernel, out_shape=shapes, in_specs=[place] * len(operands)...  4.16 us
    ppermute x2, waiting for transfers between devices, swapped(): lax.ppermute(x, AXES, [(a, b) for a, b in groups] + [(b, a) for a, b in g...  2.51 us
  transfers between devices with their start and end apart: 2, of which 1 were waited for; matrix products, arithmetic and copies ran while one was open for 0% of the time, Pallas kernels for 4%

profile of v2, /device:TPU:6, one launch (start us, length us, event | category | flops | bytes accessed | tf_op | source)
XLA Modules:
  0.0 31.7 jit_solution(8745098645220671705)
XLA Ops:
  0.0 1.3 %shard_map.64 = (f32[40,128]{1,0:T(8,128)S(1)}, f32[768,128]{1,0:T(8,128)S(1)}, f32[128,128]{1,0:T(8,128)S(1)}, f32[128,128]{1,0:T(8,128)S(1)}, s32[128,128]{1,0:T(8,128)S(1)}) custom-call(f32[768,128]{1,0:T(8,128)} %bitcast.7, f32[128,128]{1,0:T(8,128)} %bitcast.8, f32[128,128]{1,0:T(8,128)} %bitcast.9, s32[128,128]{1,0:T(8,128)} %bitcast.10), custom_call_target="tpu_custom_call" | custom-call | tf_op jit(solution)/shard_map/pallas_call | solution.py:373
  1.3 8.4 %collective-permute-start = (f32[40,128]{1,0:T(8,128)S(1)}, f32[40,128]{1,0:T(8,128)S(1)}, u32[]{:S(2)}, u32[]{:S(2)}) collective-permute-start(f32[40,128]{1,0:T(8,128)S(1)} %get-tuple-element.23.own), channel_id=1, source_target_pairs={{1,2},{3,4},{5,6},{7,8},{9,10},{11,12},{13,14},{15,16},{17,18},{19... | collective-permute-start | bytes 61448 | tf_op jit(solution)/shard_map/ppermute | solution.py:398
  9.7 0.8 %shard_map.65 = (f32[768,128]{1,0:T(8,128)S(1)}, f32[512,128]{1,0:T(8,128)S(1)}, f32[232,128]{1,0:T(8,128)S(1)}, f32[232,128]{1,0:T(8,128)S(1)}) custom-call(f32[768,128]{1,0:T(8,128)S(1)} %get-tuple-element.24.tracer, f32[128,128]{1,0:T(8,128)S(1)} %get-tuple-element.25.east, f32[128,128]{1,0:T(8,128)S(1)} %get-tuple-element.26.north, ...), custom_call_target="tpu_custom_call" | custom-call | tf_op jit(solution)/shard_map/pallas_call | solution.py:373
  10.6 1.8 %all-gather.near = f32[80,128]{1,0:T(8,128)S(1)} all-gather(f32[40,128]{1,0:T(8,128)S(1)} %get-tuple-element.23.own), channel_id=2, replica_groups={{0,1},{2,3},{4,5},{6,7},{8,9},{10,11},{12,13},{14,15},{16,17},{18,19},{..., dimensions={0}, use_global_device_ids=true | all-gather | bytes 61440 | tf_op jit(solution)/shard_map/all_gather | solution.py:402
  12.4 0.0 collective-permute-done.far
  12.4 0.0 copy-start
  12.4 0.3 %shard_map.66 = (f32[232,128]{1,0:T(8,128)S(1)}, f32[232,128]{1,0:T(8,128)S(1)}, f32[104,128]{1,0:T(8,128)S(1)}) custom-call(f32[40,128]{1,0:T(8,128)S(1)} %get-tuple-element.23.own, f32[80,128]{1,0:T(8,128)S(1)} %all-gather.near, f32[40,128]{1,0:T(8,128)S(1)} %collective-permute-done.far, f32[232,128]{1,0:T(8,128)S(1)} %get-tuple-element.28.pay_far_in, ...), custom_call_target="tpu_custom_call" | custom-call | tf_op jit(solution)/shard_map/pallas_call | solution.py:373
  12.7 0.0 copy-start.1
  12.7 9.0 %collective-permute-start.1 = (f32[232,128]{1,0:T(8,128)S(1)}, f32[232,128]{1,0:T(8,128)S(1)}, u32[]{:S(2)}, u32[]{:S(2)}) collective-permute-start(f32[232,128]{1,0:T(8,128)S(1)} %get-tuple-element.30), channel_id=1, source_target_pairs={{32,64},{33,65},{34,66},{35,67},{36,68},{37,69},{38,70},{39,71},{4... | collective-permute-start | bytes 356360 | tf_op jit(solution)/shard_map/ppermute | solution.py:398
  21.8 0.0 copy-done
  21.8 0.0 copy-done.1
  21.8 0.3 shard_map.67
  22.1 5.7 %all-gather.1.near = f32[464,128]{1,0:T(8,128)S(1)} all-gather(f32[232,128]{1,0:T(8,128)S(1)} %get-tuple-element.31), channel_id=3, replica_groups={{0,32},{1,33},{2,34},{3,35},{4,36},{5,37},{6,38},{7,39},{8,40},{9,41},{..., dimensions={0}, use_global_device_ids=true | all-gather | bytes 356352 | tf_op jit(solution)/shard_map/all_gather | solution.py:402
  27.8 2.5 %collective-permute-done.1.far = f32[232,128]{1,0:T(8,128)S(1)} collective-permute-done((f32[232,128]{1,0:T(8,128)S(1)}, f32[232,128]{1,0:T(8,128)S(1)}, u32[]{:S(2)}, u32[]{:S(2)}) %collective-permute-start.1) | collective-permute-done | bytes 118816 | tf_op jit(solution)/shard_map/ppermute | solution.py:398
  30.3 1.4 %shard_map.68 = f32[768,128]{1,0:T(8,128)} custom-call(f32[232,128]{1,0:T(8,128)S(1)} %collective-permute-done.1.far, f32[464,128]{1,0:T(8,128)S(1)} %all-gather.1.near, f32[768,128]{1,0:T(8,128)S(1)} %get-tuple-element.24.tracer, f32[128,128]{1,0:T(8,128)S(1)} %get-tuple-element.26.north, s32[128,128]{1,0:T(8,128)S(1)} %get-tuple-element.27.mask, ...), custom_call_target="tpu_custom_call" | custom-call | tf_op jit(solution)/shard_map/pallas_call | solution.py:373
Async XLA Ops:
  1.3 11.1 %collective-permute-start = (f32[40,128]{1,0:T(8,128)S(1)}, f32[40,128]{1,0:T(8,128)S(1)}, u32[]{:S(2)}, u32[]{:S(2)}) collective-permute-start(f32[40,128]{1,0:T(8,128)S(1)} %get-tuple-element.23.own), channel_id=1, source_target_pairs={{1,2},{3,4},{5,6},{7,8},{9,10},{11,12},{13,14},{15,16},{17,18},{19... | collective-permute-start | bytes 61448 | tf_op jit(solution)/shard_map/ppermute | solution.py:398
  12.4 9.4 %copy-start = (f32[16,8,128]{2,1,0:T(8,128)S(1)}, f32[16,8,128]{2,1,0:T(8,128)}, u32[]{:S(2)}) copy-start(f32[16,8,128]{2,1,0:T(8,128)} %param.11) | copy-start | bytes 196612
  12.7 9.0 %copy-start.1 = (s32[8,128]{1,0:T(8,128)S(1)}, s32[8,128]{1,0:T(8,128)}, u32[]{:S(2)}) copy-start(s32[8,128]{1,0:T(8,128)} %bottom.1) | copy-start | bytes 12292
  12.7 17.6 %collective-permute-start.1 = (f32[232,128]{1,0:T(8,128)S(1)}, f32[232,128]{1,0:T(8,128)S(1)}, u32[]{:S(2)}, u32[]{:S(2)}) collective-permute-start(f32[232,128]{1,0:T(8,128)S(1)} %get-tuple-element.30), channel_id=1, source_target_pairs={{32,64},{33,65},{34,66},{35,67},{36,68},{37,69},{38,70},{39,71},{4... | collective-permute-start | bytes 356360 | tf_op jit(solution)/shard_map/ppermute | solution.py:398

commit v3 on v2

--- a/solution.py
+++ b/solution.py
@@ -78,15 +78,29 @@
     return total
 
 
+def row_part(tracer, east, north, mask, row, inward):
+    u, m = edge(east, 0, K, row), edge(mask, 0, K, row).astype(jnp.float32)
+    v, v_in = edge(north, 0, K, row), edge(north, 0, K, inward)
+    m_in = edge(mask, 0, K, inward).astype(jnp.float32)
+    ax, bx = face(0.5 * (u + roll(u, -1, 1)), jnp.where(lanes(K) < COLS - 1, m * roll(m, -1, 1), 0.0))
+    ay, by = face(0.5 * (v + v_in), m * m_in)
+    ts, sums = [], []
+    for f in range(NT):
+        t, t_in = edge(tracer, f * K, K, row), edge(tracer, f * K, K, inward)
+        fe = ax * t + bx * roll(t, -1, 1)
+        g = -(ay * t + by * t_in) if inward > row else ay * t_in + by * t
+        ts.append(t)
+        sums.append(t + ((roll(fe, 1, 1) - fe) + g))
+    return ts + sums + [v, m]
+
+
 def load_kernel(tracer, east, north, mask, pack, t, u, v, m, sems):
     copies = [
         pltpu.make_async_copy(src, dst, sems.at[i])
-        for i, (src, dst) in enumerate(((east, u), (north, v), (mask, m), (tracer, t)))
+        for i, (src, dst) in enumerate(((tracer, t), (east, u), (north, v), (mask, m)))
     ]
     for copy in copies:
         copy.start()
-    for copy in copies[:3]:
-        copy.wait()
 
     def load(field, k):
         if field < NT:
@@ -97,11 +111,31 @@
             return tile(m, k).astype(jnp.float32)
         return tile(v, k)
 
+    for copy in copies[1:]:
+        copy.wait()
     for p in range(TPACKS, PACKS):
         put(pack, p, packed_edges(load, range(2 * p, min(2 * p + 2, FIELDS))))
-    copies[3].wait()
+    copies[0].wait()
     for p in range(TPACKS):
         put(pack, p, packed_edges(load, range(2 * p, 2 * p + 2)))
+
+
+def rows_kernel(t, u, v, m, pay_far, pay_near):
+    odd = lax.rem(lax.axis_index("lat"), 2) == 1
+    upper = row_part(t, u, v, m, ROWS - 1, ROWS - 2)
+    lower = row_part(t, u, v, m, 0, 1)
+    for i, (x, y) in enumerate(zip(upper, lower)):
+        pay_far[i * K : (i + 1) * K, :] = jnp.where(odd, x, y)
+        pay_near[i * K : (i + 1) * K, :] = jnp.where(odd, y, x)
+    for pay in (pay_far, pay_near):
+        pay[ROW_C:, :] = jnp.zeros((ROWS, COLS), jnp.float32)
+
+    @pl.when(lax.axis_index("lat") == lax.axis_size("lat") - 1)
+    def _():
+        x = flipped(pay_far[:ROW_C, :])
+        pay_far[:ROW_V, :] = x[:ROW_V]
+        pay_far[ROW_V:ROW_M, :] = -x[ROW_V:ROW_M]
+        pay_far[ROW_M:ROW_C, :] = x[ROW_M:]
 
 
 def level_faces(east, north, mask, k):
@@ -127,9 +161,8 @@
     return x
 
 
-def inner_kernel(tracer, east, north, mask, part, coeff, pay_far, pay_near):
-    lat_odd = lax.rem(lax.axis_index("lat"), 2)
-    is_top = lax.axis_index("lat") == lax.axis_size("lat") - 1
+def inner_kernel(tracer, east, north, mask, ahead, part, coeff):
+    del ahead
     for k in range(K):
         faces = level_faces(east, north, mask, k)
         for i in range(4):
@@ -138,19 +171,6 @@
             index = f * K + k
             t = tile(tracer, index)
             put(part, index, t + inner_sum(t, faces))
-    for pay, row in ((pay_far, (ROWS - 1) * lat_odd), (pay_near, (ROWS - 1) * (1 - lat_odd))):
-        pay[ROW_T : ROW_T + TILES, :] = edge(tracer, 0, TILES, row)
-        pay[ROW_P : ROW_P + TILES, :] = edge(part, 0, TILES, row)
-        pay[ROW_V : ROW_V + K, :] = edge(north, 0, K, row)
-        pay[ROW_M : ROW_M + K, :] = edge(mask, 0, K, row).astype(jnp.float32)
-        pay[ROW_C : ROW_C + ROWS, :] = jnp.zeros((ROWS, COLS), jnp.float32)
-
-    @pl.when(is_top)
-    def _():
-        x = flipped(pay_far[:ROW_C, :])
-        pay_far[:ROW_V, :] = x[:ROW_V]
-        pay_far[ROW_V:ROW_M, :] = -x[ROW_V:ROW_M]
-        pay_far[ROW_M:ROW_C, :] = x[ROW_M:]
 
 
 def both_halves(x, half):
@@ -164,7 +184,7 @@
     return jnp.where(lane == 0, 1.0, jnp.where(lane == COLS - 1, -1.0, 0.0))
 
 
-def outward_kernel(own, near, far, pay_far_in, pay_near_in, pay_far, pay_near, aux):
+def outward_kernel(own, near, far, far_in, near_in, pay_far, pay_near, aux):
     lat_odd = lax.rem(lax.axis_index("lat"), 2)
     lon_odd = lax.rem(lax.axis_index("lon"), 2)
     is_top = lax.axis_index("lat") == lax.axis_size("lat") - 1
@@ -208,36 +228,17 @@
     put(aux, AUX_A, a1)
     put(aux, AUX_B, b1)
 
-    lane = lanes()
-    sign = edge_sign()
-    sign_top = -sign
+    del far_in, near_in
+    pay_near[ROW_C:, :] = aux[pl.ds(AUX_T * ROWS + (ROWS - 1) * (1 - lat_odd), ROWS, stride=ROWS), :]
+    c = aux[pl.ds(AUX_T * ROWS + (ROWS - 1) * lat_odd, ROWS, stride=ROWS), :]
+    turned = jnp.where(
+        place == 0,
+        roll(c, -3, 1),
+        jnp.where(place == 1, roll(c, -1, 1), jnp.where(place == 2, roll(c, 1, 1), roll(c, 3, 1))),
+    )
     rows = row_ids()
-    for pay, source, row, top in (
-        (pay_far, pay_far_in, (ROWS - 1) * lat_odd, is_top),
-        (pay_near, pay_near_in, (ROWS - 1) * (1 - lat_odd), None),
-    ):
-        pay[:ROW_P, :] = source[:ROW_P, :]
-        pay[ROW_V:ROW_C, :] = source[ROW_V:ROW_C, :]
-        for p in range(TPACKS):
-            line = jnp.broadcast_to(aux[pl.ds((AUX_F + p) * ROWS + row, 1), :], (ROWS, COLS))
-            for f in (2 * p, 2 * p + 1):
-                for k in (0, ROWS):
-                    shift = COLS - 1 - (lane_base(f, k) + 1)
-                    x = sign * pltpu.roll(line, shift, 1, stride=4, stride_axis=0)
-                    if top is not None:
-                        turned = jnp.where(lane == 0, roll(x, 1, 1), roll(x, -1, 1))
-                        x = jnp.where(top, jnp.where(sign != 0.0, turned, 0.0), x)
-                    start = ROW_P + f * K + k
-                    pay[start : start + ROWS, :] = source[start : start + ROWS, :] + x
-        c = aux[pl.ds(AUX_T * ROWS + row, ROWS, stride=ROWS), :]
-        if top is not None:
-            turned = jnp.where(
-                place == 0,
-                roll(c, -3, 1),
-                jnp.where(place == 1, roll(c, -1, 1), jnp.where(place == 2, roll(c, 1, 1), roll(c, 3, 1))),
-            )
-            c = jnp.where(top, jnp.where(rows == AUX_V, -turned, turned), c)
-        pay[ROW_C : ROW_C + ROWS, :] = c
+    turned = jnp.where((rows == AUX_V) | (rows >= AUX_F), -turned, turned)
+    pay_far[ROW_C:, :] = jnp.where(is_top, turned, c)
 
 
 def column_kernel(tracer, part, aux, own, mix, bottom, full, both, rows_0, rows_7, packs, solve, spread):
@@ -328,9 +329,21 @@
         0.5 * (edge(north, 0, K, ROWS - 1) + v_n), edge(mask, 0, K, ROWS - 1).astype(jnp.float32) * m_n
     )
     as_, bs = face(0.5 * (v_s + edge(north, 0, K, 0)), m_s * edge(mask, 0, K, 0).astype(jnp.float32))
+
+    def edge_flux(c, f):
+        line = jnp.broadcast_to(c[AUX_F + f // 2 : AUX_F + f // 2 + 1], (ROWS, COLS))
+        return jnp.concatenate(
+            [
+                sign * pltpu.roll(line, COLS - 1 - (lane_base(f, k) + 1), 1, stride=4, stride_axis=0)
+                for k in (0, ROWS)
+            ],
+            axis=0,
+        )
+
     for f in range(NT):
         t_n, t_s = both(ROW_T + f * K, K)
         p_n, p_s = both(ROW_P + f * K, K)
+        p_n, p_s = p_n + edge_flux(c_n, f), p_s + edge_flux(c_s, f)
         g_n = an * edge(tracer, f * K, K, ROWS - 1) + bn * t_n
         g_s = as_ * t_s + bs * edge(tracer, f * K, K, 0)
         h_n = an * (rows_7[f * K : (f + 1) * K, :] - g_n) + bn * (p_n + g_n)
@@ -363,7 +376,7 @@
             put(out, index, value)
 
 
-def call(kernel, outs, scratch_rows, *operands, hbm=False, scratch=(), cost=None):
+def call(kernel, outs, scratch_rows, *operands, hbm=False, scratch=(), alias=None):
     vmem = pl.BlockSpec(memory_space=pltpu.VMEM)
     place = pl.BlockSpec(memory_space=pltpu.HBM) if hbm else vmem
     shapes = [
@@ -377,7 +390,7 @@
         out_specs=[vmem] * len(shapes),
         scratch_shapes=[pltpu.VMEM((rows, COLS), jnp.float32) for rows in scratch_rows] + list(scratch),
         compiler_params=pltpu.CompilerParams(vmem_limit_bytes=24 * 1024 * 1024),
-        cost_estimate=cost,
+        input_output_aliases=alias or {},
     )(*operands)
 
 
@@ -419,14 +432,17 @@
         scratch=[pltpu.SemaphoreType.DMA((4,))],
     )
     far = swapped(own, lon_far)
+    pay_far, pay_near = call(rows_kernel, [PAY_ROWS, PAY_ROWS], [], t, u, v, m)
     near = gathered(own, lon_near)
-    part, coeff, pay_far, pay_near = call(
-        inner_kernel, [TILES * ROWS, 4 * K * ROWS, PAY_ROWS, PAY_ROWS], [], t, u, v, m
-    )
     pay_far, pay_near, aux = call(
-        outward_kernel, [PAY_ROWS, PAY_ROWS, AUX * ROWS], [], own, near, far, pay_far, pay_near
+        outward_kernel,
+        [PAY_ROWS, PAY_ROWS, AUX * ROWS],
+        [],
+        own, near, far, pay_far, pay_near,
+        alias={3: 0, 4: 1},
     )
     far_rows = swapped(pay_far, lat_far)
+    part, coeff = call(inner_kernel, [TILES * ROWS, 4 * K * ROWS], [], t, u, v, m, aux)
     near_rows = gathered(pay_near, lat_near)
     full, both, rows_0, rows_7, packs, solve = call(
         column_kernel,

time: 32.1 us -> 31.5 us (0.981)
  waiting for transfers between devices: 2.51 us -> 1.69 us
    ppermute x2, waiting for transfers between devices: 2.51 us -> 1.69 us  [swapped(): lax.ppermute(x, AXES, [(a, b) for a, b in groups] + [(b, a) for a, b in g...]
    pallas_call x5 -> x6, Pallas kernels: 4.16 us -> 4.29 us  [call(): pl.pallas_call(kernel, out_shape=shapes, in_specs=[place] * len(operands)...]
where the time goes in v3:
time: 31.5 us; the launch traced here: 31.1 us
  starting transfers between devices  17.4 us (55%)
  blocking collectives  7.54 us (24%)
  Pallas kernels  4.29 us (14%)
  waiting for transfers between devices  1.69 us (5%)
    ppermute x2, starting transfers between devices, swapped(): lax.ppermute(x, AXES, [(a, b) for a, b in groups] + [(b, a) for a, b in g...  17.4 us
    all_gather x2, blocking collectives, gathered(): both = lax.all_gather(x, AXES, axis_index_groups=[list(g) for g in groups])  7.54 us
    pallas_call x6, Pallas kernels, call(): pl.pallas_call(kernel, out_shape=shapes, in_specs=[place] * len(operands)...  4.29 us
    ppermute x2, waiting for transfers between devices, swapped(): lax.ppermute(x, AXES, [(a, b) for a, b in groups] + [(b, a) for a, b in g...  1.69 us
  transfers between devices with their start and end apart: 2, of which 1 were waited for; matrix products, arithmetic and copies ran while one was open for 0% of the time, Pallas kernels for 4%

profile of v3, /device:TPU:6, one launch (start us, length us, event | category | flops | bytes accessed | tf_op | source)
XLA Modules:
  0.0 31.1 jit_solution(403602711666480722)
XLA Ops:
  0.0 1.3 %shard_map.64 = (f32[40,128]{1,0:T(8,128)S(1)}, f32[768,128]{1,0:T(8,128)S(1)}, f32[128,128]{1,0:T(8,128)S(1)}, f32[128,128]{1,0:T(8,128)S(1)}, s32[128,128]{1,0:T(8,128)S(1)}) custom-call(f32[768,128]{1,0:T(8,128)} %bitcast.7, f32[128,128]{1,0:T(8,128)} %bitcast.8, f32[128,128]{1,0:T(8,128)} %bitcast.9, s32[128,128]{1,0:T(8,128)} %bitcast.10), custom_call_target="tpu_custom_call" | custom-call | tf_op jit(solution)/shard_map/pallas_call | solution.py:386
  1.3 8.4 %collective-permute-start = (f32[40,128]{1,0:T(8,128)S(1)}, f32[40,128]{1,0:T(8,128)S(1)}, u32[]{:S(2)}, u32[]{:S(2)}) collective-permute-start(f32[40,128]{1,0:T(8,128)S(1)} %get-tuple-element.23.own), channel_id=1, source_target_pairs={{1,2},{3,4},{5,6},{7,8},{9,10},{11,12},{13,14},{15,16},{17,18},{19... | collective-permute-start | bytes 61448 | tf_op jit(solution)/shard_map/ppermute | solution.py:411
  9.8 0.2 shard_map.65
  10.0 1.8 %all-gather.near = f32[80,128]{1,0:T(8,128)S(1)} all-gather(f32[40,128]{1,0:T(8,128)S(1)} %get-tuple-element.23.own), channel_id=2, replica_groups={{0,1},{2,3},{4,5},{6,7},{8,9},{10,11},{12,13},{14,15},{16,17},{18,19},{..., dimensions={0}, use_global_device_ids=true | all-gather | bytes 61440 | tf_op jit(solution)/shard_map/all_gather | solution.py:415
  11.8 0.0 collective-permute-done.far
  11.8 0.2 shard_map.66
  12.0 9.0 %collective-permute-start.1 = (f32[232,128]{1,0:T(8,128)S(1)}, f32[232,128]{1,0:T(8,128)S(1)}, u32[]{:S(2)}, u32[]{:S(2)}) collective-permute-start(f32[232,128]{1,0:T(8,128)S(1)} %get-tuple-element.30), channel_id=1, source_target_pairs={{32,64},{33,65},{34,66},{35,67},{36,68},{37,69},{38,70},{39,71},{4... | collective-permute-start | bytes 356360 | tf_op jit(solution)/shard_map/ppermute | solution.py:411
  21.0 0.0 copy-start
  21.1 0.0 copy-start.1
  21.1 0.8 %shard_map.67 = (f32[768,128]{1,0:T(8,128)S(1)}, f32[512,128]{1,0:T(8,128)S(1)}) custom-call(f32[768,128]{1,0:T(8,128)S(1)} %get-tuple-element.24.t.tracer, f32[128,128]{1,0:T(8,128)S(1)} %get-tuple-element.25.u.east, f32[128,128]{1,0:T(8,128)S(1)} %get-tuple-element.26.v.north, s32[128,128]{1,0:T(8,128)S(1)} %get-tuple-element.27.m.mask, ...), custom_call_target="tpu_custom_call" | custom-call | tf_op jit(solution)/shard_map/pallas_call | solution.py:386
  21.9 0.0 copy-done
  21.9 0.0 copy-done.1
  21.9 0.3 shard_map.68
  22.2 5.7 %all-gather.1.near = f32[464,128]{1,0:T(8,128)S(1)} all-gather(f32[232,128]{1,0:T(8,128)S(1)} %get-tuple-element.31), channel_id=3, replica_groups={{0,32},{1,33},{2,34},{3,35},{4,36},{5,37},{6,38},{7,39},{8,40},{9,41},{..., dimensions={0}, use_global_device_ids=true | all-gather | bytes 356352 | tf_op jit(solution)/shard_map/all_gather | solution.py:415
  27.9 1.7 %collective-permute-done.1.far = f32[232,128]{1,0:T(8,128)S(1)} collective-permute-done((f32[232,128]{1,0:T(8,128)S(1)}, f32[232,128]{1,0:T(8,128)S(1)}, u32[]{:S(2)}, u32[]{:S(2)}) %collective-permute-start.1) | collective-permute-done | bytes 118816 | tf_op jit(solution)/shard_map/ppermute | solution.py:411
  29.6 1.5 %shard_map.69 = f32[768,128]{1,0:T(8,128)} custom-call(f32[232,128]{1,0:T(8,128)S(1)} %collective-permute-done.1.far, f32[464,128]{1,0:T(8,128)S(1)} %all-gather.1.near, f32[768,128]{1,0:T(8,128)S(1)} %get-tuple-element.24.t.tracer, f32[128,128]{1,0:T(8,128)S(1)} %get-tuple-element.26.v.north, s32[128,128]{1,0:T(8,128)S(1)} %get-tuple-element.27.m.mask, ...), custom_call_target="tpu_custom_call" | custom-call | tf_op jit(solution)/shard_map/pallas_call | solution.py:386
Async XLA Ops:
  1.3 10.5 %collective-permute-start = (f32[40,128]{1,0:T(8,128)S(1)}, f32[40,128]{1,0:T(8,128)S(1)}, u32[]{:S(2)}, u32[]{:S(2)}) collective-permute-start(f32[40,128]{1,0:T(8,128)S(1)} %get-tuple-element.23.own), channel_id=1, source_target_pairs={{1,2},{3,4},{5,6},{7,8},{9,10},{11,12},{13,14},{15,16},{17,18},{19... | collective-permute-start | bytes 61448 | tf_op jit(solution)/shard_map/ppermute | solution.py:411
  12.0 17.6 %collective-permute-start.1 = (f32[232,128]{1,0:T(8,128)S(1)}, f32[232,128]{1,0:T(8,128)S(1)}, u32[]{:S(2)}, u32[]{:S(2)}) collective-permute-start(f32[232,128]{1,0:T(8,128)S(1)} %get-tuple-element.30), channel_id=1, source_target_pairs={{32,64},{33,65},{34,66},{35,67},{36,68},{37,69},{38,70},{39,71},{4... | collective-permute-start | bytes 356360 | tf_op jit(solution)/shard_map/ppermute | solution.py:411
  21.0 0.8 %copy-start = (f32[16,8,128]{2,1,0:T(8,128)S(1)}, f32[16,8,128]{2,1,0:T(8,128)}, u32[]{:S(2)}) copy-start(f32[16,8,128]{2,1,0:T(8,128)} %param.11) | copy-start | bytes 196612
  21.1 0.8 %copy-start.1 = (s32[8,128]{1,0:T(8,128)S(1)}, s32[8,128]{1,0:T(8,128)}, u32[]{:S(2)}) copy-start(s32[8,128]{1,0:T(8,128)} %bottom.1) | copy-start | bytes 12292

commit v4 on v3

--- a/solution.py
+++ b/solution.py
@@ -24,6 +24,7 @@
 ROW_M = ROW_V + K
 ROW_C = ROW_M + K
 PAY_ROWS = ROW_C + ROWS
+EARLY_ROWS = PAY_ROWS + ROWS
 
 AUX_T = 0
 AUX_V = TPACKS
@@ -52,16 +53,28 @@
     return opening * (jnp.maximum(speed, 0.0) + mixing), opening * (jnp.minimum(speed, 0.0) - mixing)
 
 
+def rows_at(start, size):
+    return pl.ds(start if isinstance(start, int) else pl.multiple_of(start, ROWS), size)
+
+
 def tile(ref, index):
-    return ref[index * ROWS : (index + 1) * ROWS, :]
+    return ref[rows_at(index * ROWS, ROWS), :]
 
 
 def put(ref, index, value):
-    ref[index * ROWS : (index + 1) * ROWS, :] = value
+    ref[rows_at(index * ROWS, ROWS), :] = value
 
 
 def edge(ref, start, size, row):
     return ref[pl.ds(start * ROWS + row, size, stride=ROWS), :]
+
+
+def repeat(count, body, unroll=1):
+    def step(i, carry):
+        body(i)
+        return carry
+
+    lax.fori_loop(0, count, step, 0, unroll=unroll)
 
 
 def lane_base(field, k):
@@ -138,20 +151,26 @@
         pay_far[ROW_M:ROW_C, :] = x[ROW_M:]
 
 
+def early_kernel(pay_far, own, early, own_out):
+    own_out[...] = own[...]
+    early[:ROW_C, :] = pay_far[:ROW_C, :]
+    early[ROW_C:, :] = jnp.zeros((EARLY_ROWS - ROW_C, COLS), jnp.float32)
+
+
 def level_faces(east, north, mask, k):
     u, v, m = tile(east, k), tile(north, k), tile(mask, k).astype(jnp.float32)
     open_x = jnp.where(lanes() < COLS - 1, m * roll(m, -1, 1), 0.0)
     open_y = jnp.where(row_ids() < ROWS - 1, m * roll(m, -1, 0), 0.0)
     ax, bx = face(0.5 * (u + roll(u, -1, 1)), open_x)
     ay, by = face(0.5 * (v + roll(v, -1, 0)), open_y)
-    return ax, bx, ay, by
+    middle = (roll(bx, 1, 1) - ax) + (roll(by, 1, 0) - ay)
+    return middle, roll(ax, 1, 1), -bx, roll(ay, 1, 0), -by
 
 
 def inner_sum(t, faces):
-    ax, bx, ay, by = faces
-    fe = ax * t + bx * roll(t, -1, 1)
-    gn = ay * t + by * roll(t, -1, 0)
-    return (roll(fe, 1, 1) - fe) + (roll(gn, 1, 0) - gn)
+    middle, west, east, south, north = faces
+    sides = (west * roll(t, 1, 1) + east * roll(t, -1, 1)) + (south * roll(t, 1, 0) + north * roll(t, -1, 0))
+    return middle * t + sides
 
 
 def flipped(x):
@@ -161,18 +180,6 @@
     return x
 
 
-def inner_kernel(tracer, east, north, mask, ahead, part, coeff):
-    del ahead
-    for k in range(K):
-        faces = level_faces(east, north, mask, k)
-        for i in range(4):
-            put(coeff, i * K + k, faces[i])
-        for f in range(NT):
-            index = f * K + k
-            t = tile(tracer, index)
-            put(part, index, t + inner_sum(t, faces))
-
-
 def both_halves(x, half):
     swapped = roll(x, 64, 1)
     low = lanes() < 64
@@ -184,7 +191,10 @@
     return jnp.where(lane == 0, 1.0, jnp.where(lane == COLS - 1, -1.0, 0.0))
 
 
-def outward_kernel(own, near, far, far_in, near_in, pay_far, pay_near, aux):
+def outward_kernel(
+    own, near, far, far_in, near_in, tracer, east, north, mask, mix, bottom,
+    pay_far, pay_near, aux, corner_far, *refs,
+):
     lat_odd = lax.rem(lax.axis_index("lat"), 2)
     lon_odd = lax.rem(lax.axis_index("lon"), 2)
     is_top = lax.axis_index("lat") == lax.axis_size("lat") - 1
@@ -238,19 +248,42 @@
     )
     rows = row_ids()
     turned = jnp.where((rows == AUX_V) | (rows >= AUX_F), -turned, turned)
-    pay_far[ROW_C:, :] = jnp.where(is_top, turned, c)
-
-
-def column_kernel(tracer, part, aux, own, mix, bottom, full, both, rows_0, rows_7, packs, solve, spread):
+    c = jnp.where(is_top, turned, c)
+    pay_far[ROW_C:, :] = c
+    corner_far[...] = c
+
+    @pl.when(ahead_of_partner())
+    def _():
+        columns(tracer, east, north, mask, mix, bottom, aux, *refs)
+
+
+def spread_out(spread, packed, sign):
+    def pair(p):
+        x = packed(p)
+        for f in (0, 1):
+            for k in range(K):
+                put(spread, (2 * p + f) * K + k, sign * roll(x, COLS - 1 - (lane_base(f, k) + 1), 1))
+
+    for p in range(TPACKS):
+        pair(p)
+
+
+def columns(tracer, east, north, mask, mix, bottom, aux, full, both, rows_0, rows_7, packs, solve, coeff, spread):
     sign = edge_sign()
-    for f in range(NT):
-        packed = tile(aux, AUX_F + f // 2)
-        for k in range(K):
-            put(spread, f * K + k, sign * roll(packed, COLS - 1 - (lane_base(f, k) + 1), 1))
-    for index in range(TILES):
-        x = tile(part, index) + tile(spread, index)
-        put(full, index, x)
-        put(both, index, tile(tracer, index) + x)
+    spread_out(spread, lambda p: tile(aux, AUX_F + p), sign)
+
+    def level(k):
+        faces = level_faces(east, north, mask, k)
+        for i in range(5):
+            put(coeff, i * K + k, faces[i])
+        for f in range(NT):
+            index = f * K + k
+            t = tile(tracer, index)
+            x = t + (inner_sum(t, faces) + tile(spread, index))
+            put(full, index, x)
+            put(both, index, t + x)
+
+    repeat(K, level, unroll=8)
     rows_0[...] = edge(full, 0, TILES, 0)
     rows_7[...] = edge(full, 0, TILES, ROWS - 1)
     for p in range(TPACKS):
@@ -276,10 +309,29 @@
         lower = upper
 
 
+COLUMN_ROWS = [TILES * ROWS, TILES * ROWS, TILES, TILES, TPACKS * ROWS, 3 * K * ROWS, 5 * K * ROWS]
+
+
+def ahead_of_partner():
+    lat, count = lax.axis_index("lat"), lax.axis_size("lat")
+    place = lax.rem(lat, 4)
+    waits = ((place >= 2) & (lat < count // 2)) | ((place < 2) & (lat >= count // 2))
+    return waits & (lax.rem(lax.axis_index("lon"), 8) < 2)
+
+
+def column_kernel(tracer, east, north, mask, mix, bottom, aux, *refs):
+    count = len(COLUMN_ROWS)
+
+    @pl.when(jnp.logical_not(ahead_of_partner()))
+    def _():
+        columns(tracer, east, north, mask, mix, bottom, aux, *refs[count:])
+
+
 def last_kernel(
-    far, near, tracer, north, mask, coeff, full, both_sums, rows_0, rows_7, packs, solve, own, aux,
-    out, edge_1, edge_2, spread,
+    early, corner, far, near, tracer, north, mask, coeff, full, both_sums, rows_0, rows_7, packs, solve, own, aux,
+    result, edge_1, edge_2, spread, out, line_1, line_2, line_3, line_4, sems,
 ):
+    lines_refs = (line_1, line_2, line_3, line_4)
     lat_odd = lax.rem(lax.axis_index("lat"), 2)
     odd = lat_odd == 1
     offset = pl.multiple_of((1 - lat_odd) * PAY_ROWS, ROWS)
@@ -288,9 +340,13 @@
     rows = row_ids()
     at_south, at_north = rows == 0, rows == ROWS - 1
 
-    def both(start, size):
-        a = far[start : start + size, :]
-        b = near[pl.ds(pl.multiple_of(offset + start, ROWS), size), :]
+    is_early = early_lon(lax.axis_index("lon"))
+
+    def both(start, size, step=0):
+        place = rows_at(start + step, size)
+        first = early[place, :] if start < ROW_C else corner[...]
+        a = jnp.where(is_early, first, far[place, :])
+        b = near[rows_at(offset + start + step, size), :]
         return jnp.where(odd, a, b), jnp.where(odd, b, a)
 
     c_n, c_s = both(ROW_C, ROWS)
@@ -313,15 +369,23 @@
     own_sum = corner_faces(v0, m0, d_n, d_s)
     a1, b1 = tile(aux, AUX_A), tile(aux, AUX_B)
     sign = edge_sign()
-    for p in range(TPACKS):
+
+    def corner_row(c, ref, p):
+        del c
+        return ref[pl.ds(p, 1), :]
+
+    for c, ref in zip((c_n, c_s, d_n, d_s), lines_refs):
+        ref[...] = c
+
+    def flux_of(p):
+        lines = [corner_row(c, ref, p) for c, ref in zip((c_n, c_s, d_n, d_s), lines_refs)]
         f1 = tile(aux, AUX_F + p)
         s1 = tile(aux, AUX_Q + p) + jnp.where(at_east, f1, -f1)
-        s1 = s1 + halo_sum(tile(aux, AUX_T + p), c_n[p : p + 1], c_s[p : p + 1])
-        s0 = tile(packs, p) + own_sum(tile(own, p), d_n[p : p + 1], d_s[p : p + 1])
-        flux = a1 * jnp.where(at_east, s0, s1) + b1 * jnp.where(at_east, s1, s0)
-        for f in (2 * p, 2 * p + 1):
-            for k in range(K):
-                put(spread, f * K + k, sign * roll(flux, COLS - 1 - (lane_base(f, k) + 1), 1))
+        s1 = s1 + halo_sum(tile(aux, AUX_T + p), lines[0], lines[1])
+        s0 = tile(packs, p) + own_sum(tile(own, p), lines[2], lines[3])
+        return a1 * jnp.where(at_east, s0, s1) + b1 * jnp.where(at_east, s1, s0)
+
+    spread_out(spread, flux_of, sign)
 
     v_n, v_s = both(ROW_V, K)
     m_n, m_s = both(ROW_M, K)
@@ -330,8 +394,8 @@
     )
     as_, bs = face(0.5 * (v_s + edge(north, 0, K, 0)), m_s * edge(mask, 0, K, 0).astype(jnp.float32))
 
-    def edge_flux(c, f):
-        line = jnp.broadcast_to(c[AUX_F + f // 2 : AUX_F + f // 2 + 1], (ROWS, COLS))
+    def edge_flux(ref, p, f):
+        line = jnp.broadcast_to(ref[pl.ds(AUX_F + p, 1), :], (ROWS, COLS))
         return jnp.concatenate(
             [
                 sign * pltpu.roll(line, COLS - 1 - (lane_base(f, k) + 1), 1, stride=4, stride_axis=0)
@@ -340,29 +404,42 @@
             axis=0,
         )
 
-    for f in range(NT):
-        t_n, t_s = both(ROW_T + f * K, K)
-        p_n, p_s = both(ROW_P + f * K, K)
-        p_n, p_s = p_n + edge_flux(c_n, f), p_s + edge_flux(c_s, f)
-        g_n = an * edge(tracer, f * K, K, ROWS - 1) + bn * t_n
-        g_s = as_ * t_s + bs * edge(tracer, f * K, K, 0)
-        h_n = an * (rows_7[f * K : (f + 1) * K, :] - g_n) + bn * (p_n + g_n)
-        h_s = as_ * (p_s - g_s) + bs * (rows_0[f * K : (f + 1) * K, :] + g_s)
-        edge_1[f * K : (f + 1) * K, :] = g_s
-        edge_1[TILES + f * K : TILES + (f + 1) * K, :] = -g_n
-        edge_2[f * K : (f + 1) * K, :] = g_s + h_s
-        edge_2[TILES + f * K : TILES + (f + 1) * K, :] = -(g_n + h_n)
+    def edge_pair(p):
+        for half in (0, 1):
+            f = 2 * p + half
+            t_n, t_s = both(ROW_T, K, f * K)
+            p_n, p_s = both(ROW_P, K, f * K)
+            p_n = p_n + edge_flux(lines_refs[0], p, half)
+            p_s = p_s + edge_flux(lines_refs[1], p, half)
+            g_n = an * edge(tracer, f * K, K, ROWS - 1) + bn * t_n
+            g_s = as_ * t_s + bs * edge(tracer, f * K, K, 0)
+            here = rows_at(f * K, K)
+            there = rows_at(TILES + f * K, K)
+            h_n = an * (rows_7[here, :] - g_n) + bn * (p_n + g_n)
+            h_s = as_ * (p_s - g_s) + bs * (rows_0[here, :] + g_s)
+            edge_1[here, :] = g_s
+            edge_1[there, :] = -g_n
+            edge_2[here, :] = g_s + h_s
+            edge_2[there, :] = -(g_n + h_n)
+
+    for p in range(TPACKS):
+        edge_pair(p)
 
     def outer(ref, index):
-        low = ref[index : index + 1, :]
-        high = ref[TILES + index : TILES + index + 1, :]
+        low = ref[pl.ds(index, 1), :]
+        high = ref[pl.ds(TILES + index, 1), :]
         return jnp.where(at_south, low, jnp.where(at_north, high, 0.0))
 
-    for f in range(NT):
+
+    def copy_of(f):
+        place = rows_at(f * K * ROWS, K * ROWS)
+        return pltpu.make_async_copy(out.at[place, :], result.at[place, :], sems.at[f])
+
+    def tracer_columns(f):
         value = None
         for k in range(K):
             index = f * K + k
-            faces = [tile(coeff, i * K + k) for i in range(4)]
+            faces = [tile(coeff, i * K + k) for i in range(5)]
             s = tile(full, index) + outer(edge_1, index)
             rhs = (tile(both_sums, index) + inner_sum(s, faces)) + (tile(spread, index) + outer(edge_2, index))
             value_new = rhs * tile(solve, k)
@@ -374,11 +451,22 @@
             index = f * K + k
             value = tile(out, index) - tile(solve, 2 * K + k) * value
             put(out, index, value)
-
-
-def call(kernel, outs, scratch_rows, *operands, hbm=False, scratch=(), alias=None):
+        copy_of(f).start()
+
+    for f in range(NT):
+        tracer_columns(f)
+    for f in range(NT):
+        copy_of(f).wait()
+
+
+def early_lon(lon):
+    place = lax.rem(lon, 8) if not isinstance(lon, int) else lon % 8
+    return (place >= 2) & (place < 6)
+
+
+def call(kernel, outs, scratch_rows, *operands, hbm=False, hbm_out=False, scratch=(), alias=None):
     vmem = pl.BlockSpec(memory_space=pltpu.VMEM)
-    place = pl.BlockSpec(memory_space=pltpu.HBM) if hbm else vmem
+    in_hbm = pl.BlockSpec(memory_space=pltpu.HBM)
     shapes = [
         x if isinstance(x, jax.ShapeDtypeStruct) else jax.ShapeDtypeStruct((x, COLS), jnp.float32)
         for x in outs
@@ -386,8 +474,8 @@
     return pl.pallas_call(
         kernel,
         out_shape=shapes,
-        in_specs=[place] * len(operands),
-        out_specs=[vmem] * len(shapes),
+        in_specs=[in_hbm if hbm else vmem] * len(operands),
+        out_specs=[in_hbm if hbm_out else vmem] * len(shapes),
         scratch_shapes=[pltpu.VMEM((rows, COLS), jnp.float32) for rows in scratch_rows] + list(scratch),
         compiler_params=pltpu.CompilerParams(vmem_limit_bytes=24 * 1024 * 1024),
         input_output_aliases=alias or {},
@@ -433,28 +521,37 @@
     )
     far = swapped(own, lon_far)
     pay_far, pay_near = call(rows_kernel, [PAY_ROWS, PAY_ROWS], [], t, u, v, m)
-    near = gathered(own, lon_near)
-    pay_far, pay_near, aux = call(
+    lon_count = lax.axis_size("lon")
+    lat_early = [(a, b) for a, b in lat_far if early_lon(a % lon_count)]
+    lat_late = [(a, b) for a, b in lat_far if not early_lon(a % lon_count)]
+    early, own_again = call(early_kernel, [EARLY_ROWS, PACK_ROWS], [], pay_far, own)
+    early_rows = swapped(early, lat_early)
+    near = gathered(own_again, lon_near)
+    vertical = flat(vertical_mix)
+    pay_far, pay_near, aux, corner, *ready = call(
         outward_kernel,
-        [PAY_ROWS, PAY_ROWS, AUX * ROWS],
-        [],
-        own, near, far, pay_far, pay_near,
+        [PAY_ROWS, PAY_ROWS, AUX * ROWS, ROWS] + COLUMN_ROWS,
+        [TILES * ROWS],
+        own, near, far, pay_far, pay_near, t, u, v, m, vertical, bottom_level,
         alias={3: 0, 4: 1},
     )
-    far_rows = swapped(pay_far, lat_far)
-    part, coeff = call(inner_kernel, [TILES * ROWS, 4 * K * ROWS], [], t, u, v, m, aux)
+    far_rows = swapped(pay_far, lat_late)
+    corner_rows = swapped(corner, lat_early)
     near_rows = gathered(pay_near, lat_near)
-    full, both, rows_0, rows_7, packs, solve = call(
+    full, both, rows_0, rows_7, packs, solve, coeff = call(
         column_kernel,
-        [TILES * ROWS, TILES * ROWS, TILES, TILES, TPACKS * ROWS, 3 * K * ROWS],
+        COLUMN_ROWS,
         [TILES * ROWS],
-        t, part, aux, own, flat(vertical_mix), bottom_level,
+        t, u, v, m, vertical, bottom_level, aux, *ready,
+        alias={7 + i: i for i in range(len(COLUMN_ROWS))},
     )
     (out,) = call(
         last_kernel,
         [TILES * ROWS],
-        [2 * TILES, 2 * TILES, TILES * ROWS],
-        far_rows, near_rows, t, v, m, coeff, full, both, rows_0, rows_7, packs, solve, own, aux,
+        [2 * TILES, 2 * TILES, TILES * ROWS, TILES * ROWS] + [ROWS] * 4,
+        early_rows, corner_rows, far_rows, near_rows, t, v, m, coeff, full, both, rows_0, rows_7, packs, solve, own, aux,
+        scratch=[pltpu.SemaphoreType.DMA((NT,))],
+        hbm_out=True,
     )
     return out.reshape(tracer.shape)
 

time: 31.5 us -> 30.3 us (0.962)
  the two profiles are of different devices: /device:TPU:6 before, /device:TPU:94 now
where the time goes in v4:
time: 30.3 us; the launch traced here: 30.1 us
  starting transfers between devices  14.6 us (48%)
  blocking collectives  9.12 us (30%)
  Pallas kernels  3.97 us (13%)
  waiting for transfers between devices  2.32 us (8%)
    ppermute x4, starting transfers between devices, swapped(): lax.ppermute(x, AXES, [(a, b) for a, b in groups] + [(b, a) for a, b in g...  14.6 us
    all_gather x2, blocking collectives, gathered(): both = lax.all_gather(x, AXES, axis_index_groups=[list(g) for g in groups])  9.12 us
    pallas_call x6, Pallas kernels, call(): pl.pallas_call(kernel, out_shape=shapes, in_specs=[in_hbm if hbm else vme...  3.97 us
    ppermute x4, waiting for transfers between devices, swapped(): lax.ppermute(x, AXES, [(a, b) for a, b in groups] + [(b, a) for a, b in g...  2.32 us
  transfers between devices with their start and end apart: 4, of which 1 were waited for; matrix products, arithmetic and copies ran while one was open for 0% of the time, Pallas kernels for 4%

profile of v4, /device:TPU:94, one launch (start us, length us, event | category | flops | bytes accessed | tf_op | source)
XLA Modules:
  0.0 30.1 jit_solution(11296556887655861553)
XLA Ops:
  0.0 1.3 %shard_map.64 = (f32[40,128]{1,0:T(8,128)S(1)}, f32[768,128]{1,0:T(8,128)S(1)}, f32[128,128]{1,0:T(8,128)S(1)}, f32[128,128]{1,0:T(8,128)S(1)}, s32[128,128]{1,0:T(8,128)S(1)}) custom-call(f32[768,128]{1,0:T(8,128)} %bitcast.8, f32[128,128]{1,0:T(8,128)} %bitcast.9, f32[128,128]{1,0:T(8,128)} %bitcast.10, s32[128,128]{1,0:T(8,128)} %bitcast.11), custom_call_target="tpu_custom_call" | custom-call | tf_op jit(solution)/shard_map/pallas_call | solution.py:474
  1.4 1.9 %collective-permute-start.1 = (f32[40,128]{1,0:T(8,128)S(1)}, f32[40,128]{1,0:T(8,128)S(1)}, u32[]{:S(2)}, u32[]{:S(2)}) collective-permute-start(f32[40,128]{1,0:T(8,128)S(1)} %get-tuple-element.37.own), channel_id=1, source_target_pairs={{1,2},{3,4},{5,6},{7,8},{9,10},{11,12},{13,14},{15,16},{17,18},{19... | collective-permute-start | bytes 61448 | tf_op jit(solution)/shard_map/ppermute | solution.py:499
  3.3 0.2 shard_map.65
  3.5 0.0 copy-start.1
  3.5 0.0 copy-start
  3.5 9.1 %collective-permute-start = (f32[240,128]{1,0:T(8,128)S(1)}, f32[240,128]{1,0:T(8,128)S(1)}, u32[]{:S(2)}, u32[]{:S(2)}) collective-permute-start(f32[240,128]{1,0:T(8,128)S(1)} %get-tuple-element.38), channel_id=1, source_target_pairs={{34,66},{35,67},{36,68},{37,69},{42,74},{43,75},{44,76},{45,77},{5... | collective-permute-start | bytes 368648 | tf_op jit(solution)/shard_map/ppermute | solution.py:499
  12.7 3.2 %all-gather.near = f32[80,128]{1,0:T(8,128)S(1)} all-gather(f32[40,128]{1,0:T(8,128)S(1)} %get-tuple-element.39), channel_id=2, replica_groups={{0,1},{2,3},{4,5},{6,7},{8,9},{10,11},{12,13},{14,15},{16,17},{18,19},{..., dimensions={0}, use_global_device_ids=true | all-gather | bytes 61440 | tf_op jit(solution)/shard_map/all_gather | solution.py:503
  15.9 0.0 collective-permute-done.1.far
  15.9 0.0 copy-done.1
  15.9 0.0 copy-done
  15.9 0.2 shard_map.67
  16.1 0.7 %collective-permute-start.3 = (f32[232,128]{1,0:T(8,128)S(1)}, f32[232,128]{1,0:T(8,128)S(1)}, u32[]{:S(2)}, u32[]{:S(2)}) collective-permute-start(f32[232,128]{1,0:T(8,128)S(1)} %get-tuple-element.42), channel_id=1, source_target_pairs={{32,64},{33,65},{38,70},{39,71},{40,72},{41,73},{46,78},{47,79},{4... | collective-permute-start | bytes 356360 | tf_op jit(solution)/shard_map/ppermute | solution.py:499
  16.8 2.8 %collective-permute-start.2 = (f32[8,128]{1,0:T(8,128)S(1)}, f32[8,128]{1,0:T(8,128)S(1)}, u32[]{:S(2)}, u32[]{:S(2)}) collective-permute-start(f32[8,128]{1,0:T(8,128)S(1)} %get-tuple-element.41), channel_id=1, source_target_pairs={{34,66},{35,67},{36,68},{37,69},{42,74},{43,75},{44,76},{45,77},{5... | collective-permute-start | bytes 12296 | tf_op jit(solution)/shard_map/ppermute | solution.py:499
  19.7 5.9 %all-gather.1.near = f32[464,128]{1,0:T(8,128)S(1)} all-gather(f32[232,128]{1,0:T(8,128)S(1)} %get-tuple-element.43), channel_id=3, replica_groups={{0,32},{1,33},{2,34},{3,35},{4,36},{5,37},{6,38},{7,39},{8,40},{9,41},{..., dimensions={0}, use_global_device_ids=true | all-gather | bytes 356352 | tf_op jit(solution)/shard_map/all_gather | solution.py:503
  25.6 0.9 %shard_map.68 = (f32[768,128]{1,0:T(8,128)S(1)}, f32[768,128]{1,0:T(8,128)S(1)}, f32[96,128]{1,0:T(8,128)S(1)}, f32[96,128]{1,0:T(8,128)S(1)}, f32[24,128]{1,0:T...) custom-call(f32[768,128]{1,0:T(8,128)S(1)} %get-tuple-element.32.t.t, ...), custom_call_target="tpu_custom_call", output_to_operand_aliasing={{0}: (7, {}), {1}: (8, {}), {2}: (9, {}), {3}: (10, {}), {4... | custom-call | tf_op jit(solution)/shard_map/pallas_call | solution.py:474
  26.4 2.3 %collective-permute-done.2.corner = f32[8,128]{1,0:T(8,128)S(1)} collective-permute-done((f32[8,128]{1,0:T(8,128)S(1)}, f32[8,128]{1,0:T(8,128)S(1)}, u32[]{:S(2)}, u32[]{:S(2)}) %collective-permute-start.2) | collective-permute-done | bytes 4128 | tf_op jit(solution)/shard_map/ppermute | solution.py:499
  28.7 0.0 collective-permute-done.early
  28.7 0.0 collective-permute-done.3.far
  28.7 1.3 %shard_map.69 = f32[768,128]{1,0:T(8,128)} custom-call(f32[240,128]{1,0:T(8,128)S(1)} %collective-permute-done.early, f32[8,128]{1,0:T(8,128)S(1)} %collective-permute-done.2.corner, f32[232,128]{1,0:T(8,128)S(1)} %collective-permute-done.3.far, f32[464,128]{1,0:T(8,128)S(1)} %all-gather.1.near, f32[768,128]{1,0:T(8,128)S(1)} %get-tuple-element.32.t.tracer, ...), custom_call_target="tpu_custom_call" | custom-call | tf_op jit(solution)/shard_map/pallas_call | solution.py:474
  (1 shorter events, 0.0 us)
Async XLA Ops:
  1.4 14.5 %collective-permute-start.1 = (f32[40,128]{1,0:T(8,128)S(1)}, f32[40,128]{1,0:T(8,128)S(1)}, u32[]{:S(2)}, u32[]{:S(2)}) collective-permute-start(f32[40,128]{1,0:T(8,128)S(1)} %get-tuple-element.37.own), channel_id=1, source_target_pairs={{1,2},{3,4},{5,6},{7,8},{9,10},{11,12},{13,14},{15,16},{17,18},{19... | collective-permute-start | bytes 61448 | tf_op jit(solution)/shard_map/ppermute | solution.py:499
  3.5 12.4 %copy-start.1 = (s32[8,128]{1,0:T(8,128)S(1)}, s32[8,128]{1,0:T(8,128)}, u32[]{:S(2)}) copy-start(s32[8,128]{1,0:T(8,128)} %bottom.3) | copy-start | bytes 12292
  3.5 12.4 %copy-start = (f32[16,8,128]{2,1,0:T(8,128)S(1)}, f32[16,8,128]{2,1,0:T(8,128)}, u32[]{:S(2)}) copy-start(f32[16,8,128]{2,1,0:T(8,128)} %param.11) | copy-start | bytes 196612
  3.5 25.2 %collective-permute-start = (f32[240,128]{1,0:T(8,128)S(1)}, f32[240,128]{1,0:T(8,128)S(1)}, u32[]{:S(2)}, u32[]{:S(2)}) collective-permute-start(f32[240,128]{1,0:T(8,128)S(1)} %get-tuple-element.38), channel_id=1, source_target_pairs={{34,66},{35,67},{36,68},{37,69},{42,74},{43,75},{44,76},{45,77},{5... | collective-permute-start | bytes 368648 | tf_op jit(solution)/shard_map/ppermute | solution.py:499
  16.1 12.6 %collective-permute-start.3 = (f32[232,128]{1,0:T(8,128)S(1)}, f32[232,128]{1,0:T(8,128)S(1)}, u32[]{:S(2)}, u32[]{:S(2)}) collective-permute-start(f32[232,128]{1,0:T(8,128)S(1)} %get-tuple-element.42), channel_id=1, source_target_pairs={{32,64},{33,65},{38,70},{39,71},{40,72},{41,73},{46,78},{47,79},{4... | collective-permute-start | bytes 356360 | tf_op jit(solution)/shard_map/ppermute | solution.py:499
  16.8 11.9 %collective-permute-start.2 = (f32[8,128]{1,0:T(8,128)S(1)}, f32[8,128]{1,0:T(8,128)S(1)}, u32[]{:S(2)}, u32[]{:S(2)}) collective-permute-start(f32[8,128]{1,0:T(8,128)S(1)} %get-tuple-element.41), channel_id=1, source_target_pairs={{34,66},{35,67},{36,68},{37,69},{42,74},{43,75},{44,76},{45,77},{5... | collective-permute-start | bytes 12296 | tf_op jit(solution)/shard_map/ppermute | solution.py:499

commit v5 on v4

--- a/solution.py
+++ b/solution.py
@@ -107,10 +107,12 @@
     return ts + sums + [v, m]
 
 
-def load_kernel(tracer, east, north, mask, pack, t, u, v, m, sems):
+def load_kernel(tracer, east, north, mask, mix, bottom, pack, t, u, v, m, vertical, depth, sems):
     copies = [
         pltpu.make_async_copy(src, dst, sems.at[i])
-        for i, (src, dst) in enumerate(((tracer, t), (east, u), (north, v), (mask, m)))
+        for i, (src, dst) in enumerate(
+            ((tracer, t), (east, u), (north, v), (mask, m), (mix, vertical), (bottom, depth))
+        )
     ]
     for copy in copies:
         copy.start()
@@ -124,16 +126,18 @@
             return tile(m, k).astype(jnp.float32)
         return tile(v, k)
 
-    for copy in copies[1:]:
+    for copy in copies[1:4]:
         copy.wait()
     for p in range(TPACKS, PACKS):
         put(pack, p, packed_edges(load, range(2 * p, min(2 * p + 2, FIELDS))))
     copies[0].wait()
     for p in range(TPACKS):
         put(pack, p, packed_edges(load, range(2 * p, 2 * p + 2)))
-
-
-def rows_kernel(t, u, v, m, pay_far, pay_near):
+    for copy in copies[4:]:
+        copy.wait()
+
+
+def rows_kernel(t, u, v, m, own, pay_far, pay_near, early, own_out):
     odd = lax.rem(lax.axis_index("lat"), 2) == 1
     upper = row_part(t, u, v, m, ROWS - 1, ROWS - 2)
     lower = row_part(t, u, v, m, 0, 1)
@@ -150,11 +154,9 @@
         pay_far[ROW_V:ROW_M, :] = -x[ROW_V:ROW_M]
         pay_far[ROW_M:ROW_C, :] = x[ROW_M:]
 
-
-def early_kernel(pay_far, own, early, own_out):
-    own_out[...] = own[...]
     early[:ROW_C, :] = pay_far[:ROW_C, :]
     early[ROW_C:, :] = jnp.zeros((EARLY_ROWS - ROW_C, COLS), jnp.float32)
+    own_out[...] = own[...]
 
 
 def level_faces(east, north, mask, k):
@@ -268,7 +270,7 @@
         pair(p)
 
 
-def columns(tracer, east, north, mask, mix, bottom, aux, full, both, rows_0, rows_7, packs, solve, coeff, spread):
+def columns(tracer, east, north, mask, mix, bottom, aux, full, both, packs, solve, coeff, spread):
     sign = edge_sign()
     spread_out(spread, lambda p: tile(aux, AUX_F + p), sign)
 
@@ -284,8 +286,6 @@
             put(both, index, t + x)
 
     repeat(K, level, unroll=8)
-    rows_0[...] = edge(full, 0, TILES, 0)
-    rows_7[...] = edge(full, 0, TILES, ROWS - 1)
     for p in range(TPACKS):
         put(packs, p, packed_edges(lambda f, k: tile(full, f * K + k), (2 * p, 2 * p + 1)))
     depth = bottom[...]
@@ -309,7 +309,7 @@
         lower = upper
 
 
-COLUMN_ROWS = [TILES * ROWS, TILES * ROWS, TILES, TILES, TPACKS * ROWS, 3 * K * ROWS, 5 * K * ROWS]
+COLUMN_ROWS = [TILES * ROWS, TILES * ROWS, TPACKS * ROWS, 3 * K * ROWS, 5 * K * ROWS]
 
 
 def ahead_of_partner():
@@ -328,9 +328,10 @@
 
 
 def last_kernel(
-    early, corner, far, near, tracer, north, mask, coeff, full, both_sums, rows_0, rows_7, packs, solve, own, aux,
-    result, edge_1, edge_2, spread, out, line_1, line_2, line_3, line_4, sems,
+    early, corner, far, near, tracer, north, mask, coeff, full_in, sums_in, packs, solve, own, aux,
+    result, full, sums, spread, out, line_1, line_2, line_3, line_4, sems,
 ):
+    del full_in, sums_in
     lines_refs = (line_1, line_2, line_3, line_4)
     lat_odd = lax.rem(lax.axis_index("lat"), 2)
     odd = lat_odd == 1
@@ -340,7 +341,7 @@
     rows = row_ids()
     at_south, at_north = rows == 0, rows == ROWS - 1
 
-    is_early = early_lon(lax.axis_index("lon"))
+    is_early = early_far(lax.axis_index("lat"), lax.axis_index("lon"), lax.axis_size("lat"), lax.axis_size("lon"))
 
     def both(start, size, step=0):
         place = rows_at(start + step, size)
@@ -413,23 +414,16 @@
             p_s = p_s + edge_flux(lines_refs[1], p, half)
             g_n = an * edge(tracer, f * K, K, ROWS - 1) + bn * t_n
             g_s = as_ * t_s + bs * edge(tracer, f * K, K, 0)
-            here = rows_at(f * K, K)
-            there = rows_at(TILES + f * K, K)
-            h_n = an * (rows_7[here, :] - g_n) + bn * (p_n + g_n)
-            h_s = as_ * (p_s - g_s) + bs * (rows_0[here, :] + g_s)
-            edge_1[here, :] = g_s
-            edge_1[there, :] = -g_n
-            edge_2[here, :] = g_s + h_s
-            edge_2[there, :] = -(g_n + h_n)
+            low = pl.ds(f * K * ROWS, K, stride=ROWS)
+            high = pl.ds(f * K * ROWS + ROWS - 1, K, stride=ROWS)
+            s_low, s_high = full[low, :] + g_s, full[high, :] - g_n
+            full[low, :] = s_low
+            full[high, :] = s_high
+            sums[low, :] = sums[low, :] + (g_s + (as_ * (p_s - g_s) + bs * s_low))
+            sums[high, :] = sums[high, :] - (g_n + (an * s_high + bn * (p_n + g_n)))
 
     for p in range(TPACKS):
         edge_pair(p)
-
-    def outer(ref, index):
-        low = ref[pl.ds(index, 1), :]
-        high = ref[pl.ds(TILES + index, 1), :]
-        return jnp.where(at_south, low, jnp.where(at_north, high, 0.0))
-
 
     def copy_of(f):
         place = rows_at(f * K * ROWS, K * ROWS)
@@ -440,8 +434,7 @@
         for k in range(K):
             index = f * K + k
             faces = [tile(coeff, i * K + k) for i in range(5)]
-            s = tile(full, index) + outer(edge_1, index)
-            rhs = (tile(both_sums, index) + inner_sum(s, faces)) + (tile(spread, index) + outer(edge_2, index))
+            rhs = (tile(sums, index) + tile(spread, index)) + inner_sum(tile(full, index), faces)
             value_new = rhs * tile(solve, k)
             if k:
                 value_new = value_new + tile(solve, K + k) * value
@@ -459,12 +452,12 @@
         copy_of(f).wait()
 
 
-def early_lon(lon):
-    place = lax.rem(lon, 8) if not isinstance(lon, int) else lon % 8
-    return (place >= 2) & (place < 6)
-
-
-def call(kernel, outs, scratch_rows, *operands, hbm=False, hbm_out=False, scratch=(), alias=None):
+def early_far(lat, lon, lat_count, lon_count):
+    mirrored = lon_count - 1 - lon
+    return (lon % 8 >= 2) & ((lat < lat_count - 1) | (mirrored % 8 >= 2))
+
+
+def call(kernel, outs, scratch_rows, *operands, hbm=False, hbm_out=0, scratch=(), alias=None):
     vmem = pl.BlockSpec(memory_space=pltpu.VMEM)
     in_hbm = pl.BlockSpec(memory_space=pltpu.HBM)
     shapes = [
@@ -475,7 +468,7 @@
         kernel,
         out_shape=shapes,
         in_specs=[in_hbm if hbm else vmem] * len(operands),
-        out_specs=[in_hbm if hbm_out else vmem] * len(shapes),
+        out_specs=[in_hbm] * hbm_out + [vmem] * (len(shapes) - hbm_out),
         scratch_shapes=[pltpu.VMEM((rows, COLS), jnp.float32) for rows in scratch_rows] + list(scratch),
         compiler_params=pltpu.CompilerParams(vmem_limit_bytes=24 * 1024 * 1024),
         input_output_aliases=alias or {},
@@ -509,49 +502,50 @@
     flat = lambda x: x.reshape(-1, COLS)
     fields = [
         pltpu.with_memory_space_constraint(flat(x), pltpu.HBM)
-        for x in (tracer, east_vel, north_vel, wet_mask)
+        for x in (tracer, east_vel, north_vel, wet_mask, vertical_mix, bottom_level)
     ]
-    own, t, u, v, m = call(
+    own, t, u, v, m, vertical, depth = call(
         load_kernel,
         [PACK_ROWS] + [jax.ShapeDtypeStruct(x.shape, x.dtype) for x in fields],
         [],
         *fields,
         hbm=True,
-        scratch=[pltpu.SemaphoreType.DMA((4,))],
+        scratch=[pltpu.SemaphoreType.DMA((6,))],
     )
     far = swapped(own, lon_far)
-    pay_far, pay_near = call(rows_kernel, [PAY_ROWS, PAY_ROWS], [], t, u, v, m)
-    lon_count = lax.axis_size("lon")
-    lat_early = [(a, b) for a, b in lat_far if early_lon(a % lon_count)]
-    lat_late = [(a, b) for a, b in lat_far if not early_lon(a % lon_count)]
-    early, own_again = call(early_kernel, [EARLY_ROWS, PACK_ROWS], [], pay_far, own)
+    pay_far, pay_near, early, own_again = call(
+        rows_kernel, [PAY_ROWS, PAY_ROWS, EARLY_ROWS, PACK_ROWS], [], t, u, v, m, own
+    )
+    counts = lax.axis_size("lat"), lax.axis_size("lon")
+    lat_early = [(a, b) for a, b in lat_far if early_far(*divmod(b, counts[1]), *counts)]
+    lat_late = [pair for pair in lat_far if pair not in lat_early]
     early_rows = swapped(early, lat_early)
     near = gathered(own_again, lon_near)
-    vertical = flat(vertical_mix)
     pay_far, pay_near, aux, corner, *ready = call(
         outward_kernel,
         [PAY_ROWS, PAY_ROWS, AUX * ROWS, ROWS] + COLUMN_ROWS,
         [TILES * ROWS],
-        own, near, far, pay_far, pay_near, t, u, v, m, vertical, bottom_level,
+        own, near, far, pay_far, pay_near, t, u, v, m, vertical, depth,
         alias={3: 0, 4: 1},
     )
     far_rows = swapped(pay_far, lat_late)
     corner_rows = swapped(corner, lat_early)
     near_rows = gathered(pay_near, lat_near)
-    full, both, rows_0, rows_7, packs, solve, coeff = call(
+    full, both, packs, solve, coeff = call(
         column_kernel,
         COLUMN_ROWS,
         [TILES * ROWS],
-        t, u, v, m, vertical, bottom_level, aux, *ready,
+        t, u, v, m, vertical, depth, aux, *ready,
         alias={7 + i: i for i in range(len(COLUMN_ROWS))},
     )
-    (out,) = call(
+    out, _, _ = call(
         last_kernel,
-        [TILES * ROWS],
-        [2 * TILES, 2 * TILES, TILES * ROWS, TILES * ROWS] + [ROWS] * 4,
-        early_rows, corner_rows, far_rows, near_rows, t, v, m, coeff, full, both, rows_0, rows_7, packs, solve, own, aux,
+        [TILES * ROWS] * 3,
+        [TILES * ROWS, TILES * ROWS] + [ROWS] * 4,
+        early_rows, corner_rows, far_rows, near_rows, t, v, m, coeff, full, both, packs, solve, own, aux,
+        alias={8: 1, 9: 2},
         scratch=[pltpu.SemaphoreType.DMA((NT,))],
-        hbm_out=True,
+        hbm_out=1,
     )
     return out.reshape(tracer.shape)
 

time: 30.3 us -> 30.1 us (level)
    pallas_call x6 -> x5, Pallas kernels: 3.97 us -> 3.92 us  [call(): pl.pallas_call(kernel, out_shape=shapes, in_specs=[in_hbm if hbm else vme...]
where the time goes in v5:
time: 30.1 us; the launch traced here: 29.9 us
  starting transfers between devices  14.4 us (48%)
  blocking collectives  9.11 us (30%)
  Pallas kernels  3.92 us (13%)
  waiting for transfers between devices  2.33 us (8%)
    ppermute x4, starting transfers between devices, swapped(): lax.ppermute(x, AXES, [(a, b) for a, b in groups] + [(b, a) for a, b in g...  14.4 us
    all_gather x2, blocking collectives, gathered(): both = lax.all_gather(x, AXES, axis_index_groups=[list(g) for g in groups])  9.11 us
    pallas_call x5, Pallas kernels, call(): pl.pallas_call(kernel, out_shape=shapes, in_specs=[in_hbm if hbm else vme...  3.92 us
    ppermute x4, waiting for transfers between devices, swapped(): lax.ppermute(x, AXES, [(a, b) for a, b in groups] + [(b, a) for a, b in g...  2.33 us
  transfers between devices with their start and end apart: 4, of which 1 were waited for; matrix products, arithmetic and copies ran while one was open for 0% of the time, Pallas kernels for 4%

profile of v5, /device:TPU:94, one launch (start us, length us, event | category | flops | bytes accessed | tf_op | source)
XLA Modules:
  0.0 29.9 jit_solution(3126521225770504951)
XLA Ops:
  0.0 1.4 %shard_map.64 = (f32[40,128]{1,0:T(8,128)S(1)}, f32[768,128]{1,0:T(8,128)S(1)}, f32[128,128]{1,0:T(8,128)S(1)}, f32[128,128]{1,0:T(8,128)S(1)}, s32[128,128]{1,0...) custom-call(f32[768,128]{1,0:T(8,128)} %bitcast.6, f32[128,128]{1,0:T(8,128)} %bitcast.7, ...), custom_call_target="tpu_custom_call" | custom-call | tf_op jit(solution)/shard_map/pallas_call | solution.py:467
  1.4 1.9 %collective-permute-start.1 = (f32[40,128]{1,0:T(8,128)S(1)}, f32[40,128]{1,0:T(8,128)S(1)}, u32[]{:S(2)}, u32[]{:S(2)}) collective-permute-start(f32[40,128]{1,0:T(8,128)S(1)} %get-tuple-element.35.own), channel_id=1, source_target_pairs={{1,2},{3,4},{5,6},{7,8},{9,10},{11,12},{13,14},{15,16},{17,18},{19... | collective-permute-start | bytes 61448 | tf_op jit(solution)/shard_map/ppermute | solution.py:492
  3.3 0.2 shard_map.65
  3.5 9.0 %collective-permute-start = (f32[240,128]{1,0:T(8,128)S(1)}, f32[240,128]{1,0:T(8,128)S(1)}, u32[]{:S(2)}, u32[]{:S(2)}) collective-permute-start(f32[240,128]{1,0:T(8,128)S(1)} %get-tuple-element.36), channel_id=1, source_target_pairs={{34,66},{35,67},{36,68},{37,69},{38,70},{39,71},{42,74},{43,75},{4... | collective-permute-start | bytes 368648 | tf_op jit(solution)/shard_map/ppermute | solution.py:492
  12.5 3.2 %all-gather.near = f32[80,128]{1,0:T(8,128)S(1)} all-gather(f32[40,128]{1,0:T(8,128)S(1)} %get-tuple-element.37), channel_id=2, replica_groups={{0,1},{2,3},{4,5},{6,7},{8,9},{10,11},{12,13},{14,15},{16,17},{18,19},{..., dimensions={0}, use_global_device_ids=true | all-gather | bytes 61440 | tf_op jit(solution)/shard_map/all_gather | solution.py:496
  15.7 0.0 collective-permute-done.1.far
  15.8 0.2 shard_map.66
  16.0 0.7 %collective-permute-start.3 = (f32[232,128]{1,0:T(8,128)S(1)}, f32[232,128]{1,0:T(8,128)S(1)}, u32[]{:S(2)}, u32[]{:S(2)}) collective-permute-start(f32[232,128]{1,0:T(8,128)S(1)} %get-tuple-element.43), channel_id=1, source_target_pairs={{32,64},{33,65},{40,72},{41,73},{48,80},{49,81},{56,88},{57,89},{9... | collective-permute-start | bytes 356360 | tf_op jit(solution)/shard_map/ppermute | solution.py:492
  16.7 2.8 %collective-permute-start.2 = (f32[8,128]{1,0:T(8,128)S(1)}, f32[8,128]{1,0:T(8,128)S(1)}, u32[]{:S(2)}, u32[]{:S(2)}) collective-permute-start(f32[8,128]{1,0:T(8,128)S(1)} %get-tuple-element.42), channel_id=1, source_target_pairs={{34,66},{35,67},{36,68},{37,69},{38,70},{39,71},{42,74},{43,75},{4... | collective-permute-start | bytes 12296 | tf_op jit(solution)/shard_map/ppermute | solution.py:492
  19.5 5.9 %all-gather.1.near = f32[464,128]{1,0:T(8,128)S(1)} all-gather(f32[232,128]{1,0:T(8,128)S(1)} %get-tuple-element.44), channel_id=3, replica_groups={{0,32},{1,33},{2,34},{3,35},{4,36},{5,37},{6,38},{7,39},{8,40},{9,41},{..., dimensions={0}, use_global_device_ids=true | all-gather | bytes 356352 | tf_op jit(solution)/shard_map/all_gather | solution.py:496
  25.4 0.9 %shard_map.67 = (f32[768,128]{1,0:T(8,128)S(1)}, f32[768,128]{1,0:T(8,128)S(1)}, f32[24,128]{1,0:T(8,128)S(1)}, f32[384,128]{1,0:T(8,128)S(1)}, f32[640,128]{1,0:T(8,128)S(1)}) custom-call(f32[768,128]{1,0:T(8,128)S(1)} %get-tuple-element.31.t.tracer, ...), custom_call_target="tpu_custom_call", output_to_operand_aliasing={{0}: (7, {}), {1}: (8, {}), {2}: (9, {}), {3}: (10, {}), {4... | custom-call | tf_op jit(solution)/shard_map/pallas_call | solution.py:467
  26.3 2.3 %collective-permute-done.2.corner = f32[8,128]{1,0:T(8,128)S(1)} collective-permute-done((f32[8,128]{1,0:T(8,128)S(1)}, f32[8,128]{1,0:T(8,128)S(1)}, u32[]{:S(2)}, u32[]{:S(2)}) %collective-permute-start.2) | collective-permute-done | bytes 4128 | tf_op jit(solution)/shard_map/ppermute | solution.py:492
  28.6 0.0 collective-permute-done.early
  28.6 0.0 collective-permute-done.3.far
  28.6 1.3 %shard_map.68 = (f32[768,128]{1,0:T(8,128)}, f32[768,128]{1,0:T(8,128)S(1)}, f32[768,128]{1,0:T(8,128)S(1)}) custom-call(f32[240,128]{1,0:T(8,128)S(1)} %collective-permute-done.early, f32[8,128]{1,0:T(8,128)S(1)} %collective-permute-done.2.corner, f32[232,128]{1,0:T(8,128)S(1)} %collective-permute-done.3.far, ...), custom_call_target="tpu_custom_call", output_to_operand_aliasing={{1}: (8, {}), {2}: (9, {})} | custom-call | tf_op jit(solution)/shard_map/pallas_call | solution.py:467
Async XLA Ops:
  1.4 14.4 %collective-permute-start.1 = (f32[40,128]{1,0:T(8,128)S(1)}, f32[40,128]{1,0:T(8,128)S(1)}, u32[]{:S(2)}, u32[]{:S(2)}) collective-permute-start(f32[40,128]{1,0:T(8,128)S(1)} %get-tuple-element.35.own), channel_id=1, source_target_pairs={{1,2},{3,4},{5,6},{7,8},{9,10},{11,12},{13,14},{15,16},{17,18},{19... | collective-permute-start | bytes 61448 | tf_op jit(solution)/shard_map/ppermute | solution.py:492
  3.5 25.1 %collective-permute-start = (f32[240,128]{1,0:T(8,128)S(1)}, f32[240,128]{1,0:T(8,128)S(1)}, u32[]{:S(2)}, u32[]{:S(2)}) collective-permute-start(f32[240,128]{1,0:T(8,128)S(1)} %get-tuple-element.36), channel_id=1, source_target_pairs={{34,66},{35,67},{36,68},{37,69},{38,70},{39,71},{42,74},{43,75},{4... | collective-permute-start | bytes 368648 | tf_op jit(solution)/shard_map/ppermute | solution.py:492
  16.0 12.6 %collective-permute-start.3 = (f32[232,128]{1,0:T(8,128)S(1)}, f32[232,128]{1,0:T(8,128)S(1)}, u32[]{:S(2)}, u32[]{:S(2)}) collective-permute-start(f32[232,128]{1,0:T(8,128)S(1)} %get-tuple-element.43), channel_id=1, source_target_pairs={{32,64},{33,65},{40,72},{41,73},{48,80},{49,81},{56,88},{57,89},{9... | collective-permute-start | bytes 356360 | tf_op jit(solution)/shard_map/ppermute | solution.py:492
  16.7 11.9 %collective-permute-start.2 = (f32[8,128]{1,0:T(8,128)S(1)}, f32[8,128]{1,0:T(8,128)S(1)}, u32[]{:S(2)}, u32[]{:S(2)}) collective-permute-start(f32[8,128]{1,0:T(8,128)S(1)} %get-tuple-element.42), channel_id=1, source_target_pairs={{34,66},{35,67},{36,68},{37,69},{38,70},{39,71},{42,74},{43,75},{4... | collective-permute-start | bytes 12296 | tf_op jit(solution)/shard_map/ppermute | solution.py:492

commit v6 on v5

--- a/solution.py
+++ b/solution.py
@@ -313,25 +313,67 @@
 
 
 def ahead_of_partner():
-    lat, count = lax.axis_index("lat"), lax.axis_size("lat")
-    place = lax.rem(lat, 4)
-    waits = ((place >= 2) & (lat < count // 2)) | ((place < 2) & (lat >= count // 2))
-    return waits & (lax.rem(lax.axis_index("lon"), 8) < 2)
-
-
-def column_kernel(tracer, east, north, mask, mix, bottom, aux, *refs):
+    lat = lax.axis_index("lat")
+    return (lat >= 2) & (lat < 4) & (lax.axis_index("lon") < 2)
+
+
+class Edge:
+    def __init__(self, is_north, tracer, north, mask, other):
+        self.is_north, self.tracer, self.other = is_north, tracer, other
+        self.row = jnp.where(is_north, ROWS - 1, 0)
+        first, second = face(
+            0.5 * (edge(north, 0, K, self.row) + other(ROW_V, K)),
+            edge(mask, 0, K, self.row).astype(jnp.float32) * other(ROW_M, K),
+        )
+        self.mine = jnp.where(is_north, -first, second)
+        self.theirs = jnp.where(is_north, -second, first)
+
+    def place(self, f):
+        return pl.ds(f * K * ROWS + self.row, K, stride=ROWS)
+
+    def fluxes(self, f, flux_row, before):
+        line = jnp.broadcast_to(flux_row, (ROWS, COLS))
+        sign = edge_sign()
+        added = [
+            sign * pltpu.roll(line, COLS - 1 - (lane_base(f, k) + 1), 1, stride=4, stride_axis=0) for k in (0, ROWS)
+        ]
+        beyond = self.other(ROW_P + f * K, K) + jnp.concatenate(added, axis=0)
+        g = self.mine * edge(self.tracer, f * K, K, self.row) + self.theirs * self.other(ROW_T + f * K, K)
+        s = before + g
+        return g, s, self.mine * s + self.theirs * (beyond - g)
+
+
+def column_kernel(tracer, east, north, mask, mix, bottom, aux, near, *refs):
     count = len(COLUMN_ROWS)
 
     @pl.when(jnp.logical_not(ahead_of_partner()))
     def _():
         columns(tracer, east, north, mask, mix, bottom, aux, *refs[count:])
 
+    full, sums, _, _, coeff = refs[count : 2 * count]
+    lat_odd = lax.rem(lax.axis_index("lat"), 2)
+    offset = pl.multiple_of((1 - lat_odd) * PAY_ROWS, ROWS)
+    side = Edge(lat_odd == 0, tracer, north, mask, lambda start, size: near[rows_at(offset + start, size), :])
+    for f in range(NT):
+        place = side.place(f)
+        g, s, h = side.fluxes(f, near[pl.ds(offset + ROW_C + AUX_F + f // 2, 1), :], full[place, :])
+        full[place, :] = s
+        sums[place, :] = sums[place, :] + (g + h)
+
+    def level(k):
+        faces = [tile(coeff, i * K + k) for i in range(5)]
+        for f in range(NT):
+            index = f * K + k
+            put(sums, index, tile(sums, index) + inner_sum(tile(full, index), faces))
+
+    repeat(K, level, unroll=8)
+
 
 def last_kernel(
-    early, corner, far, near, tracer, north, mask, coeff, full_in, sums_in, packs, solve, own, aux,
-    result, full, sums, spread, out, line_1, line_2, line_3, line_4, sems,
+    early, corner, far, near, tracer, north, mask, coeff, full, sums_in, packs, solve, own, aux,
+    result, sums, spread, out, line_1, line_2, line_3, line_4, line_5, sems,
 ):
-    del full_in, sums_in
+    del sums_in
     lines_refs = (line_1, line_2, line_3, line_4)
     lat_odd = lax.rem(lax.axis_index("lat"), 2)
     odd = lat_odd == 1
@@ -343,14 +385,13 @@
 
     is_early = early_far(lax.axis_index("lat"), lax.axis_index("lon"), lax.axis_size("lat"), lax.axis_size("lon"))
 
-    def both(start, size, step=0):
-        place = rows_at(start + step, size)
-        first = early[place, :] if start < ROW_C else corner[...]
-        a = jnp.where(is_early, first, far[place, :])
-        b = near[rows_at(offset + start + step, size), :]
-        return jnp.where(odd, a, b), jnp.where(odd, b, a)
-
-    c_n, c_s = both(ROW_C, ROWS)
+    def beyond(start, size):
+        return jnp.where(is_early, early[start : start + size, :], far[start : start + size, :])
+
+    c_far = jnp.where(is_early, corner[...], far[ROW_C:, :])
+    c_near = near[rows_at(offset + ROW_C, ROWS), :]
+    c_n, c_s = jnp.where(odd, c_far, c_near), jnp.where(odd, c_near, c_far)
+    line_5[...] = c_far
 
     def inner_columns(c):
         return jnp.where(at_east, roll(c, 1, 1), roll(c, -1, 1))
@@ -388,42 +429,16 @@
 
     spread_out(spread, flux_of, sign)
 
-    v_n, v_s = both(ROW_V, K)
-    m_n, m_s = both(ROW_M, K)
-    an, bn = face(
-        0.5 * (edge(north, 0, K, ROWS - 1) + v_n), edge(mask, 0, K, ROWS - 1).astype(jnp.float32) * m_n
-    )
-    as_, bs = face(0.5 * (v_s + edge(north, 0, K, 0)), m_s * edge(mask, 0, K, 0).astype(jnp.float32))
-
-    def edge_flux(ref, p, f):
-        line = jnp.broadcast_to(ref[pl.ds(AUX_F + p, 1), :], (ROWS, COLS))
-        return jnp.concatenate(
-            [
-                sign * pltpu.roll(line, COLS - 1 - (lane_base(f, k) + 1), 1, stride=4, stride_axis=0)
-                for k in (0, ROWS)
-            ],
-            axis=0,
-        )
-
-    def edge_pair(p):
-        for half in (0, 1):
-            f = 2 * p + half
-            t_n, t_s = both(ROW_T, K, f * K)
-            p_n, p_s = both(ROW_P, K, f * K)
-            p_n = p_n + edge_flux(lines_refs[0], p, half)
-            p_s = p_s + edge_flux(lines_refs[1], p, half)
-            g_n = an * edge(tracer, f * K, K, ROWS - 1) + bn * t_n
-            g_s = as_ * t_s + bs * edge(tracer, f * K, K, 0)
-            low = pl.ds(f * K * ROWS, K, stride=ROWS)
-            high = pl.ds(f * K * ROWS + ROWS - 1, K, stride=ROWS)
-            s_low, s_high = full[low, :] + g_s, full[high, :] - g_n
-            full[low, :] = s_low
-            full[high, :] = s_high
-            sums[low, :] = sums[low, :] + (g_s + (as_ * (p_s - g_s) + bs * s_low))
-            sums[high, :] = sums[high, :] - (g_n + (an * s_high + bn * (p_n + g_n)))
-
-    for p in range(TPACKS):
-        edge_pair(p)
+    side = Edge(odd, tracer, north, mask, beyond)
+    inward = jnp.where(odd, ROWS - 2, 1)
+    middle, west, east = (edge(coeff, i * K, K, side.row) for i in range(3))
+    beside = jnp.where(odd, edge(coeff, 4 * K, K, ROWS - 2), edge(coeff, 3 * K, K, 1))
+    for f in range(NT):
+        place = side.place(f)
+        g, _, h = side.fluxes(f, line_5[AUX_F + f // 2 : AUX_F + f // 2 + 1, :], full[place, :])
+        sums[place, :] = sums[place, :] + (g + h + (middle * g + (west * roll(g, 1, 1) + east * roll(g, -1, 1))))
+        place = pl.ds(f * K * ROWS + inward, K, stride=ROWS)
+        sums[place, :] = sums[place, :] + beside * g
 
     def copy_of(f):
         place = rows_at(f * K * ROWS, K * ROWS)
@@ -433,9 +448,7 @@
         value = None
         for k in range(K):
             index = f * K + k
-            faces = [tile(coeff, i * K + k) for i in range(5)]
-            rhs = (tile(sums, index) + tile(spread, index)) + inner_sum(tile(full, index), faces)
-            value_new = rhs * tile(solve, k)
+            value_new = (tile(sums, index) + tile(spread, index)) * tile(solve, k)
             if k:
                 value_new = value_new + tile(solve, K + k) * value
             value = value_new
@@ -454,7 +467,7 @@
 
 def early_far(lat, lon, lat_count, lon_count):
     mirrored = lon_count - 1 - lon
-    return (lon % 8 >= 2) & ((lat < lat_count - 1) | (mirrored % 8 >= 2))
+    return (lon % 8 >= 4) & ((lat < lat_count - 1) | (mirrored % 8 >= 4))
 
 
 def call(kernel, outs, scratch_rows, *operands, hbm=False, hbm_out=0, scratch=(), alias=None):
@@ -535,15 +548,15 @@
         column_kernel,
         COLUMN_ROWS,
         [TILES * ROWS],
-        t, u, v, m, vertical, depth, aux, *ready,
-        alias={7 + i: i for i in range(len(COLUMN_ROWS))},
-    )
-    out, _, _ = call(
+        t, u, v, m, vertical, depth, aux, near_rows, *ready,
+        alias={8 + i: i for i in range(len(COLUMN_ROWS))},
+    )
+    out, _ = call(
         last_kernel,
-        [TILES * ROWS] * 3,
-        [TILES * ROWS, TILES * ROWS] + [ROWS] * 4,
+        [TILES * ROWS] * 2,
+        [TILES * ROWS, TILES * ROWS] + [ROWS] * 5,
         early_rows, corner_rows, far_rows, near_rows, t, v, m, coeff, full, both, packs, solve, own, aux,
-        alias={8: 1, 9: 2},
+        alias={9: 1},
         scratch=[pltpu.SemaphoreType.DMA((NT,))],
         hbm_out=1,
     )

time: 30.1 us -> 29.9 us (level)
  the two profiles are of different devices: /device:TPU:94 before, /device:TPU:6 now
where the time goes in v6:
time: 29.9 us; the launch traced here: 29.7 us
  starting transfers between devices  17.9 us (60%)
  blocking collectives  7.54 us (25%)
  Pallas kernels  4.17 us (14%)
    ppermute x4, starting transfers between devices, swapped(): lax.ppermute(x, AXES, [(a, b) for a, b in groups] + [(b, a) for a, b in g...  17.9 us
    all_gather x2, blocking collectives, gathered(): both = lax.all_gather(x, AXES, axis_index_groups=[list(g) for g in groups])  7.54 us
    pallas_call x5, Pallas kernels, call(): pl.pallas_call(kernel, out_shape=shapes, in_specs=[in_hbm if hbm else vme...  4.17 us
  transfers between devices with their start and end apart: 4, of which 0 were waited for; matrix products, arithmetic and copies ran while one was open for 0% of the time, Pallas kernels for 6%

profile of v6, /device:TPU:6, one launch (start us, length us, event | category | flops | bytes accessed | tf_op | source)
XLA Modules:
  0.0 29.7 jit_solution(7508090475548829918)
XLA Ops:
  0.0 1.4 %shard_map.64 = (f32[40,128]{1,0:T(8,128)S(1)}, f32[768,128]{1,0:T(8,128)S(1)}, f32[128,128]{1,0:T(8,128)S(1)}, f32[128,128]{1,0:T(8,128)S(1)}, s32[128,128]{1,0...) custom-call(f32[768,128]{1,0:T(8,128)} %bitcast.6, f32[128,128]{1,0:T(8,128)} %bitcast.7, ...), custom_call_target="tpu_custom_call" | custom-call | tf_op jit(solution)/shard_map/pallas_call | solution.py:480
  1.4 8.4 %collective-permute-start.1 = (f32[40,128]{1,0:T(8,128)S(1)}, f32[40,128]{1,0:T(8,128)S(1)}, u32[]{:S(2)}, u32[]{:S(2)}) collective-permute-start(f32[40,128]{1,0:T(8,128)S(1)} %get-tuple-element.35.own), channel_id=1, source_target_pairs={{1,2},{3,4},{5,6},{7,8},{9,10},{11,12},{13,14},{15,16},{17,18},{19... | collective-permute-start | bytes 61448 | tf_op jit(solution)/shard_map/ppermute | solution.py:505
  9.8 0.2 shard_map.65
  10.0 0.7 %collective-permute-start = (f32[240,128]{1,0:T(8,128)S(1)}, f32[240,128]{1,0:T(8,128)S(1)}, u32[]{:S(2)}, u32[]{:S(2)}) collective-permute-start(f32[240,128]{1,0:T(8,128)S(1)} %get-tuple-element.36), channel_id=1, source_target_pairs={{36,68},{37,69},{38,70},{39,71},{44,76},{45,77},{46,78},{47,79},{5... | collective-permute-start | bytes 368648 | tf_op jit(solution)/shard_map/ppermute | solution.py:505
  10.7 1.8 %all-gather.near = f32[80,128]{1,0:T(8,128)S(1)} all-gather(f32[40,128]{1,0:T(8,128)S(1)} %get-tuple-element.37), channel_id=2, replica_groups={{0,1},{2,3},{4,5},{6,7},{8,9},{10,11},{12,13},{14,15},{16,17},{18,19},{..., dimensions={0}, use_global_device_ids=true | all-gather | bytes 61440 | tf_op jit(solution)/shard_map/all_gather | solution.py:509
  12.5 0.0 collective-permute-done.1.far
  12.5 1.1 %shard_map.66 = (f32[232,128]{1,0:T(8,128)S(1)}, f32[232,128]{1,0:T(8,128)S(1)}, f32[104,128]{1,0:T(8,128)S(1)}, f32[8,128]{1,0:T(8,128)S(1)}, f32[768,128]{1,0:...) custom-call(f32[40,128]{1,0:T(8,128)S(1)} %get-tuple-element.35.own,, ...), custom_call_target="tpu_custom_call", output_to_operand_aliasing={{0}: (3, {}), {1}: (4, {})} | custom-call | tf_op jit(solution)/shard_map/pallas_call | solution.py:480
  13.6 8.1 %collective-permute-start.3 = (f32[232,128]{1,0:T(8,128)S(1)}, f32[232,128]{1,0:T(8,128)S(1)}, u32[]{:S(2)}, u32[]{:S(2)}) collective-permute-start(f32[232,128]{1,0:T(8,128)S(1)} %get-tuple-element.43), channel_id=1, source_target_pairs={{32,64},{33,65},{34,66},{35,67},{40,72},{41,73},{42,74},{43,75},{4... | collective-permute-start | bytes 356360 | tf_op jit(solution)/shard_map/ppermute | solution.py:505
  21.8 0.7 %collective-permute-start.2 = (f32[8,128]{1,0:T(8,128)S(1)}, f32[8,128]{1,0:T(8,128)S(1)}, u32[]{:S(2)}, u32[]{:S(2)}) collective-permute-start(f32[8,128]{1,0:T(8,128)S(1)} %get-tuple-element.42), channel_id=1, source_target_pairs={{36,68},{37,69},{38,70},{39,71},{44,76},{45,77},{46,78},{47,79},{5... | collective-permute-start | bytes 12296 | tf_op jit(solution)/shard_map/ppermute | solution.py:505
  22.4 5.7 %all-gather.1.near = f32[464,128]{1,0:T(8,128)S(1)} all-gather(f32[232,128]{1,0:T(8,128)S(1)} %get-tuple-element.44), channel_id=3, replica_groups={{0,32},{1,33},{2,34},{3,35},{4,36},{5,37},{6,38},{7,39},{8,40},{9,41},{..., dimensions={0}, use_global_device_ids=true | all-gather | bytes 356352 | tf_op jit(solution)/shard_map/all_gather | solution.py:509
  28.1 0.4 %shard_map.67 = (f32[768,128]{1,0:T(8,128)S(1)}, f32[768,128]{1,0:T(8,128)S(1)}, f32[24,128]{1,0:T(8,128)S(1)}, f32[384,128]{1,0:T(8,128)S(1)}, f32[640,128]{1,0:T(8,128)S(1)}) custom-call(f32[768,128]{1,0:T(8,128)S(1)} %get-tuple-element.31.t.tracer, ...), custom_call_target="tpu_custom_call", output_to_operand_aliasing={{0}: (8, {}), {1}: (9, {}), {2}: (10, {}), {3}: (11, {}), {... | custom-call | tf_op jit(solution)/shard_map/pallas_call | solution.py:480
  28.6 0.0 collective-permute-done.2.corner
  28.6 0.0 collective-permute-done.early
  28.6 0.0 collective-permute-done.3.far
  28.6 1.1 %shard_map.68 = (f32[768,128]{1,0:T(8,128)}, f32[768,128]{1,0:T(8,128)S(1)}) custom-call(f32[240,128]{1,0:T(8,128)S(1)} %collective-permute-done.early, f32[8,128]{1,0:T(8,128)S(1)} %collective-permute-done.2.corner, f32[232,128]{1,0:T(8,128)S(1)} %collective-permute-done.3.far, f32[464,128]{1,0:T(8,128)S(1)} %all-gather.1.near, ...), custom_call_target="tpu_custom_call", output_to_operand_aliasing={{1}: (9, {})} | custom-call | tf_op jit(solution)/shard_map/pallas_call | solution.py:480
Async XLA Ops:
  1.4 11.1 %collective-permute-start.1 = (f32[40,128]{1,0:T(8,128)S(1)}, f32[40,128]{1,0:T(8,128)S(1)}, u32[]{:S(2)}, u32[]{:S(2)}) collective-permute-start(f32[40,128]{1,0:T(8,128)S(1)} %get-tuple-element.35.own), channel_id=1, source_target_pairs={{1,2},{3,4},{5,6},{7,8},{9,10},{11,12},{13,14},{15,16},{17,18},{19... | collective-permute-start | bytes 61448 | tf_op jit(solution)/shard_map/ppermute | solution.py:505
  10.0 18.6 %collective-permute-start = (f32[240,128]{1,0:T(8,128)S(1)}, f32[240,128]{1,0:T(8,128)S(1)}, u32[]{:S(2)}, u32[]{:S(2)}) collective-permute-start(f32[240,128]{1,0:T(8,128)S(1)} %get-tuple-element.36), channel_id=1, source_target_pairs={{36,68},{37,69},{38,70},{39,71},{44,76},{45,77},{46,78},{47,79},{5... | collective-permute-start | bytes 368648 | tf_op jit(solution)/shard_map/ppermute | solution.py:505
  13.6 15.0 %collective-permute-start.3 = (f32[232,128]{1,0:T(8,128)S(1)}, f32[232,128]{1,0:T(8,128)S(1)}, u32[]{:S(2)}, u32[]{:S(2)}) collective-permute-start(f32[232,128]{1,0:T(8,128)S(1)} %get-tuple-element.43), channel_id=1, source_target_pairs={{32,64},{33,65},{34,66},{35,67},{40,72},{41,73},{42,74},{43,75},{4... | collective-permute-start | bytes 356360 | tf_op jit(solution)/shard_map/ppermute | solution.py:505
  21.8 6.8 %collective-permute-start.2 = (f32[8,128]{1,0:T(8,128)S(1)}, f32[8,128]{1,0:T(8,128)S(1)}, u32[]{:S(2)}, u32[]{:S(2)}) collective-permute-start(f32[8,128]{1,0:T(8,128)S(1)} %get-tuple-element.42), channel_id=1, source_target_pairs={{36,68},{37,69},{38,70},{39,71},{44,76},{45,77},{46,78},{47,79},{5... | collective-permute-start | bytes 12296 | tf_op jit(solution)/shard_map/ppermute | solution.py:505

commit v7 on v6

--- a/solution.py
+++ b/solution.py
@@ -444,23 +444,26 @@
         place = rows_at(f * K * ROWS, K * ROWS)
         return pltpu.make_async_copy(out.at[place, :], result.at[place, :], sems.at[f])
 
-    def tracer_columns(f):
-        value = None
+    def tracer_columns(fields):
+        values = {}
         for k in range(K):
-            index = f * K + k
-            value_new = (tile(sums, index) + tile(spread, index)) * tile(solve, k)
-            if k:
-                value_new = value_new + tile(solve, K + k) * value
-            value = value_new
-            put(out, index, value)
+            for f in fields:
+                index = f * K + k
+                value = (tile(sums, index) + tile(spread, index)) * tile(solve, k)
+                if k:
+                    value = value + tile(solve, K + k) * values[f]
+                values[f] = value
+                put(out, index, value)
         for k in range(K - 2, -1, -1):
-            index = f * K + k
-            value = tile(out, index) - tile(solve, 2 * K + k) * value
-            put(out, index, value)
-        copy_of(f).start()
-
-    for f in range(NT):
-        tracer_columns(f)
+            for f in fields:
+                index = f * K + k
+                values[f] = tile(out, index) - tile(solve, 2 * K + k) * values[f]
+                put(out, index, values[f])
+        for f in fields:
+            copy_of(f).start()
+
+    for start in range(0, NT, 3):
+        tracer_columns(range(start, start + 3))
     for f in range(NT):
         copy_of(f).wait()
 

time: 29.9 us -> 29.9 us (level)
  no operation moved by 1% of the time
where the time goes in v7:
time: 29.9 us; the launch traced here: 29.7 us
  starting transfers between devices  17.9 us (60%)
  blocking collectives  7.54 us (25%)
  Pallas kernels  4.15 us (14%)
    ppermute x4, starting transfers between devices, swapped(): lax.ppermute(x, AXES, [(a, b) for a, b in groups] + [(b, a) for a, b in g...  17.9 us
    all_gather x2, blocking collectives, gathered(): both = lax.all_gather(x, AXES, axis_index_groups=[list(g) for g in groups])  7.54 us
    pallas_call x5, Pallas kernels, call(): pl.pallas_call(kernel, out_shape=shapes, in_specs=[in_hbm if hbm else vme...  4.15 us
  transfers between devices with their start and end apart: 4, of which 0 were waited for; matrix products, arithmetic and copies ran while one was open for 0% of the time, Pallas kernels for 6%

profile of v7, /device:TPU:6, one launch (start us, length us, event | category | flops | bytes accessed | tf_op | source)
XLA Modules:
  0.0 29.7 jit_solution(718180204696028408)
XLA Ops:
  0.0 1.4 %shard_map.64 = (f32[40,128]{1,0:T(8,128)S(1)}, f32[768,128]{1,0:T(8,128)S(1)}, f32[128,128]{1,0:T(8,128)S(1)}, f32[128,128]{1,0:T(8,128)S(1)}, s32[128,128]{1,0...) custom-call(f32[768,128]{1,0:T(8,128)} %bitcast.6, f32[128,128]{1,0:T(8,128)} %bitcast.7, ...), custom_call_target="tpu_custom_call" | custom-call | tf_op jit(solution)/shard_map/pallas_call | solution.py:483
  1.4 8.4 %collective-permute-start.1 = (f32[40,128]{1,0:T(8,128)S(1)}, f32[40,128]{1,0:T(8,128)S(1)}, u32[]{:S(2)}, u32[]{:S(2)}) collective-permute-start(f32[40,128]{1,0:T(8,128)S(1)} %get-tuple-element.35.own), channel_id=1, source_target_pairs={{1,2},{3,4},{5,6},{7,8},{9,10},{11,12},{13,14},{15,16},{17,18},{19... | collective-permute-start | bytes 61448 | tf_op jit(solution)/shard_map/ppermute | solution.py:508
  9.8 0.2 shard_map.65
  10.0 0.7 %collective-permute-start = (f32[240,128]{1,0:T(8,128)S(1)}, f32[240,128]{1,0:T(8,128)S(1)}, u32[]{:S(2)}, u32[]{:S(2)}) collective-permute-start(f32[240,128]{1,0:T(8,128)S(1)} %get-tuple-element.36), channel_id=1, source_target_pairs={{36,68},{37,69},{38,70},{39,71},{44,76},{45,77},{46,78},{47,79},{5... | collective-permute-start | bytes 368648 | tf_op jit(solution)/shard_map/ppermute | solution.py:508
  10.7 1.8 %all-gather.near = f32[80,128]{1,0:T(8,128)S(1)} all-gather(f32[40,128]{1,0:T(8,128)S(1)} %get-tuple-element.37), channel_id=2, replica_groups={{0,1},{2,3},{4,5},{6,7},{8,9},{10,11},{12,13},{14,15},{16,17},{18,19},{..., dimensions={0}, use_global_device_ids=true | all-gather | bytes 61440 | tf_op jit(solution)/shard_map/all_gather | solution.py:512
  12.5 0.0 collective-permute-done.1.far
  12.5 1.1 %shard_map.66 = (f32[232,128]{1,0:T(8,128)S(1)}, f32[232,128]{1,0:T(8,128)S(1)}, f32[104,128]{1,0:T(8,128)S(1)}, f32[8,128]{1,0:T(8,128)S(1)}, f32[768,128]{1,0:...) custom-call(f32[40,128]{1,0:T(8,128)S(1)} %get-tuple-element.35.own,, ...), custom_call_target="tpu_custom_call", output_to_operand_aliasing={{0}: (3, {}), {1}: (4, {})} | custom-call | tf_op jit(solution)/shard_map/pallas_call | solution.py:483
  13.6 8.1 %collective-permute-start.3 = (f32[232,128]{1,0:T(8,128)S(1)}, f32[232,128]{1,0:T(8,128)S(1)}, u32[]{:S(2)}, u32[]{:S(2)}) collective-permute-start(f32[232,128]{1,0:T(8,128)S(1)} %get-tuple-element.43), channel_id=1, source_target_pairs={{32,64},{33,65},{34,66},{35,67},{40,72},{41,73},{42,74},{43,75},{4... | collective-permute-start | bytes 356360 | tf_op jit(solution)/shard_map/ppermute | solution.py:508
  21.8 0.7 %collective-permute-start.2 = (f32[8,128]{1,0:T(8,128)S(1)}, f32[8,128]{1,0:T(8,128)S(1)}, u32[]{:S(2)}, u32[]{:S(2)}) collective-permute-start(f32[8,128]{1,0:T(8,128)S(1)} %get-tuple-element.42), channel_id=1, source_target_pairs={{36,68},{37,69},{38,70},{39,71},{44,76},{45,77},{46,78},{47,79},{5... | collective-permute-start | bytes 12296 | tf_op jit(solution)/shard_map/ppermute | solution.py:508
  22.4 5.7 %all-gather.1.near = f32[464,128]{1,0:T(8,128)S(1)} all-gather(f32[232,128]{1,0:T(8,128)S(1)} %get-tuple-element.44), channel_id=3, replica_groups={{0,32},{1,33},{2,34},{3,35},{4,36},{5,37},{6,38},{7,39},{8,40},{9,41},{..., dimensions={0}, use_global_device_ids=true | all-gather | bytes 356352 | tf_op jit(solution)/shard_map/all_gather | solution.py:512
  28.1 0.4 %shard_map.67 = (f32[768,128]{1,0:T(8,128)S(1)}, f32[768,128]{1,0:T(8,128)S(1)}, f32[24,128]{1,0:T(8,128)S(1)}, f32[384,128]{1,0:T(8,128)S(1)}, f32[640,128]{1,0:T(8,128)S(1)}) custom-call(f32[768,128]{1,0:T(8,128)S(1)} %get-tuple-element.31.t.tracer, ...), custom_call_target="tpu_custom_call", output_to_operand_aliasing={{0}: (8, {}), {1}: (9, {}), {2}: (10, {}), {3}: (11, {}), {... | custom-call | tf_op jit(solution)/shard_map/pallas_call | solution.py:483
  28.6 0.0 collective-permute-done.2.corner
  28.6 0.0 collective-permute-done.early
  28.6 0.0 collective-permute-done.3.far
  28.6 1.1 %shard_map.68 = (f32[768,128]{1,0:T(8,128)}, f32[768,128]{1,0:T(8,128)S(1)}) custom-call(f32[240,128]{1,0:T(8,128)S(1)} %collective-permute-done.early, f32[8,128]{1,0:T(8,128)S(1)} %collective-permute-done.2.corner, f32[232,128]{1,0:T(8,128)S(1)} %collective-permute-done.3.far, f32[464,128]{1,0:T(8,128)S(1)} %all-gather.1.near, ...), custom_call_target="tpu_custom_call", output_to_operand_aliasing={{1}: (9, {})} | custom-call | tf_op jit(solution)/shard_map/pallas_call | solution.py:483
Async XLA Ops:
  1.4 11.1 %collective-permute-start.1 = (f32[40,128]{1,0:T(8,128)S(1)}, f32[40,128]{1,0:T(8,128)S(1)}, u32[]{:S(2)}, u32[]{:S(2)}) collective-permute-start(f32[40,128]{1,0:T(8,128)S(1)} %get-tuple-element.35.own), channel_id=1, source_target_pairs={{1,2},{3,4},{5,6},{7,8},{9,10},{11,12},{13,14},{15,16},{17,18},{19... | collective-permute-start | bytes 61448 | tf_op jit(solution)/shard_map/ppermute | solution.py:508
  10.0 18.6 %collective-permute-start = (f32[240,128]{1,0:T(8,128)S(1)}, f32[240,128]{1,0:T(8,128)S(1)}, u32[]{:S(2)}, u32[]{:S(2)}) collective-permute-start(f32[240,128]{1,0:T(8,128)S(1)} %get-tuple-element.36), channel_id=1, source_target_pairs={{36,68},{37,69},{38,70},{39,71},{44,76},{45,77},{46,78},{47,79},{5... | collective-permute-start | bytes 368648 | tf_op jit(solution)/shard_map/ppermute | solution.py:508
  13.6 15.0 %collective-permute-start.3 = (f32[232,128]{1,0:T(8,128)S(1)}, f32[232,128]{1,0:T(8,128)S(1)}, u32[]{:S(2)}, u32[]{:S(2)}) collective-permute-start(f32[232,128]{1,0:T(8,128)S(1)} %get-tuple-element.43), channel_id=1, source_target_pairs={{32,64},{33,65},{34,66},{35,67},{40,72},{41,73},{42,74},{43,75},{4... | collective-permute-start | bytes 356360 | tf_op jit(solution)/shard_map/ppermute | solution.py:508
  21.8 6.8 %collective-permute-start.2 = (f32[8,128]{1,0:T(8,128)S(1)}, f32[8,128]{1,0:T(8,128)S(1)}, u32[]{:S(2)}, u32[]{:S(2)}) collective-permute-start(f32[8,128]{1,0:T(8,128)S(1)} %get-tuple-element.42), channel_id=1, source_target_pairs={{36,68},{37,69},{38,70},{39,71},{44,76},{45,77},{46,78},{47,79},{5... | collective-permute-start | bytes 12296 | tf_op jit(solution)/shard_map/ppermute | solution.py:508

commit v8 on v7

--- a/solution.py
+++ b/solution.py
@@ -470,7 +470,7 @@
 
 def early_far(lat, lon, lat_count, lon_count):
     mirrored = lon_count - 1 - lon
-    return (lon % 8 >= 4) & ((lat < lat_count - 1) | (mirrored % 8 >= 4))
+    return (lon % 4 >= 2) & ((lat < lat_count - 1) | (mirrored % 4 >= 2))
 
 
 def call(kernel, outs, scratch_rows, *operands, hbm=False, hbm_out=0, scratch=(), alias=None):

time: 29.9 us -> 29.9 us (level)
  no operation moved by 1% of the time
where the time goes in v8:
time: 29.9 us; the launch traced here: 29.7 us
  starting transfers between devices  17.9 us (60%)
  blocking collectives  7.54 us (25%)
  Pallas kernels  4.15 us (14%)
    ppermute x4, starting transfers between devices, swapped(): lax.ppermute(x, AXES, [(a, b) for a, b in groups] + [(b, a) for a, b in g...  17.9 us
    all_gather x2, blocking collectives, gathered(): both = lax.all_gather(x, AXES, axis_index_groups=[list(g) for g in groups])  7.54 us
    pallas_call x5, Pallas kernels, call(): pl.pallas_call(kernel, out_shape=shapes, in_specs=[in_hbm if hbm else vme...  4.15 us
  transfers between devices with their start and end apart: 4, of which 0 were waited for; matrix products, arithmetic and copies ran while one was open for 0% of the time, Pallas kernels for 6%

profile of v8, /device:TPU:6, one launch (start us, length us, event | category | flops | bytes accessed | tf_op | source)
XLA Modules:
  0.0 29.7 jit_solution(6360658227549901928)
XLA Ops:
  0.0 1.4 %shard_map.64 = (f32[40,128]{1,0:T(8,128)S(1)}, f32[768,128]{1,0:T(8,128)S(1)}, f32[128,128]{1,0:T(8,128)S(1)}, f32[128,128]{1,0:T(8,128)S(1)}, s32[128,128]{1,0...) custom-call(f32[768,128]{1,0:T(8,128)} %bitcast.6, f32[128,128]{1,0:T(8,128)} %bitcast.7, ...), custom_call_target="tpu_custom_call" | custom-call | tf_op jit(solution)/shard_map/pallas_call | solution.py:483
  1.4 8.4 %collective-permute-start.1 = (f32[40,128]{1,0:T(8,128)S(1)}, f32[40,128]{1,0:T(8,128)S(1)}, u32[]{:S(2)}, u32[]{:S(2)}) collective-permute-start(f32[40,128]{1,0:T(8,128)S(1)} %get-tuple-element.35.own), channel_id=1, source_target_pairs={{1,2},{3,4},{5,6},{7,8},{9,10},{11,12},{13,14},{15,16},{17,18},{19... | collective-permute-start | bytes 61448 | tf_op jit(solution)/shard_map/ppermute | solution.py:508
  9.8 0.2 shard_map.65
  10.0 0.7 %collective-permute-start = (f32[240,128]{1,0:T(8,128)S(1)}, f32[240,128]{1,0:T(8,128)S(1)}, u32[]{:S(2)}, u32[]{:S(2)}) collective-permute-start(f32[240,128]{1,0:T(8,128)S(1)} %get-tuple-element.36), channel_id=1, source_target_pairs={{34,66},{35,67},{38,70},{39,71},{42,74},{43,75},{46,78},{47,79},{5... | collective-permute-start | bytes 368648 | tf_op jit(solution)/shard_map/ppermute | solution.py:508
  10.7 1.8 %all-gather.near = f32[80,128]{1,0:T(8,128)S(1)} all-gather(f32[40,128]{1,0:T(8,128)S(1)} %get-tuple-element.37), channel_id=2, replica_groups={{0,1},{2,3},{4,5},{6,7},{8,9},{10,11},{12,13},{14,15},{16,17},{18,19},{..., dimensions={0}, use_global_device_ids=true | all-gather | bytes 61440 | tf_op jit(solution)/shard_map/all_gather | solution.py:512
  12.5 0.0 collective-permute-done.1.far
  12.5 1.1 %shard_map.66 = (f32[232,128]{1,0:T(8,128)S(1)}, f32[232,128]{1,0:T(8,128)S(1)}, f32[104,128]{1,0:T(8,128)S(1)}, f32[8,128]{1,0:T(8,128)S(1)}, f32[768,128]{1,0:...) custom-call(f32[40,128]{1,0:T(8,128)S(1)} %get-tuple-element.35.own,, ...), custom_call_target="tpu_custom_call", output_to_operand_aliasing={{0}: (3, {}), {1}: (4, {})} | custom-call | tf_op jit(solution)/shard_map/pallas_call | solution.py:483
  13.6 8.1 %collective-permute-start.3 = (f32[232,128]{1,0:T(8,128)S(1)}, f32[232,128]{1,0:T(8,128)S(1)}, u32[]{:S(2)}, u32[]{:S(2)}) collective-permute-start(f32[232,128]{1,0:T(8,128)S(1)} %get-tuple-element.43), channel_id=1, source_target_pairs={{32,64},{33,65},{36,68},{37,69},{40,72},{41,73},{44,76},{45,77},{4... | collective-permute-start | bytes 356360 | tf_op jit(solution)/shard_map/ppermute | solution.py:508
  21.8 0.7 %collective-permute-start.2 = (f32[8,128]{1,0:T(8,128)S(1)}, f32[8,128]{1,0:T(8,128)S(1)}, u32[]{:S(2)}, u32[]{:S(2)}) collective-permute-start(f32[8,128]{1,0:T(8,128)S(1)} %get-tuple-element.42), channel_id=1, source_target_pairs={{34,66},{35,67},{38,70},{39,71},{42,74},{43,75},{46,78},{47,79},{5... | collective-permute-start | bytes 12296 | tf_op jit(solution)/shard_map/ppermute | solution.py:508
  22.4 5.7 %all-gather.1.near = f32[464,128]{1,0:T(8,128)S(1)} all-gather(f32[232,128]{1,0:T(8,128)S(1)} %get-tuple-element.44), channel_id=3, replica_groups={{0,32},{1,33},{2,34},{3,35},{4,36},{5,37},{6,38},{7,39},{8,40},{9,41},{..., dimensions={0}, use_global_device_ids=true | all-gather | bytes 356352 | tf_op jit(solution)/shard_map/all_gather | solution.py:512
  28.1 0.4 %shard_map.67 = (f32[768,128]{1,0:T(8,128)S(1)}, f32[768,128]{1,0:T(8,128)S(1)}, f32[24,128]{1,0:T(8,128)S(1)}, f32[384,128]{1,0:T(8,128)S(1)}, f32[640,128]{1,0:T(8,128)S(1)}) custom-call(f32[768,128]{1,0:T(8,128)S(1)} %get-tuple-element.31.t.tracer, ...), custom_call_target="tpu_custom_call", output_to_operand_aliasing={{0}: (8, {}), {1}: (9, {}), {2}: (10, {}), {3}: (11, {}), {... | custom-call | tf_op jit(solution)/shard_map/pallas_call | solution.py:483
  28.6 0.0 collective-permute-done.2.corner
  28.6 0.0 collective-permute-done.early
  28.6 0.0 collective-permute-done.3.far
  28.6 1.1 %shard_map.68 = (f32[768,128]{1,0:T(8,128)}, f32[768,128]{1,0:T(8,128)S(1)}) custom-call(f32[240,128]{1,0:T(8,128)S(1)} %collective-permute-done.early, f32[8,128]{1,0:T(8,128)S(1)} %collective-permute-done.2.corner, f32[232,128]{1,0:T(8,128)S(1)} %collective-permute-done.3.far, f32[464,128]{1,0:T(8,128)S(1)} %all-gather.1.near, ...), custom_call_target="tpu_custom_call", output_to_operand_aliasing={{1}: (9, {})} | custom-call | tf_op jit(solution)/shard_map/pallas_call | solution.py:483
Async XLA Ops:
  1.4 11.1 %collective-permute-start.1 = (f32[40,128]{1,0:T(8,128)S(1)}, f32[40,128]{1,0:T(8,128)S(1)}, u32[]{:S(2)}, u32[]{:S(2)}) collective-permute-start(f32[40,128]{1,0:T(8,128)S(1)} %get-tuple-element.35.own), channel_id=1, source_target_pairs={{1,2},{3,4},{5,6},{7,8},{9,10},{11,12},{13,14},{15,16},{17,18},{19... | collective-permute-start | bytes 61448 | tf_op jit(solution)/shard_map/ppermute | solution.py:508
  10.0 18.6 %collective-permute-start = (f32[240,128]{1,0:T(8,128)S(1)}, f32[240,128]{1,0:T(8,128)S(1)}, u32[]{:S(2)}, u32[]{:S(2)}) collective-permute-start(f32[240,128]{1,0:T(8,128)S(1)} %get-tuple-element.36), channel_id=1, source_target_pairs={{34,66},{35,67},{38,70},{39,71},{42,74},{43,75},{46,78},{47,79},{5... | collective-permute-start | bytes 368648 | tf_op jit(solution)/shard_map/ppermute | solution.py:508
  13.6 15.0 %collective-permute-start.3 = (f32[232,128]{1,0:T(8,128)S(1)}, f32[232,128]{1,0:T(8,128)S(1)}, u32[]{:S(2)}, u32[]{:S(2)}) collective-permute-start(f32[232,128]{1,0:T(8,128)S(1)} %get-tuple-element.43), channel_id=1, source_target_pairs={{32,64},{33,65},{36,68},{37,69},{40,72},{41,73},{44,76},{45,77},{4... | collective-permute-start | bytes 356360 | tf_op jit(solution)/shard_map/ppermute | solution.py:508
  21.8 6.8 %collective-permute-start.2 = (f32[8,128]{1,0:T(8,128)S(1)}, f32[8,128]{1,0:T(8,128)S(1)}, u32[]{:S(2)}, u32[]{:S(2)}) collective-permute-start(f32[8,128]{1,0:T(8,128)S(1)} %get-tuple-element.42), channel_id=1, source_target_pairs={{34,66},{35,67},{38,70},{39,71},{42,74},{43,75},{46,78},{47,79},{5... | collective-permute-start | bytes 12296 | tf_op jit(solution)/shard_map/ppermute | solution.py:508

commit v9 on v7

--- a/solution.py
+++ b/solution.py
@@ -462,8 +462,8 @@
         for f in fields:
             copy_of(f).start()
 
-    for start in range(0, NT, 3):
-        tracer_columns(range(start, start + 3))
+    for start in range(0, NT, 6):
+        tracer_columns(range(start, start + 6))
     for f in range(NT):
         copy_of(f).wait()
 

time: 29.9 us -> 29.9 us (level)
  no operation moved by 1% of the time
where the time goes in v9:
time: 29.9 us; the launch traced here: 29.7 us
  starting transfers between devices  17.9 us (60%)
  blocking collectives  7.54 us (25%)
  Pallas kernels  4.19 us (14%)
    ppermute x4, starting transfers between devices, swapped(): lax.ppermute(x, AXES, [(a, b) for a, b in groups] + [(b, a) for a, b in g...  17.9 us
    all_gather x2, blocking collectives, gathered(): both = lax.all_gather(x, AXES, axis_index_groups=[list(g) for g in groups])  7.54 us
    pallas_call x5, Pallas kernels, call(): pl.pallas_call(kernel, out_shape=shapes, in_specs=[in_hbm if hbm else vme...  4.19 us
  transfers between devices with their start and end apart: 4, of which 0 were waited for; matrix products, arithmetic and copies ran while one was open for 0% of the time, Pallas kernels for 6%

profile of v9, /device:TPU:6, one launch (start us, length us, event | category | flops | bytes accessed | tf_op | source)
XLA Modules:
  0.0 29.7 jit_solution(12787768478395711373)
XLA Ops:
  0.0 1.4 %shard_map.64 = (f32[40,128]{1,0:T(8,128)S(1)}, f32[768,128]{1,0:T(8,128)S(1)}, f32[128,128]{1,0:T(8,128)S(1)}, f32[128,128]{1,0:T(8,128)S(1)}, s32[128,128]{1,0...) custom-call(f32[768,128]{1,0:T(8,128)} %bitcast.6, f32[128,128]{1,0:T(8,128)} %bitcast.7, ...), custom_call_target="tpu_custom_call" | custom-call | tf_op jit(solution)/shard_map/pallas_call | solution.py:483
  1.4 8.4 %collective-permute-start.1 = (f32[40,128]{1,0:T(8,128)S(1)}, f32[40,128]{1,0:T(8,128)S(1)}, u32[]{:S(2)}, u32[]{:S(2)}) collective-permute-start(f32[40,128]{1,0:T(8,128)S(1)} %get-tuple-element.35.own), channel_id=1, source_target_pairs={{1,2},{3,4},{5,6},{7,8},{9,10},{11,12},{13,14},{15,16},{17,18},{19... | collective-permute-start | bytes 61448 | tf_op jit(solution)/shard_map/ppermute | solution.py:508
  9.8 0.2 shard_map.65
  10.0 0.7 %collective-permute-start = (f32[240,128]{1,0:T(8,128)S(1)}, f32[240,128]{1,0:T(8,128)S(1)}, u32[]{:S(2)}, u32[]{:S(2)}) collective-permute-start(f32[240,128]{1,0:T(8,128)S(1)} %get-tuple-element.36), channel_id=1, source_target_pairs={{36,68},{37,69},{38,70},{39,71},{44,76},{45,77},{46,78},{47,79},{5... | collective-permute-start | bytes 368648 | tf_op jit(solution)/shard_map/ppermute | solution.py:508
  10.7 1.8 %all-gather.near = f32[80,128]{1,0:T(8,128)S(1)} all-gather(f32[40,128]{1,0:T(8,128)S(1)} %get-tuple-element.37), channel_id=2, replica_groups={{0,1},{2,3},{4,5},{6,7},{8,9},{10,11},{12,13},{14,15},{16,17},{18,19},{..., dimensions={0}, use_global_device_ids=true | all-gather | bytes 61440 | tf_op jit(solution)/shard_map/all_gather | solution.py:512
  12.5 0.0 collective-permute-done.1.far
  12.5 1.1 %shard_map.66 = (f32[232,128]{1,0:T(8,128)S(1)}, f32[232,128]{1,0:T(8,128)S(1)}, f32[104,128]{1,0:T(8,128)S(1)}, f32[8,128]{1,0:T(8,128)S(1)}, f32[768,128]{1,0:...) custom-call(f32[40,128]{1,0:T(8,128)S(1)} %get-tuple-element.35.own,, ...), custom_call_target="tpu_custom_call", output_to_operand_aliasing={{0}: (3, {}), {1}: (4, {})} | custom-call | tf_op jit(solution)/shard_map/pallas_call | solution.py:483
  13.6 8.1 %collective-permute-start.3 = (f32[232,128]{1,0:T(8,128)S(1)}, f32[232,128]{1,0:T(8,128)S(1)}, u32[]{:S(2)}, u32[]{:S(2)}) collective-permute-start(f32[232,128]{1,0:T(8,128)S(1)} %get-tuple-element.43), channel_id=1, source_target_pairs={{32,64},{33,65},{34,66},{35,67},{40,72},{41,73},{42,74},{43,75},{4... | collective-permute-start | bytes 356360 | tf_op jit(solution)/shard_map/ppermute | solution.py:508
  21.8 0.7 %collective-permute-start.2 = (f32[8,128]{1,0:T(8,128)S(1)}, f32[8,128]{1,0:T(8,128)S(1)}, u32[]{:S(2)}, u32[]{:S(2)}) collective-permute-start(f32[8,128]{1,0:T(8,128)S(1)} %get-tuple-element.42), channel_id=1, source_target_pairs={{36,68},{37,69},{38,70},{39,71},{44,76},{45,77},{46,78},{47,79},{5... | collective-permute-start | bytes 12296 | tf_op jit(solution)/shard_map/ppermute | solution.py:508
  22.4 5.7 %all-gather.1.near = f32[464,128]{1,0:T(8,128)S(1)} all-gather(f32[232,128]{1,0:T(8,128)S(1)} %get-tuple-element.44), channel_id=3, replica_groups={{0,32},{1,33},{2,34},{3,35},{4,36},{5,37},{6,38},{7,39},{8,40},{9,41},{..., dimensions={0}, use_global_device_ids=true | all-gather | bytes 356352 | tf_op jit(solution)/shard_map/all_gather | solution.py:512
  28.1 0.4 %shard_map.67 = (f32[768,128]{1,0:T(8,128)S(1)}, f32[768,128]{1,0:T(8,128)S(1)}, f32[24,128]{1,0:T(8,128)S(1)}, f32[384,128]{1,0:T(8,128)S(1)}, f32[640,128]{1,0:T(8,128)S(1)}) custom-call(f32[768,128]{1,0:T(8,128)S(1)} %get-tuple-element.31.t.tracer, ...), custom_call_target="tpu_custom_call", output_to_operand_aliasing={{0}: (8, {}), {1}: (9, {}), {2}: (10, {}), {3}: (11, {}), {... | custom-call | tf_op jit(solution)/shard_map/pallas_call | solution.py:483
  28.6 0.0 collective-permute-done.2.corner
  28.6 0.0 collective-permute-done.early
  28.6 0.0 collective-permute-done.3.far
  28.6 1.1 %shard_map.68 = (f32[768,128]{1,0:T(8,128)}, f32[768,128]{1,0:T(8,128)S(1)}) custom-call(f32[240,128]{1,0:T(8,128)S(1)} %collective-permute-done.early, f32[8,128]{1,0:T(8,128)S(1)} %collective-permute-done.2.corner, f32[232,128]{1,0:T(8,128)S(1)} %collective-permute-done.3.far, f32[464,128]{1,0:T(8,128)S(1)} %all-gather.1.near, ...), custom_call_target="tpu_custom_call", output_to_operand_aliasing={{1}: (9, {})} | custom-call | tf_op jit(solution)/shard_map/pallas_call | solution.py:483
Async XLA Ops:
  1.4 11.1 %collective-permute-start.1 = (f32[40,128]{1,0:T(8,128)S(1)}, f32[40,128]{1,0:T(8,128)S(1)}, u32[]{:S(2)}, u32[]{:S(2)}) collective-permute-start(f32[40,128]{1,0:T(8,128)S(1)} %get-tuple-element.35.own), channel_id=1, source_target_pairs={{1,2},{3,4},{5,6},{7,8},{9,10},{11,12},{13,14},{15,16},{17,18},{19... | collective-permute-start | bytes 61448 | tf_op jit(solution)/shard_map/ppermute | solution.py:508
  10.0 18.6 %collective-permute-start = (f32[240,128]{1,0:T(8,128)S(1)}, f32[240,128]{1,0:T(8,128)S(1)}, u32[]{:S(2)}, u32[]{:S(2)}) collective-permute-start(f32[240,128]{1,0:T(8,128)S(1)} %get-tuple-element.36), channel_id=1, source_target_pairs={{36,68},{37,69},{38,70},{39,71},{44,76},{45,77},{46,78},{47,79},{5... | collective-permute-start | bytes 368648 | tf_op jit(solution)/shard_map/ppermute | solution.py:508
  13.6 15.0 %collective-permute-start.3 = (f32[232,128]{1,0:T(8,128)S(1)}, f32[232,128]{1,0:T(8,128)S(1)}, u32[]{:S(2)}, u32[]{:S(2)}) collective-permute-start(f32[232,128]{1,0:T(8,128)S(1)} %get-tuple-element.43), channel_id=1, source_target_pairs={{32,64},{33,65},{34,66},{35,67},{40,72},{41,73},{42,74},{43,75},{4... | collective-permute-start | bytes 356360 | tf_op jit(solution)/shard_map/ppermute | solution.py:508
  21.8 6.8 %collective-permute-start.2 = (f32[8,128]{1,0:T(8,128)S(1)}, f32[8,128]{1,0:T(8,128)S(1)}, u32[]{:S(2)}, u32[]{:S(2)}) collective-permute-start(f32[8,128]{1,0:T(8,128)S(1)} %get-tuple-element.42), channel_id=1, source_target_pairs={{36,68},{37,69},{38,70},{39,71},{44,76},{45,77},{46,78},{47,79},{5... | collective-permute-start | bytes 12296 | tf_op jit(solution)/shard_map/ppermute | solution.py:508
